TPU v7x, 32 devices: a whole 2x2x4 slice. The times are simulated.
32 devices in a mesh: seq: 4 (over z), head: 8 (over y, x, core).
Axes of the slice: x: 2, y: 2, z: 4, core: 2. Of those that a mesh axis runs over, the one named last changes fastest.
Arguments:
- tokens: bfloat16 [12288, 2048], P(('seq', 'head')), may hold values from -6 to 6
- segment: int32 [12288], P('seq'), may hold values from 0 to 32, as said below
- attn_gain: float32 [2048], replicated, may hold values from 0.1 to 1.9
- query_weight: bfloat16 [2048, 2048], P('seq', 'head'), may hold values from -0.125 to 0.125
- key_weight: bfloat16 [2048, 2048], P('seq', 'head'), may hold values from -0.125 to 0.125
- value_weight: bfloat16 [2048, 2048], P('seq', 'head'), may hold values from -0.125 to 0.125
- out_weight: bfloat16 [2048, 2048], P('head', 'seq'), may hold values from -1 to 1
- ffn_gain: float32 [2048], replicated, may hold values from 0.1 to 1.9
- gate_weight: bfloat16 [2048, 5504], P('seq', 'head'), may hold values from -0.125 to 0.125
- up_weight: bfloat16 [2048, 5504], P('seq', 'head'), may hold values from -0.125 to 0.125
- down_weight: bfloat16 [5504, 2048], P('head', 'seq'), may hold values from -0.078125 to 0.078125
- cotangent: bfloat16 [12288, 2048], P(('seq', 'head'))
Outputs:
- output: bfloat16 [12288, 2048], P(('seq', 'head'))
- input_grad: float32 [12288, 2048], P(('seq', 'head'))
- attn_gain_grad: float32 [2048], P(('seq', 'head'))
- query_grad: float32 [2048, 2048], P('seq', 'head')
- key_grad: float32 [2048, 2048], P('seq', 'head')
- value_grad: float32 [2048, 2048], P('seq', 'head')
- out_grad: float32 [2048, 2048], P('head', 'seq')
- ffn_gain_grad: float32 [2048], P(('seq', 'head'))
- gate_grad: float32 [2048, 5504], P('seq', 'head')
- up_grad: float32 [2048, 5504], P('seq', 'head')
- down_grad: float32 [5504, 2048], P('head', 'seq')
Inputs may be any that keep to these rules, and one draw needn't show every extreme that they name: segment ids never fall along the tokens, no document starts within the first 768 tokens of an aligned block of 3072 tokens, and the last token's id is always the largest allowed.
All inputs are finite; a program needn't handle non-finite values.
Results may differ from a plain program's by a relative error of at most 0.018.
Values may be sent and summed in bfloat16 or wider, within the bound.
A program may use at most 320 MiB of HBM per device.

v0:
```python
import jax
import jax.numpy as jnp
from jax import lax
from jax.sharding import PartitionSpec as P

HEAD_DIM = 128
WINDOW = 1024


EPS = 1e-06
NEG = -1e30


def from_behind(value, axis, by):
    count = lax.axis_size(axis)
    pairs = [(i, i + by) for i in range(count) if 0 <= i + by < count]
    return lax.ppermute(value, axis, pairs)


def product(left, right):
    return jnp.dot(left, right, preferred_element_type=jnp.float32)


def product_tn(left, right):
    return lax.dot_general(
        left, right, (((0,), (0,)), ((), ())), preferred_element_type=jnp.float32
    )


def product_nt(left, right):
    return lax.dot_general(
        left, right, (((1,), (1,)), ((), ())), preferred_element_type=jnp.float32
    )


def normalize(rows):
    inverse = lax.rsqrt(jnp.mean(rows * rows, axis=-1, keepdims=True) + EPS)
    return (rows * inverse, inverse)


def norm_back(unit, inverse, gain, grad):
    scaled = grad * gain
    return inverse * (scaled - unit * jnp.mean(scaled * unit, axis=-1, keepdims=True))


def gather_rows(rows):
    return lax.all_gather(rows, "head", axis=0, tiled=True)


def block_scores(query_heads, key_heads, seg_query, seg_keys, valid, start, block):
    query_part = query_heads[start : start + block]
    key_part = key_heads[start : start + block + WINDOW]
    scores = jnp.einsum(
        "qhd,khd->hqk", query_part, key_part, preferred_element_type=jnp.float32
    ) * HEAD_DIM ** (-0.5)
    rows = jnp.arange(block)[:, None] + WINDOW
    cols = jnp.arange(block + WINDOW)[None, :]
    distance = rows - cols
    same_doc = (
        seg_query[start : start + block][:, None]
        == seg_keys[start : start + block + WINDOW][None, :]
    )
    visible = (
        (distance >= 0)
        & (distance <= WINDOW)
        & same_doc
        & valid[start : start + block + WINDOW][None, :]
    )
    return jnp.where(visible[None], scores, NEG)


def local(
    tokens,
    segment,
    attn_gain,
    query_weight,
    key_weight,
    value_weight,
    out_weight,
    ffn_gain,
    gate_weight,
    up_weight,
    down_weight,
    cotangent,
):
    own_rows = tokens.shape[0]
    group = own_rows * lax.axis_size("head")
    heads_here = query_weight.shape[1] // HEAD_DIM
    offset = lax.axis_index("head") * own_rows
    seq_index = lax.axis_index("seq")
    block = min(512, group)
    scale = HEAD_DIM ** (-0.5)
    w_query, w_key, w_value, w_out, w_gate, w_up, w_down = (
        lax.all_gather(query_weight, "seq", axis=0, tiled=True),
        lax.all_gather(key_weight, "seq", axis=0, tiled=True),
        lax.all_gather(value_weight, "seq", axis=0, tiled=True),
        lax.all_gather(out_weight, "seq", axis=1, tiled=True),
        lax.all_gather(gate_weight, "seq", axis=0, tiled=True),
        lax.all_gather(up_weight, "seq", axis=0, tiled=True),
        lax.all_gather(down_weight, "seq", axis=1, tiled=True),
    )
    inputs = tokens.astype(jnp.float32)
    unit_one, inverse_one = normalize(inputs)
    normed_full = gather_rows((unit_one * attn_gain).astype(jnp.bfloat16))
    queries = product(normed_full, w_query).astype(jnp.bfloat16)
    keys = product(normed_full, w_key).astype(jnp.bfloat16)
    values = product(normed_full, w_value).astype(jnp.bfloat16)
    halo_keys, halo_values, halo_segs = ([], [], [])
    hop = 1
    take = min(group, WINDOW - (hop - 1) * group)
    got_keys, got_values, got_segs = from_behind(
        (keys[group - take :], values[group - take :], segment[group - take :]), "seq", hop
    )
    halo_keys.append(got_keys)
    halo_values.append(got_values)
    halo_segs.append(got_segs)
    keys_ext = jnp.concatenate(halo_keys + [keys], axis=0)
    values_ext = jnp.concatenate(halo_values + [values], axis=0)
    segs_ext = jnp.concatenate(halo_segs + [segment], axis=0)
    positions = seq_index * group - WINDOW + jnp.arange(WINDOW + group)
    valid = positions >= 0
    query_heads = queries.reshape(group, heads_here, HEAD_DIM)
    key_heads = keys_ext.reshape(WINDOW + group, heads_here, HEAD_DIM)
    value_heads = values_ext.reshape(WINDOW + group, heads_here, HEAD_DIM)
    outputs, logsums = ([], [])
    for start in range(0, group, block):
        scores = block_scores(query_heads, key_heads, segment, segs_ext, valid, start, block)
        highest = jnp.max(scores, axis=-1, keepdims=True)
        weights = jnp.exp(scores - highest)
        total = jnp.sum(weights, axis=-1, keepdims=True)
        probs = (weights / total).astype(jnp.bfloat16)
        outputs.append(
            jnp.einsum(
                "hqk,khd->qhd",
                probs,
                value_heads[start : start + block + WINDOW],
                preferred_element_type=jnp.float32,
            )
        )
        logsums.append(highest + jnp.log(total))
    attended = (
        jnp.concatenate(outputs, axis=0).reshape(group, heads_here * HEAD_DIM).astype(jnp.bfloat16)
    )
    partial_out = product(attended, w_out)
    own_part = lax.dynamic_slice_in_dim(partial_out, offset, own_rows, 0)
    placed = lax.dynamic_update_slice_in_dim(partial_out, own_part + inputs, offset, 0)
    middle_full = lax.psum(placed, "head")
    middle = lax.dynamic_slice_in_dim(middle_full, offset, own_rows, 0)
    unit_full, inverse_full = normalize(middle_full)
    normed_two_full = (unit_full * ffn_gain).astype(jnp.bfloat16)
    unit_two, inverse_two = normalize(middle)
    gate = product(normed_two_full, w_gate)
    up = product(normed_two_full, w_up)
    sigmoid = jax.nn.sigmoid(gate)
    activated = gate * sigmoid
    hidden = (activated * up).astype(jnp.bfloat16)
    ffn_out = lax.psum_scatter(
        product(hidden, w_down).astype(jnp.bfloat16), "head", scatter_dimension=0, tiled=True
    ).astype(jnp.float32)
    result = middle + ffn_out
    grad_out = lax.all_gather(cotangent, "head", axis=0, tiled=True)
    grad_hidden = product_nt(grad_out, w_down)
    grad_gate = (grad_hidden * up * sigmoid * (1.0 + gate * (1.0 - sigmoid))).astype(jnp.bfloat16)
    grad_up = (grad_hidden * activated).astype(jnp.bfloat16)
    down_grad = product_tn(hidden, grad_out)
    gate_grad = product_tn(normed_two_full, grad_gate)
    up_grad = product_tn(normed_two_full, grad_up)
    grad_normed_two = lax.psum_scatter(
        (product_nt(grad_gate, w_gate) + product_nt(grad_up, w_up)).astype(jnp.bfloat16),
        "head",
        scatter_dimension=0,
        tiled=True,
    ).astype(jnp.float32)
    ffn_gain_part = jnp.sum(grad_normed_two * unit_two, axis=0)
    grad_middle = cotangent.astype(jnp.float32) + norm_back(
        unit_two, inverse_two, ffn_gain, grad_normed_two
    )
    grad_branch = lax.all_gather(grad_middle.astype(jnp.bfloat16), "head", axis=0, tiled=True)
    out_grad = product_tn(attended, grad_branch)
    grad_attended = product_nt(grad_branch, w_out).astype(jnp.bfloat16)
    grad_heads = grad_attended.reshape(group, heads_here, HEAD_DIM)
    grad_query_list = []
    grad_keys_ext = jnp.zeros((WINDOW + group, heads_here, HEAD_DIM), jnp.float32)
    grad_values_ext = jnp.zeros((WINDOW + group, heads_here, HEAD_DIM), jnp.float32)
    for number, start in enumerate(range(0, group, block)):
        scores = block_scores(query_heads, key_heads, segment, segs_ext, valid, start, block)
        probs = jnp.exp(scores - logsums[number])
        probs_low = probs.astype(jnp.bfloat16)
        key_part = key_heads[start : start + block + WINDOW]
        value_part = value_heads[start : start + block + WINDOW]
        query_part = query_heads[start : start + block]
        grad_part = grad_heads[start : start + block]
        grad_probs = jnp.einsum(
            "qhd,khd->hqk", grad_part, value_part, preferred_element_type=jnp.float32
        )
        inner = jnp.sum(probs * grad_probs, axis=-1, keepdims=True)
        grad_scores = (probs * (grad_probs - inner)).astype(jnp.bfloat16)
        grad_query_list.append(
            jnp.einsum("hqk,khd->qhd", grad_scores, key_part, preferred_element_type=jnp.float32)
            * scale
        )
        key_term = (
            jnp.einsum("hqk,qhd->khd", grad_scores, query_part, preferred_element_type=jnp.float32)
            * scale
        )
        value_term = jnp.einsum(
            "hqk,qhd->khd", probs_low, grad_part, preferred_element_type=jnp.float32
        )
        grad_keys_ext = grad_keys_ext.at[start : start + block + WINDOW].add(key_term)
        grad_values_ext = grad_values_ext.at[start : start + block + WINDOW].add(value_term)
    grad_keys_ext = grad_keys_ext.reshape(WINDOW + group, heads_here * HEAD_DIM)
    grad_values_ext = grad_values_ext.reshape(WINDOW + group, heads_here * HEAD_DIM)
    grad_keys = grad_keys_ext[WINDOW:]
    grad_values = grad_values_ext[WINDOW:]
    cursor = 0
    hop = 1
    take = min(group, WINDOW - (hop - 1) * group)
    back_keys = from_behind(
        grad_keys_ext[cursor : cursor + take].astype(jnp.bfloat16), "seq", -hop
    ).astype(jnp.float32)
    back_values = from_behind(
        grad_values_ext[cursor : cursor + take].astype(jnp.bfloat16), "seq", -hop
    ).astype(jnp.float32)
    grad_keys = grad_keys.at[group - take :].add(back_keys)
    grad_values = grad_values.at[group - take :].add(back_values)
    grad_queries = (
        jnp.concatenate(grad_query_list, axis=0)
        .reshape(group, heads_here * HEAD_DIM)
        .astype(jnp.bfloat16)
    )
    grad_keys = grad_keys.astype(jnp.bfloat16)
    grad_values = grad_values.astype(jnp.bfloat16)
    query_grad = product_tn(normed_full, grad_queries)
    key_grad = product_tn(normed_full, grad_keys)
    value_grad = product_tn(normed_full, grad_values)
    grad_normed_one = lax.psum_scatter(
        (
            product_nt(grad_queries, w_query)
            + product_nt(grad_keys, w_key)
            + product_nt(grad_values, w_value)
        ).astype(jnp.bfloat16),
        "head",
        scatter_dimension=0,
        tiled=True,
    ).astype(jnp.float32)
    attn_gain_part = jnp.sum(grad_normed_one * unit_one, axis=0)
    input_grad = grad_middle + norm_back(unit_one, inverse_one, attn_gain, grad_normed_one)
    summed = (
        lax.psum_scatter(
            query_grad.astype(jnp.bfloat16), "seq", scatter_dimension=0, tiled=True
        ).astype(jnp.float32),
        lax.psum_scatter(
            key_grad.astype(jnp.bfloat16), "seq", scatter_dimension=0, tiled=True
        ).astype(jnp.float32),
        lax.psum_scatter(
            value_grad.astype(jnp.bfloat16), "seq", scatter_dimension=0, tiled=True
        ).astype(jnp.float32),
        lax.psum_scatter(
            out_grad.astype(jnp.bfloat16), "seq", scatter_dimension=1, tiled=True
        ).astype(jnp.float32),
        lax.psum_scatter(
            gate_grad.astype(jnp.bfloat16), "seq", scatter_dimension=0, tiled=True
        ).astype(jnp.float32),
        lax.psum_scatter(
            up_grad.astype(jnp.bfloat16), "seq", scatter_dimension=0, tiled=True
        ).astype(jnp.float32),
        lax.psum_scatter(
            down_grad.astype(jnp.bfloat16), "seq", scatter_dimension=1, tiled=True
        ).astype(jnp.float32),
    )
    gain_grads = (
        lax.psum_scatter(attn_gain_part, ("seq", "head"), scatter_dimension=0, tiled=True),
        lax.psum_scatter(ffn_gain_part, ("seq", "head"), scatter_dimension=0, tiled=True),
    )
    return (
        result.astype(jnp.bfloat16),
        input_grad,
        gain_grads[0],
        summed[0],
        summed[1],
        summed[2],
        summed[3],
        gain_grads[1],
        summed[4],
        summed[5],
        summed[6],
    )


def solution(mesh):
    placed = (
        P(("seq", "head"), None),
        P("seq"),
        P(),
        P("seq", "head"),
        P("seq", "head"),
        P("seq", "head"),
        P("head", "seq"),
        P(),
        P("seq", "head"),
        P("seq", "head"),
        P("head", "seq"),
        P(("seq", "head"), None),
    )
    return jax.shard_map(
        local,
        mesh=mesh,
        in_specs=placed,
        out_specs=(
            P(("seq", "head"), None),
            P(("seq", "head"), None),
            P(("seq", "head")),
            P("seq", "head"),
            P("seq", "head"),
            P("seq", "head"),
            P("head", "seq"),
            P(("seq", "head")),
            P("seq", "head"),
            P("seq", "head"),
            P("head", "seq"),
        ),
        check_vma=False,
    )
```

profile of v0, /device:TPU:0, one launch (start us, length us, event | category | flops | bytes accessed | tf_op | source)
XLA Modules:
  0.0 1564.1 jit_solution(15343997535453354480)
XLA Ops:
  27.2 13.1 all-gather.17.cloned.1.call-done
  40.2 74.1 %all-gather.11.cloned.1.call-done = bf16[3072,2048]{1,0:T(8,128)(2,1)} async-done(((bf16[384,2048]{1,0:T(8,128)(2,1)}), bf16[3072,2048]{1,0:T(8,128)(2,1)}) %all-gather.11.cloned.1.call-update) | async-done | bytes 12582928 | tf_op jit(solution)/shard_map/all_gather | solution.py:47
  127.7 24.6 %all-gather.13.cloned.1.call-done = bf16[2048,256]{1,0:T(8,128)(2,1)} async-done(((bf16[512,256]{1,0:T(8,128)(2,1)}), bf16[2048,256]{1,0:T(8,128)(2,1)}) %all-gather.13.cloned.1.call-update) | async-done | bytes 1048592 | tf_op jit(solution)/shard_map/all_gather | solution.py:96
  167.0 23.9 %all-gather.15.cloned.1.call-done = bf16[2048,256]{1,0:T(8,128)(2,1)} async-done(((bf16[512,256]{1,0:T(8,128)(2,1)}), bf16[2048,256]{1,0:T(8,128)(2,1)}) %all-gather.15.cloned.1.call-update) | async-done | bytes 1048592 | tf_op jit(solution)/shard_map/all_gather | solution.py:94
  213.2 11.5 fusion.172
  249.8 12.0 fusion.174
  269.0 305.2 %all-reduce.7.cloned.1.call-done = f32[3072,2048]{1,0:T(8,128)} async-done(((f32[3072,2048]{1,0:T(8,128)}), f32[3072,2048]{1,0:T(8,128)}) %all-reduce.7.cloned.1.call-update) | async-done | bytes 25165840 | tf_op jit(solution)/shard_map/psum | solution.py:147
  574.2 11.0 multiply_reduce_fusion
  596.6 37.5 %all-gather.23.cloned.1.call-done = bf16[2048,688]{0,1:T(8,128)(2,1)} async-done(((bf16[512,688]{0,1:T(8,128)(2,1)}), bf16[2048,688]{0,1:T(8,128)(2,1)}) %all-gather.23.cloned.1.call-update) | async-done | bytes 2818064 | tf_op jit(solution)/shard_map/all_gather | solution.py:99
  634.1 14.7 fusion.176
  648.8 43.7 %all-gather.21.cloned.1.call-done = bf16[2048,688]{0,1:T(8,128)(2,1)} async-done(((bf16[512,688]{0,1:T(8,128)(2,1)}), bf16[2048,688]{0,1:T(8,128)(2,1)}) %all-gather.21.cloned.1.call-update) | async-done | bytes 2818064 | tf_op jit(solution)/shard_map/all_gather | solution.py:98
  692.6 14.7 fusion.175
  707.3 43.8 %all-gather.25.cloned.1.call-done = bf16[688,2048]{1,0:T(8,128)(2,1)} async-done(((bf16[688,512]{1,0:T(8,128)(2,1)}), bf16[688,2048]{1,0:T(8,128)(2,1)}) %all-gather.25.cloned.1.call-update) | async-done | bytes 2818064 | tf_op jit(solution)/shard_map/all_gather | solution.py:100
  751.0 72.8 %all-gather.27.cloned.1.call-done = bf16[3072,2048]{1,0:T(8,128)(2,1)} async-done(((bf16[384,2048]{1,0:T(8,128)(2,1)}), bf16[3072,2048]{1,0:T(8,128)(2,1)}) %all-gather.27.cloned.1.call-update) | async-done | bytes 12582928 | tf_op jit(solution)/shard_map/all_gather | solution.py:161
  823.8 22.6 %multiply_convert_fusion.1 = (bf16[3072,688]{0,1:T(8,128)(2,1)}, bf16[3072,688]{0,1:T(8,128)(2,1)}, bf16[3072,688]{0,1:T(8,128)(2,1)}) fusion(f32[3072,688]{0,1:T(8,128)} %fusion.175, f32[3072,688]{0,1:T(8,128)} %fusion.176, bf16[3072,2048]{1,0:T(8,128)(2,1)} %all-gather.27.cloned.1.call-done, bf16[688,2048]{1,0:T(8,128)(2,1)} %all-gather.25.cloned.1.call-done), kind=kOutput, calls=%fused_computation.5 | convolution fusion | flops 8688746496 | bytes 44990464 | tf_op jit(solution)/shard_map/dot_general | solution.py:31
  846.4 17.2 %fusion.177 = f32[3072,2048]{1,0:T(8,128)} fusion(bf16[3072,688]{0,1:T(8,128)(2,1)} %get-tuple-element.188, bf16[2048,688]{0,1:T(8,128)(2,1)} %all-gather.21.cloned.1.call-done), kind=kOutput, calls=%fused_computation.251 | convolution fusion | flops 8657043456 | bytes 32210944 | tf_op jit(solution)/shard_map/dot_general | solution.py:31
  863.6 19.0 %add_convert_fusion.1 = bf16[3072,2048]{1,0:T(8,128)(2,1)} fusion(f32[3072,2048]{1,0:T(8,128)} %fusion.177, bf16[3072,688]{0,1:T(8,128)(2,1)} %get-tuple-element.187, bf16[2048,688]{0,1:T(8,128)(2,1)} %all-gather.23.cloned.1.call-done), kind=kOutput, calls=%fused_computation.1 | convolution fusion | flops 8669626368 | bytes 44793856 | tf_op jit(solution)/shard_map/dot_general | solution.py:31
  885.0 90.2 %reduce-scatter.13.cloned.1.call-done = bf16[384,2048]{1,0:T(8,128)(2,1)} async-done(((bf16[3072,2048]{1,0:T(8,128)(2,1)}), bf16[384,2048]{1,0:T(8,128)(2,1)}) %reduce-scatter.13.cloned.1.call-update) | async-done | bytes 1572880 | tf_op jit(solution)/shard_map/reduce_scatter | solution.py:168
  984.0 14.3 convolution_convert_fusion.7
  998.5 14.5 convolution_convert_fusion.5
  1013.3 14.3 convolution_convert_fusion.6
  1027.9 28.4 %all-gather.29.cloned.1.call-done = bf16[3072,2048]{1,0:T(8,128)(2,1)} async-done(((bf16[384,2048]{1,0:T(8,128)(2,1)}), bf16[3072,2048]{1,0:T(8,128)(2,1)}) %all-gather.29.cloned.1.call-update) | async-done | bytes 12582928 | tf_op jit(solution)/shard_map/all_gather | solution.py:178
  1193.4 10.6 fusion.178
  1221.5 11.6 fusion.179
  1233.1 22.5 %add_convert_fusion = bf16[3072,2048]{1,0:T(8,128)(2,1)} fusion(f32[3072,2048]{1,0:T(8,128)} %fusion.178, f32[3072,2048]{1,0:T(8,128)} %fusion.179, bf16[2048,256]{1,0:T(8,128)(2,1)} %all-gather.13.cloned.1.call-done, bf16[3072,256]{0,1:T(8,128)(2,1)S(1)} %copy-done.18), kind=kOutput, calls=%fused_computation | convolution fusion | flops 3240099840 | bytes 65536000 | tf_op jit(solution)/shard_map/dot_general | solution.py:31
  1257.4 14.8 convolution_convert_fusion
  1281.5 21.8 %reduce-scatter.17.cloned.1.call-done = bf16[512,256]{1,0:T(8,128)(2,1)} async-done(((bf16[2048,256]{1,0:T(8,128)(2,1)}), bf16[512,256]{1,0:T(8,128)(2,1)}) %reduce-scatter.17.cloned.1.call-update) | async-done | bytes 262160 | tf_op jit(solution)/shard_map/reduce_scatter | solution.py:249
  1305.1 26.2 %reduce-scatter.21.cloned.1.call-done = bf16[512,256]{1,0:T(8,128)(2,1)} async-done(((bf16[2048,256]{1,0:T(8,128)(2,1)}), bf16[512,256]{1,0:T(8,128)(2,1)}) %reduce-scatter.21.cloned.1.call-update) | async-done | bytes 262160 | tf_op jit(solution)/shard_map/reduce_scatter | solution.py:255
  1333.1 27.0 %reduce-scatter.19.cloned.1.call-done = bf16[512,256]{1,0:T(8,128)(2,1)} async-done(((bf16[2048,256]{1,0:T(8,128)(2,1)}), bf16[512,256]{1,0:T(8,128)(2,1)}) %reduce-scatter.19.cloned.1.call-update) | async-done | bytes 262160 | tf_op jit(solution)/shard_map/reduce_scatter | solution.py:252
  1361.9 92.7 %reduce-scatter.15.cloned.1.call-done = bf16[384,2048]{1,0:T(8,128)(2,1)} async-done(((bf16[3072,2048]{1,0:T(8,128)(2,1)}), bf16[384,2048]{1,0:T(8,128)(2,1)}) %reduce-scatter.15.cloned.1.call-update) | async-done | bytes 1572880 | tf_op jit(solution)/shard_map/reduce_scatter | solution.py:236
  1457.1 39.8 %all-reduce.4 = (f32[2048]{0:T(1024)S(1)}, f32[2048]{0:T(1024)S(1)}) all-reduce(f32[2048]{0:T(1024)S(1)} %get-tuple-element.181, f32[2048]{0:T(1024)S(1)} %copy-done.87), channel_id=5, replica_groups=mesh['seq'=4,'head'=8] {'seq','head'}, use_global_device_ids=true, to_apply=%region_28.29.clone | all-reduce | flops 4096 | bytes 32768
  1498.1 53.0 %reduce-scatter.11.cloned.1.call-done = bf16[384,2048]{1,0:T(8,128)(2,1)} async-done(((bf16[3072,2048]{1,0:T(8,128)(2,1)}), bf16[384,2048]{1,0:T(8,128)(2,1)}) %reduce-scatter.11.cloned.1.call-update) | async-done | bytes 1572880 | tf_op jit(solution)/shard_map/reduce_scatter | solution.py:157
  (433 shorter events, 304.5 us)
Async XLA Ops:
  7.2 33.1 %all-gather.17.cloned.1.call-start = ((), (), s32[]{:S(2)}) async-start(), calls=%async_computation.13 | async-start | bytes 1310720 | tf_op jit(solution)/shard_map/all_gather | solution.py:95
  7.9 106.5 %all-gather.11.cloned.1.call-start = ((), (), s32[]{:S(2)}) async-start(), calls=%async_computation.10 | async-start | bytes 14155776 | tf_op jit(solution)/shard_map/all_gather | solution.py:47
  13.4 138.9 %all-gather.13.cloned.1.call-start = ((), (), s32[]{:S(2)}) async-start(), calls=%async_computation.11 | async-start | bytes 1310720 | tf_op jit(solution)/shard_map/all_gather | solution.py:96
  14.1 176.8 %all-gather.15.cloned.1.call-start = ((), (), s32[]{:S(2)}) async-start(), calls=%async_computation.12 | async-start | bytes 1310720 | tf_op jit(solution)/shard_map/all_gather | solution.py:94
  14.7 235.1 %all-gather.19.cloned.1.call-start = ((), (), s32[]{:S(2)}) async-start(), calls=%async_computation.14 | async-start | bytes 1310720 | tf_op jit(solution)/shard_map/all_gather | solution.py:97
  14.7 6.2 collective-permute-start.1
  19.7 554.5 %all-reduce.7.cloned.1.call-start = ((), (), s32[]{:S(2)}) async-start(), calls=%async_computation.15 | async-start | bytes 50331648 | tf_op jit(solution)/shard_map/psum | solution.py:147
  123.5 76.6 %collective-permute-start.2 = (bf16[1024,256]{0,1:T(8,128)(2,1)}, bf16[1024,256]{0,1:T(8,128)(2,1)}, u32[]{:S(2)}, u32[]{:S(2)}) collective-permute-start(bf16[1024,256]{0,1:T(8,128)(2,1)} %slice.702), channel_id=1, source_target_pairs={{0,8},{8,16},{16,24},{1,9},{9,17},{17,25},{2,10},{10,18},{18,26},{... | collective-permute-start | bytes 1572872 | tf_op jit(solution)/shard_map/ppermute | solution.py:17
  161.4 67.1 %collective-permute-start = (bf16[1024,256]{0,1:T(8,128)(2,1)}, bf16[1024,256]{0,1:T(8,128)(2,1)}, u32[]{:S(2)}, u32[]{:S(2)}) collective-permute-start(bf16[1024,256]{0,1:T(8,128)(2,1)} %slice.698), channel_id=1, source_target_pairs={{0,8},{8,16},{16,24},{1,9},{9,17},{17,25},{2,10},{10,18},{18,26},{... | collective-permute-start | bytes 1572872 | tf_op jit(solution)/shard_map/ppermute | solution.py:17
  266.1 368.0 %all-gather.23.cloned.1.call-start = ((), (), s32[]{:S(2)}) async-start(), calls=%async_computation.17 | async-start | bytes 3522560 | tf_op jit(solution)/shard_map/all_gather | solution.py:99
  266.9 425.7 %all-gather.21.cloned.1.call-start = ((), (), s32[]{:S(2)}) async-start(), calls=%async_computation.16 | async-start | bytes 3522560 | tf_op jit(solution)/shard_map/all_gather | solution.py:98
  267.6 483.4 %all-gather.25.cloned.1.call-start = ((), (), s32[]{:S(2)}) async-start(), calls=%async_computation.18 | async-start | bytes 3522560 | tf_op jit(solution)/shard_map/all_gather | solution.py:100
  268.4 555.5 %all-gather.27.cloned.1.call-start = ((), (), s32[]{:S(2)}) async-start(), calls=%async_computation.20 | async-start | bytes 14155776 | tf_op jit(solution)/shard_map/all_gather | solution.py:161
  268.9 316.3 %copy-start.70 = (f32[2048]{0:T(1024)S(1)}, f32[2048]{0:T(1024)}, u32[]{:S(2)}) copy-start(f32[2048]{0:T(1024)} %param.47) | copy-start | bytes 24580
  268.9 706.3 %reduce-scatter.13.cloned.1.call-start = ((), (), s32[]{:S(2)}) async-start(), calls=%async_computation.21 | async-start | bytes 14155776 | tf_op jit(solution)/shard_map/reduce_scatter | solution.py:168
  882.7 173.6 %all-gather.29.cloned.1.call-start = ((), (), s32[]{:S(2)}) async-start(), calls=%async_computation.22 | async-start | bytes 14155776 | tf_op jit(solution)/shard_map/all_gather | solution.py:178
  984.0 288.2 %reduce-scatter.29.cloned.1.call-start = ((), (), s32[]{:S(2)}) async-start(), calls=%async_computation.30 | async-start | bytes 3522560 | tf_op jit(solution)/shard_map/reduce_scatter | solution.py:267
  998.4 276.2 %reduce-scatter.27.cloned.1.call-start = ((), (), s32[]{:S(2)}) async-start(), calls=%async_computation.29 | async-start | bytes 3522560 | tf_op jit(solution)/shard_map/reduce_scatter | solution.py:264
  1013.0 264.2 %reduce-scatter.25.cloned.1.call-start = ((), (), s32[]{:S(2)}) async-start(), calls=%async_computation.28 | async-start | bytes 3522560 | tf_op jit(solution)/shard_map/reduce_scatter | solution.py:261
  1027.6 252.1 %reduce-scatter.23.cloned.1.call-start = ((), (), s32[]{:S(2)}) async-start(), calls=%async_computation.27 | async-start | bytes 1310720 | tf_op jit(solution)/shard_map/reduce_scatter | solution.py:258
  1095.8 87.2 %collective-permute-start.4 = (bf16[1024,256]{0,1:T(8,128)(2,1)}, bf16[1024,256]{0,1:T(8,128)(2,1)}, u32[]{:S(2)}, u32[]{:S(2)}) collective-permute-start(bf16[1024,256]{0,1:T(8,128)(2,1)} %bitcast.55), channel_id=1, source_target_pairs={{8,0},{16,8},{24,16},{9,1},{17,9},{25,17},{10,2},{18,10},{26,18},{... | collective-permute-start | bytes 1572872 | tf_op jit(solution)/shard_map/ppermute | solution.py:17
  1139.3 164.1 %reduce-scatter.17.cloned.1.call-start = ((), (), s32[]{:S(2)}) async-start(), calls=%async_computation.24 | async-start | bytes 1310720 | tf_op jit(solution)/shard_map/reduce_scatter | solution.py:249
  1175.0 156.3 %reduce-scatter.21.cloned.1.call-start = ((), (), s32[]{:S(2)}) async-start(), calls=%async_computation.26 | async-start | bytes 1310720 | tf_op jit(solution)/shard_map/reduce_scatter | solution.py:255
  1181.7 30.7 %collective-permute-start.3 = (bf16[1024,256]{0,1:T(8,128)(2,1)}, bf16[1024,256]{0,1:T(8,128)(2,1)}, u32[]{:S(2)}, u32[]{:S(2)}) collective-permute-start(bf16[1024,256]{0,1:T(8,128)(2,1)} %bitcast.46), channel_id=1, source_target_pairs={{8,0},{16,8},{24,16},{9,1},{17,9},{25,17},{10,2},{18,10},{26,18},{... | collective-permute-start | bytes 1572872 | tf_op jit(solution)/shard_map/ppermute | solution.py:17
  1193.3 166.8 %reduce-scatter.19.cloned.1.call-start = ((), (), s32[]{:S(2)}) async-start(), calls=%async_computation.25 | async-start | bytes 1310720 | tf_op jit(solution)/shard_map/reduce_scatter | solution.py:252
  1221.4 233.1 %reduce-scatter.15.cloned.1.call-start = ((), (), s32[]{:S(2)}) async-start(), calls=%async_computation.23 | async-start | bytes 14155776 | tf_op jit(solution)/shard_map/reduce_scatter | solution.py:236
  1255.6 295.5 %reduce-scatter.11.cloned.1.call-start = ((), (), s32[]{:S(2)}) async-start(), calls=%async_computation.19 | async-start | bytes 14155776 | tf_op jit(solution)/shard_map/reduce_scatter | solution.py:157
  1274.6 179.9 %copy-start.89 = (f32[384]{0:T(512)S(1)}, f32[384]{0:T(512)}, u32[]{:S(2)}) copy-start(f32[384]{0:T(512)} %copy-done.88) | copy-start | bytes 4612
  1277.2 273.9 %copy-start.12 = (bf16[384,2048]{1,0:T(8,128)(2,1)S(1)}, bf16[384,2048]{1,0:T(8,128)(2,1)}, u32[]{:S(2)}) copy-start(bf16[384,2048]{1,0:T(8,128)(2,1)} %param.51) | copy-start | bytes 4718596
  1277.2 273.9 %copy-start.71 = (f32[2048]{0:T(1024)S(1)}, f32[2048]{0:T(1024)}, u32[]{:S(2)}) copy-start(f32[2048]{0:T(1024)} %param.47) | copy-start | bytes 24580
  1277.2 273.9 %copy-start.86 = (f32[384]{0:T(512)S(1)}, f32[384]{0:T(512)}, u32[]{:S(2)}) copy-start(f32[384]{0:T(512)} %copy-done.85) | copy-start | bytes 4612
  1277.2 273.9 %copy-start.91 = (f32[384]{0:T(512)S(1)}, f32[384]{0:T(512)}, u32[]{:S(2)}) copy-start(f32[384]{0:T(512)} %copy-done.90) | copy-start | bytes 4612
  (122 other events, 1775.0 us)
Sparse Core Ops, SparseCore 0:
  9.6 30.6 all-gather.16
  42.7 71.6 all-gather.10
  116.0 36.2 all-gather.12
  153.7 37.2 all-gather.14
  192.3 28.9 all-gather.18
  266.2 307.9 all-reduce.6
  575.9 58.1 all-gather.22
  635.7 56.7 all-gather.20
  694.2 56.7 all-gather.24
  752.9 70.8 all-gather.26
  882.8 92.3 reduce-scatter.12
  984.1 72.1 all-gather.28
  1058.7 64.5 reduce-scatter.28
  1125.5 56.6 reduce-scatter.26
  1185.0 61.8 reduce-scatter.24
  1249.0 26.1 reduce-scatter.22
  1277.5 25.7 reduce-scatter.16
  1305.5 25.7 reduce-scatter.20
  1334.3 25.8 reduce-scatter.18
  1363.5 91.0 reduce-scatter.14
  1458.1 92.9 reduce-scatter.10
where the time goes:
time: 1570 us; the launch traced here: 1560 us
  waiting for transfers between devices  990 us (63%)
  matrix products  359 us (23%)
  other arithmetic  98.5 us (6%)
  local copies, waits for them, and re-layouts  41.8 us (3%)
  blocking collectives  39.8 us (3%)
  starting transfers between devices  18.4 us (1%)
  between operations  16.6 us (1%)
    psum x1, waiting for transfers between devices, local(): middle_full = lax.psum(placed, 'head')  305 us
    dot_general x7, matrix products, product_nt(): lax.dot_general(left, right, (((1,), (1,)), ((), ())), preferred_element_...  112 us
    reduce_scatter x1, waiting for transfers between devices, local(): lax.psum_scatter((product_nt(grad_queries, w_query) + product_nt(grad_key...  92.7 us
    reduce_scatter x1, waiting for transfers between devices, local(): lax.psum_scatter((product_nt(grad_gate, w_gate) + product_nt(grad_up, w_u...  90.2 us
    dot_general x7, matrix products, product(): return jnp.dot(left, right, preferred_element_type=jnp.float32)  81.1 us
    all_gather x1, waiting for transfers between devices, gather_rows(): return lax.all_gather(rows, 'head', axis=0, tiled=True)  74.1 us
    all_gather x1, waiting for transfers between devices, local(): grad_out = lax.all_gather(cotangent, 'head', axis=0, tiled=True)  72.8 us
    dot_general x7, matrix products, product_tn(): lax.dot_general(left, right, (((0,), (0,)), ((), ())), preferred_element_...  70.9 us
  transfers between devices with their start and end apart: 26, of which 18 were waited for; matrix products, arithmetic and copies ran while one was open for 25% of the time, Pallas kernels for 0%

commit v1 on v0

--- a/solution.py
+++ b/solution.py
@@ -1,6 +1,10 @@
+import functools
+
 import jax
 import jax.numpy as jnp
 from jax import lax
+from jax.experimental import pallas as pl
+from jax.experimental.pallas import tpu as pltpu
 from jax.sharding import PartitionSpec as P
 
 HEAD_DIM = 128
@@ -287,6 +291,547 @@
     )
 
 
+MESH = pl.DeviceIdType.MESH
+BF16 = jnp.bfloat16
+F32 = jnp.float32
+MIB = 2**20
+
+
+def remote(src, dst, send_sem, recv_sem, where):
+    return pltpu.make_async_remote_copy(
+        src_ref=src,
+        dst_ref=dst,
+        send_sem=send_sem,
+        recv_sem=recv_sem,
+        device_id=where,
+        device_id_type=MESH,
+    )
+
+
+class Place:
+    def __init__(self, line):
+        s, h = lax.axis_index("seq"), lax.axis_index("head")
+        core = lax.rem(h, 2)
+        x = lax.rem(lax.div(h, 2), 2)
+        y = lax.div(h, 4)
+        self.s, self.h, self.line = s, h, line
+        self.turn = 1 - 2 * core
+        self.core = h + self.turn
+        over_x, over_y = 2 - 4 * x, 4 - 8 * y
+        self.first = h + over_x * (1 - core) + over_y * core
+        self.second = h + over_y * (1 - core) + over_x * core
+        self.across = h + over_x + over_y
+
+    def at(self, head):
+        return (self.s, head)
+
+    def greet(self, along_seq=True):
+        barrier = pltpu.get_barrier_semaphore()
+        for head in (self.core, self.first, self.second):
+            pl.semaphore_signal(barrier, inc=1, device_id=self.at(head), device_id_type=MESH)
+        if along_seq:
+
+            @pl.when(self.s > 0)
+            def _():
+                pl.semaphore_signal(
+                    barrier, inc=1, device_id=(self.s - 1, self.h), device_id_type=MESH
+                )
+
+            @pl.when(self.s < self.line - 1)
+            def _():
+                pl.semaphore_signal(
+                    barrier, inc=1, device_id=(self.s + 1, self.h), device_id_type=MESH
+                )
+
+            @pl.when((self.s > 0) & (self.s < self.line - 1))
+            def _():
+                pl.semaphore_wait(barrier, 5)
+
+            @pl.when((self.s == 0) | (self.s == self.line - 1))
+            def _():
+                pl.semaphore_wait(barrier, 4)
+        else:
+            pl.semaphore_wait(barrier, 3)
+
+
+class HeadGather:
+    SEMS = 7
+
+    def __init__(self, place, block, send, recv):
+        p = place
+        self.p = p
+        plan = (
+            (p.h, p.first, p.first),
+            (p.h, p.second, p.second),
+            (p.h, p.core, p.core),
+            (p.first, p.second, p.across),
+            (p.first, p.core, p.second + p.turn),
+            (p.second, p.core, p.first + p.turn),
+            (p.across, p.core, p.across + p.turn),
+        )
+        self.out = [
+            remote(block(j), block(j), send.at[i], recv.at[i], p.at(to))
+            for i, (j, to, _) in enumerate(plan)
+        ]
+        self.come = [
+            remote(block(j), block(j), send.at[i], recv.at[i], p.at(to))
+            for i, (_, to, j) in enumerate(plan)
+        ]
+
+    def start(self):
+        for i in (0, 1, 2):
+            self.out[i].start()
+
+    def got_first(self):
+        self.come[0].wait_recv()
+        self.out[3].start()
+        self.out[4].start()
+
+    def got_second(self):
+        self.come[1].wait_recv()
+        self.out[5].start()
+
+    def got_across(self):
+        self.come[3].wait_recv()
+        self.out[6].start()
+
+    def got_core(self):
+        self.come[2].wait_recv()
+
+    def got_core_second(self):
+        self.come[4].wait_recv()
+
+    def got_core_first(self):
+        self.come[5].wait_recv()
+
+    def got_core_across(self):
+        self.come[6].wait_recv()
+
+    def finish(self):
+        for copy in self.out:
+            copy.wait_send()
+
+
+class LineGather:
+    def __init__(self, place, piece, up_send, up_recv, down_send, down_recv):
+        self.p, self.piece = place, piece
+        self.up = (up_send, up_recv)
+        self.down = (down_send, down_recv)
+
+    def _up(self, owner, t):
+        p = self.p
+        return remote(
+            self.piece(owner), self.piece(owner), self.up[0].at[t], self.up[1].at[t], (p.s + 1, p.h)
+        )
+
+    def _down(self, owner, t):
+        p = self.p
+        return remote(
+            self.piece(owner),
+            self.piece(owner),
+            self.down[0].at[t],
+            self.down[1].at[t],
+            (p.s - 1, p.h),
+        )
+
+    def start(self, t):
+        p = self.p
+
+        @pl.when((p.s < p.line - 1) & (p.s >= t))
+        def _():
+            self._up(p.s - t, t).start()
+
+        @pl.when((p.s > 0) & (p.s + t < p.line))
+        def _():
+            self._down(p.s + t, t).start()
+
+    def got(self, t):
+        p = self.p
+
+        @pl.when(p.s >= t + 1)
+        def _():
+            self._up(p.s - 1 - t, t).wait_recv()
+
+        @pl.when(p.s + 1 + t < p.line)
+        def _():
+            self._down(p.s + 1 + t, t).wait_recv()
+
+    def step(self, t):
+        self.got(t)
+        if t + 1 < self.p.line - 1:
+            self.start(t + 1)
+
+    def finish(self):
+        p = self.p
+        for t in range(p.line - 1):
+
+            @pl.when((p.s < p.line - 1) & (p.s >= t))
+            def _():
+                self._up(p.s - t, t).wait_send()
+
+            @pl.when((p.s > 0) & (p.s + t < p.line))
+            def _():
+                self._down(p.s + t, t).wait_send()
+
+
+def line_sems(line, tensors=1):
+    return [pltpu.SemaphoreType.DMA((line - 1,)) for _ in range(4 * tensors)]
+
+
+def norm_rows(rows, gain):
+    inverse = lax.rsqrt(jnp.mean(rows * rows, axis=-1, keepdims=True) + EPS)
+    return rows * inverse * gain
+
+
+def project_kernel(
+    line,
+    tokens,
+    gain,
+    wq,
+    wk,
+    wv,
+    normed_out,
+    qkv_out,
+    weight_out,
+    normed,
+    weight,
+    g_send,
+    g_recv,
+    us,
+    ur,
+    ds,
+    dr,
+    keep,
+):
+    p = Place(line)
+    rows, width = tokens.shape
+    slab, part = wq.shape
+    weight_own = weight.at[pl.ds(pl.multiple_of(p.s * slab, slab), slab)]
+    weight_own[:, 0:part] = wq[...]
+    weight_own[:, part : 2 * part] = wk[...]
+    weight_own[:, 2 * part : 3 * part] = wv[...]
+    block = lambda j: normed.at[pl.ds(pl.multiple_of(j * rows, rows), rows)]
+    home = lambda j: normed_out.at[pl.ds(pl.multiple_of(j * rows, rows), rows)]
+    piece = lambda d: weight.at[pl.ds(pl.multiple_of(d * slab, slab), slab)]
+    gather = HeadGather(p, block, g_send, g_recv)
+    line_gather = LineGather(p, piece, us, ur, ds, dr)
+    p.greet()
+    line_gather.start(0)
+    mine = block(p.h)
+    step = 32
+
+    @pl.loop(0, rows // step)
+    def _(i):
+        at = pl.ds(pl.multiple_of(i * step, step), step)
+        mine[at] = norm_rows(tokens[at].astype(F32), gain[...]).astype(BF16)
+
+    gather.start()
+
+    def multiply(j):
+        start = pl.multiple_of(j * rows, rows)
+
+        @pl.loop(0, 3)
+        def _(n):
+            cols = pl.ds(pl.multiple_of(n * part, part), part)
+            qkv_out[pl.ds(start, rows), cols] = jnp.dot(
+                normed[pl.ds(start, rows), :], weight[:, cols], preferred_element_type=F32
+            ).astype(BF16)
+
+    saved = []
+
+    def save(j):
+        copy = pltpu.make_async_copy(block(j), home(j), keep.at[len(saved)])
+        copy.start()
+        saved.append(copy)
+
+    save(p.h)
+    gather.got_core()
+    save(p.core)
+    line_gather.step(0)
+    gather.got_first()
+    gather.got_second()
+    save(p.first)
+    save(p.second)
+    line_gather.step(1)
+    gather.got_core_second()
+    gather.got_core_first()
+    save(p.second + p.turn)
+    save(p.first + p.turn)
+    line_gather.step(2)
+    out_copy = pltpu.make_async_copy(weight, weight_out, keep.at[8])
+    out_copy.start()
+    for j in (p.h, p.core, p.first, p.second):
+        multiply(j)
+    gather.got_across()
+    save(p.across)
+    for j in (p.second + p.turn, p.first + p.turn, p.across):
+        multiply(j)
+    gather.got_core_across()
+    save(p.across + p.turn)
+    multiply(p.across + p.turn)
+    gather.finish()
+    line_gather.finish()
+    for copy in saved:
+        copy.wait()
+    out_copy.wait()
+
+
+def any_spec():
+    return pl.BlockSpec(memory_space=pl.ANY)
+
+
+def vmem_spec():
+    return pl.BlockSpec(memory_space=pltpu.VMEM)
+
+
+def project(line, tokens, gain, wq, wk, wv):
+    rows, width = tokens.shape
+    slab, part = wq.shape
+    full = rows * 8
+    return pl.pallas_call(
+        functools.partial(project_kernel, line),
+        out_shape=(
+            jax.ShapeDtypeStruct((full, width), BF16),
+            jax.ShapeDtypeStruct((full, 3 * part), BF16),
+            jax.ShapeDtypeStruct((slab * line, 3 * part), BF16),
+        ),
+        in_specs=[vmem_spec()] * 5,
+        out_specs=(any_spec(), vmem_spec(), any_spec()),
+        scratch_shapes=[
+            pltpu.VMEM((full, width), BF16),
+            pltpu.VMEM((slab * line, 3 * part), BF16),
+            pltpu.SemaphoreType.DMA((7,)),
+            pltpu.SemaphoreType.DMA((7,)),
+            *line_sems(line),
+            pltpu.SemaphoreType.DMA((9,)),
+        ],
+        compiler_params=pltpu.CompilerParams(
+            collective_id=1, has_side_effects=True, vmem_limit_bytes=48 * MIB
+        ),
+        cost_estimate=pl.CostEstimate(
+            flops=2 * full * width * 3 * part, bytes_accessed=40 * MIB, transcendentals=0
+        ),
+    )(tokens, gain.reshape(1, width), wq, wk, wv)
+
+
+def fused(
+    tokens,
+    segment,
+    attn_gain,
+    query_weight,
+    key_weight,
+    value_weight,
+    out_weight,
+    ffn_gain,
+    gate_weight,
+    up_weight,
+    down_weight,
+    cotangent,
+):
+    own_rows = tokens.shape[0]
+    group = own_rows * lax.axis_size("head")
+    heads_here = query_weight.shape[1] // HEAD_DIM
+    offset = lax.axis_index("head") * own_rows
+    seq_index = lax.axis_index("seq")
+    block = min(512, group)
+    scale = HEAD_DIM ** (-0.5)
+    line = lax.axis_size("seq")
+    part = query_weight.shape[1]
+    normed_full, qkv, w_qkv = project(
+        line, tokens, attn_gain, query_weight, key_weight, value_weight
+    )
+    w_query, w_key, w_value = (w_qkv[:, i * part : (i + 1) * part] for i in range(3))
+    queries, keys, values = (qkv[:, i * part : (i + 1) * part] for i in range(3))
+    w_out, w_gate, w_up, w_down = (
+        lax.all_gather(out_weight, "seq", axis=1, tiled=True),
+        lax.all_gather(gate_weight, "seq", axis=0, tiled=True),
+        lax.all_gather(up_weight, "seq", axis=0, tiled=True),
+        lax.all_gather(down_weight, "seq", axis=1, tiled=True),
+    )
+    inputs = tokens.astype(jnp.float32)
+    unit_one, inverse_one = normalize(inputs)
+    halo_keys, halo_values, halo_segs = ([], [], [])
+    hop = 1
+    take = min(group, WINDOW - (hop - 1) * group)
+    got_keys, got_values, got_segs = from_behind(
+        (keys[group - take :], values[group - take :], segment[group - take :]), "seq", hop
+    )
+    halo_keys.append(got_keys)
+    halo_values.append(got_values)
+    halo_segs.append(got_segs)
+    keys_ext = jnp.concatenate(halo_keys + [keys], axis=0)
+    values_ext = jnp.concatenate(halo_values + [values], axis=0)
+    segs_ext = jnp.concatenate(halo_segs + [segment], axis=0)
+    positions = seq_index * group - WINDOW + jnp.arange(WINDOW + group)
+    valid = positions >= 0
+    query_heads = queries.reshape(group, heads_here, HEAD_DIM)
+    key_heads = keys_ext.reshape(WINDOW + group, heads_here, HEAD_DIM)
+    value_heads = values_ext.reshape(WINDOW + group, heads_here, HEAD_DIM)
+    outputs, logsums = ([], [])
+    for start in range(0, group, block):
+        scores = block_scores(query_heads, key_heads, segment, segs_ext, valid, start, block)
+        highest = jnp.max(scores, axis=-1, keepdims=True)
+        weights = jnp.exp(scores - highest)
+        total = jnp.sum(weights, axis=-1, keepdims=True)
+        probs = (weights / total).astype(jnp.bfloat16)
+        outputs.append(
+            jnp.einsum(
+                "hqk,khd->qhd",
+                probs,
+                value_heads[start : start + block + WINDOW],
+                preferred_element_type=jnp.float32,
+            )
+        )
+        logsums.append(highest + jnp.log(total))
+    attended = (
+        jnp.concatenate(outputs, axis=0).reshape(group, heads_here * HEAD_DIM).astype(jnp.bfloat16)
+    )
+    partial_out = product(attended, w_out)
+    own_part = lax.dynamic_slice_in_dim(partial_out, offset, own_rows, 0)
+    placed = lax.dynamic_update_slice_in_dim(partial_out, own_part + inputs, offset, 0)
+    middle_full = lax.psum(placed, "head")
+    middle = lax.dynamic_slice_in_dim(middle_full, offset, own_rows, 0)
+    unit_full, inverse_full = normalize(middle_full)
+    normed_two_full = (unit_full * ffn_gain).astype(jnp.bfloat16)
+    unit_two, inverse_two = normalize(middle)
+    gate = product(normed_two_full, w_gate)
+    up = product(normed_two_full, w_up)
+    sigmoid = jax.nn.sigmoid(gate)
+    activated = gate * sigmoid
+    hidden = (activated * up).astype(jnp.bfloat16)
+    ffn_out = lax.psum_scatter(
+        product(hidden, w_down).astype(jnp.bfloat16), "head", scatter_dimension=0, tiled=True
+    ).astype(jnp.float32)
+    result = middle + ffn_out
+    grad_out = lax.all_gather(cotangent, "head", axis=0, tiled=True)
+    grad_hidden = product_nt(grad_out, w_down)
+    grad_gate = (grad_hidden * up * sigmoid * (1.0 + gate * (1.0 - sigmoid))).astype(jnp.bfloat16)
+    grad_up = (grad_hidden * activated).astype(jnp.bfloat16)
+    down_grad = product_tn(hidden, grad_out)
+    gate_grad = product_tn(normed_two_full, grad_gate)
+    up_grad = product_tn(normed_two_full, grad_up)
+    grad_normed_two = lax.psum_scatter(
+        (product_nt(grad_gate, w_gate) + product_nt(grad_up, w_up)).astype(jnp.bfloat16),
+        "head",
+        scatter_dimension=0,
+        tiled=True,
+    ).astype(jnp.float32)
+    ffn_gain_part = jnp.sum(grad_normed_two * unit_two, axis=0)
+    grad_middle = cotangent.astype(jnp.float32) + norm_back(
+        unit_two, inverse_two, ffn_gain, grad_normed_two
+    )
+    grad_branch = lax.all_gather(grad_middle.astype(jnp.bfloat16), "head", axis=0, tiled=True)
+    out_grad = product_tn(attended, grad_branch)
+    grad_attended = product_nt(grad_branch, w_out).astype(jnp.bfloat16)
+    grad_heads = grad_attended.reshape(group, heads_here, HEAD_DIM)
+    grad_query_list = []
+    grad_keys_ext = jnp.zeros((WINDOW + group, heads_here, HEAD_DIM), jnp.float32)
+    grad_values_ext = jnp.zeros((WINDOW + group, heads_here, HEAD_DIM), jnp.float32)
+    for number, start in enumerate(range(0, group, block)):
+        scores = block_scores(query_heads, key_heads, segment, segs_ext, valid, start, block)
+        probs = jnp.exp(scores - logsums[number])
+        probs_low = probs.astype(jnp.bfloat16)
+        key_part = key_heads[start : start + block + WINDOW]
+        value_part = value_heads[start : start + block + WINDOW]
+        query_part = query_heads[start : start + block]
+        grad_part = grad_heads[start : start + block]
+        grad_probs = jnp.einsum(
+            "qhd,khd->hqk", grad_part, value_part, preferred_element_type=jnp.float32
+        )
+        inner = jnp.sum(probs * grad_probs, axis=-1, keepdims=True)
+        grad_scores = (probs * (grad_probs - inner)).astype(jnp.bfloat16)
+        grad_query_list.append(
+            jnp.einsum("hqk,khd->qhd", grad_scores, key_part, preferred_element_type=jnp.float32)
+            * scale
+        )
+        key_term = (
+            jnp.einsum("hqk,qhd->khd", grad_scores, query_part, preferred_element_type=jnp.float32)
+            * scale
+        )
+        value_term = jnp.einsum(
+            "hqk,qhd->khd", probs_low, grad_part, preferred_element_type=jnp.float32
+        )
+        grad_keys_ext = grad_keys_ext.at[start : start + block + WINDOW].add(key_term)
+        grad_values_ext = grad_values_ext.at[start : start + block + WINDOW].add(value_term)
+    grad_keys_ext = grad_keys_ext.reshape(WINDOW + group, heads_here * HEAD_DIM)
+    grad_values_ext = grad_values_ext.reshape(WINDOW + group, heads_here * HEAD_DIM)
+    grad_keys = grad_keys_ext[WINDOW:]
+    grad_values = grad_values_ext[WINDOW:]
+    cursor = 0
+    hop = 1
+    take = min(group, WINDOW - (hop - 1) * group)
+    back_keys = from_behind(
+        grad_keys_ext[cursor : cursor + take].astype(jnp.bfloat16), "seq", -hop
+    ).astype(jnp.float32)
+    back_values = from_behind(
+        grad_values_ext[cursor : cursor + take].astype(jnp.bfloat16), "seq", -hop
+    ).astype(jnp.float32)
+    grad_keys = grad_keys.at[group - take :].add(back_keys)
+    grad_values = grad_values.at[group - take :].add(back_values)
+    grad_queries = (
+        jnp.concatenate(grad_query_list, axis=0)
+        .reshape(group, heads_here * HEAD_DIM)
+        .astype(jnp.bfloat16)
+    )
+    grad_keys = grad_keys.astype(jnp.bfloat16)
+    grad_values = grad_values.astype(jnp.bfloat16)
+    query_grad = product_tn(normed_full, grad_queries)
+    key_grad = product_tn(normed_full, grad_keys)
+    value_grad = product_tn(normed_full, grad_values)
+    grad_normed_one = lax.psum_scatter(
+        (
+            product_nt(grad_queries, w_query)
+            + product_nt(grad_keys, w_key)
+            + product_nt(grad_values, w_value)
+        ).astype(jnp.bfloat16),
+        "head",
+        scatter_dimension=0,
+        tiled=True,
+    ).astype(jnp.float32)
+    attn_gain_part = jnp.sum(grad_normed_one * unit_one, axis=0)
+    input_grad = grad_middle + norm_back(unit_one, inverse_one, attn_gain, grad_normed_one)
+    summed = (
+        lax.psum_scatter(
+            query_grad.astype(jnp.bfloat16), "seq", scatter_dimension=0, tiled=True
+        ).astype(jnp.float32),
+        lax.psum_scatter(
+            key_grad.astype(jnp.bfloat16), "seq", scatter_dimension=0, tiled=True
+        ).astype(jnp.float32),
+        lax.psum_scatter(
+            value_grad.astype(jnp.bfloat16), "seq", scatter_dimension=0, tiled=True
+        ).astype(jnp.float32),
+        lax.psum_scatter(
+            out_grad.astype(jnp.bfloat16), "seq", scatter_dimension=1, tiled=True
+        ).astype(jnp.float32),
+        lax.psum_scatter(
+            gate_grad.astype(jnp.bfloat16), "seq", scatter_dimension=0, tiled=True
+        ).astype(jnp.float32),
+        lax.psum_scatter(
+            up_grad.astype(jnp.bfloat16), "seq", scatter_dimension=0, tiled=True
+        ).astype(jnp.float32),
+        lax.psum_scatter(
+            down_grad.astype(jnp.bfloat16), "seq", scatter_dimension=1, tiled=True
+        ).astype(jnp.float32),
+    )
+    gain_grads = (
+        lax.psum_scatter(attn_gain_part, ("seq", "head"), scatter_dimension=0, tiled=True),
+        lax.psum_scatter(ffn_gain_part, ("seq", "head"), scatter_dimension=0, tiled=True),
+    )
+    return (
+        result.astype(jnp.bfloat16),
+        input_grad,
+        gain_grads[0],
+        summed[0],
+        summed[1],
+        summed[2],
+        summed[3],
+        gain_grads[1],
+        summed[4],
+        summed[5],
+        summed[6],
+    )
+
+
 def solution(mesh):
     placed = (
         P(("seq", "head"), None),
@@ -302,8 +847,9 @@
         P("head", "seq"),
         P(("seq", "head"), None),
     )
+    body = fused if mesh.shape["head"] == 8 else local
     return jax.shard_map(
-        local,
+        body,
         mesh=mesh,
         in_specs=placed,
         out_specs=(

time: 1570 us -> 1520 us (0.968)
  waiting for transfers between devices: 990 us -> 833 us
  Pallas kernels: 0 us -> 90.1 us
  local copies, waits for them, and re-layouts: 41.8 us -> 79.9 us
  matrix products: 359 us -> 339 us
    all_gather x10 -> x6, waiting for transfers between devices: 362 us -> 226 us  [the longest x1 72.8 us: fused(): grad_out = lax.all_gather(cotangent, 'head', axis=0, tiled=True)]
    pallas_call x0 -> x1, Pallas kernels: none -> 90.1 us  [project(): pl.pallas_call(functools.partial(project_kernel, line), out_shape=(jax.Sh...]
    dot_general x7 -> x4, matrix products: 81.1 us -> 58.1 us  [product(): return jnp.dot(left, right, preferred_element_type=jnp.float32)]
    slice x8 -> x14, local copies, waits for them, and re-layouts: 10.8 us -> 27.3 us  [the longest x6 13.8 us: block_scores(): key_part = key_heads[start:start + block + WINDOW]]
    unnamed x255 -> x252, local copies, waits for them, and re-layouts: 25.8 us -> 34.5 us
    convert_element_type x16 -> x15, other arithmetic: 45.8 us -> 47.3 us  [the longest x6 22.5 us: fused(): grad_scores = (probs * (grad_probs - inner)).astype(jnp.bfloat16)]
  transfers between devices with their start and end apart: 26 -> 22, of which waited for: 18 -> 12; matrix products, arithmetic and copies ran while one was open for 25% -> 26% of each run, Pallas kernels for 0% -> 6%
where the time goes in v1:
time: 1520 us; the launch traced here: 1510 us
  waiting for transfers between devices  833 us (55%)
  matrix products  339 us (22%)
  other arithmetic  99.9 us (7%)
  Pallas kernels  90.1 us (6%)
  local copies, waits for them, and re-layouts  79.9 us (5%)
  blocking collectives  39.8 us (3%)
  between operations  16 us (1%)
    psum x1, waiting for transfers between devices, fused(): middle_full = lax.psum(placed, 'head')  305 us
    dot_general x7, matrix products, product_nt(): lax.dot_general(left, right, (((1,), (1,)), ((), ())), preferred_element_...  114 us
    reduce_scatter x1, waiting for transfers between devices, fused(): lax.psum_scatter((product_nt(grad_queries, w_query) + product_nt(grad_key...  92.7 us
    reduce_scatter x1, waiting for transfers between devices, fused(): lax.psum_scatter((product_nt(grad_gate, w_gate) + product_nt(grad_up, w_u...  90.3 us
    pallas_call x1, Pallas kernels, project(): pl.pallas_call(functools.partial(project_kernel, line), out_shape=(jax.Sh...  90.1 us
    dot_general x7, matrix products, product_tn(): lax.dot_general(left, right, (((0,), (0,)), ((), ())), preferred_element_...  79.9 us
    all_gather x1, waiting for transfers between devices, fused(): grad_out = lax.all_gather(cotangent, 'head', axis=0, tiled=True)  72.8 us
    dot_general x4, matrix products, product(): return jnp.dot(left, right, preferred_element_type=jnp.float32)  58.1 us
  transfers between devices with their start and end apart: 22, of which 12 were waited for; matrix products, arithmetic and copies ran while one was open for 26% of the time, Pallas kernels for 6%

profile of v1, /device:TPU:0, one launch (start us, length us, event | category | flops | bytes accessed | tf_op | source)
XLA Modules:
  0.0 1510.7 jit_solution(4659833830568773581)
XLA Ops:
  18.5 90.1 %shard_map.203 = (bf16[3072,2048]{1,0:T(8,128)(2,1)}, bf16[3072,768]{1,0:T(8,128)(2,1)}, bf16[2048,768]{1,0:T(8,128)(2,1)S(1)}) custom-call(bf16[384,2048]{1,0:T(8,128)(2,1)S(1)} %copy-done, f32[1,2048]{1,0:T(1,128)S(1)} %bitcast.272, bf16[512,256]{1,0:T(8,128)(2,1)S(1)} %copy-done.5, bf16[512,256]{1,0:T(8,128)(2,1)S(1)} %copy-done.6, ...), custom_call_target="tpu_custom_call" | custom-call | flops 9663676416 | bytes 41943040 | tf_op jit(solution)/shard_map/pallas_call | solution.py:591
  200.4 13.6 fusion.207
  221.2 304.7 %all-reduce.7.cloned.1.call-done = f32[3072,2048]{1,0:T(8,128)} async-done(((f32[3072,2048]{1,0:T(8,128)}), f32[3072,2048]{1,0:T(8,128)}) %all-reduce.7.cloned.1.call-update) | async-done | bytes 25165840 | tf_op jit(solution)/shard_map/psum | solution.py:692
  525.9 10.6 multiply_reduce_fusion
  548.3 37.4 %all-gather.11.cloned.1.call-done = bf16[2048,688]{0,1:T(8,128)(2,1)} async-done(((bf16[512,688]{0,1:T(8,128)(2,1)}), bf16[2048,688]{0,1:T(8,128)(2,1)}) %all-gather.11.cloned.1.call-update) | async-done | bytes 2818064 | tf_op jit(solution)/shard_map/all_gather | solution.py:648
  585.8 14.9 fusion.209
  600.6 43.5 %all-gather.9.cloned.1.call-done = bf16[2048,688]{0,1:T(8,128)(2,1)} async-done(((bf16[512,688]{0,1:T(8,128)(2,1)}), bf16[2048,688]{0,1:T(8,128)(2,1)}) %all-gather.9.cloned.1.call-update) | async-done | bytes 2818064 | tf_op jit(solution)/shard_map/all_gather | solution.py:647
  644.1 14.9 fusion.208
  659.0 43.5 %all-gather.13.cloned.1.call-done = bf16[688,2048]{1,0:T(8,128)(2,1)} async-done(((bf16[688,512]{1,0:T(8,128)(2,1)}), bf16[688,2048]{1,0:T(8,128)(2,1)}) %all-gather.13.cloned.1.call-update) | async-done | bytes 2818064 | tf_op jit(solution)/shard_map/all_gather | solution.py:649
  702.4 72.8 %all-gather.15.cloned.1.call-done = bf16[3072,2048]{1,0:T(8,128)(2,1)} async-done(((bf16[384,2048]{1,0:T(8,128)(2,1)}), bf16[3072,2048]{1,0:T(8,128)(2,1)}) %all-gather.15.cloned.1.call-update) | async-done | bytes 12582928 | tf_op jit(solution)/shard_map/all_gather | solution.py:706
  775.2 22.4 %multiply_convert_fusion.1 = (bf16[3072,688]{0,1:T(8,128)(2,1)}, bf16[3072,688]{0,1:T(8,128)(2,1)}, bf16[3072,688]{0,1:T(8,128)(2,1)}) fusion(f32[3072,688]{0,1:T(8,128)} %fusion.208, f32[3072,688]{0,1:T(8,128)} %fusion.209, bf16[3072,2048]{1,0:T(8,128)(2,1)} %all-gather.15.cloned.1.call-done, bf16[688,2048]{1,0:T(8,128)(2,1)} %all-gather.13.cloned.1.call-done), kind=kOutput, calls=%fused_computation.5 | convolution fusion | flops 8688746496 | bytes 44990464 | tf_op jit(solution)/shard_map/dot_general | solution.py:35
  797.6 17.2 %fusion.210 = f32[3072,2048]{1,0:T(8,128)} fusion(bf16[3072,688]{0,1:T(8,128)(2,1)} %get-tuple-element.194, bf16[2048,688]{0,1:T(8,128)(2,1)} %all-gather.9.cloned.1.call-done), kind=kOutput, calls=%fused_computation.285 | convolution fusion | flops 8657043456 | bytes 32210944 | tf_op jit(solution)/shard_map/dot_general | solution.py:35
  814.8 19.3 %add_convert_fusion.1 = bf16[3072,2048]{1,0:T(8,128)(2,1)} fusion(f32[3072,2048]{1,0:T(8,128)} %fusion.210, bf16[3072,688]{0,1:T(8,128)(2,1)} %get-tuple-element.193, bf16[2048,688]{0,1:T(8,128)(2,1)} %all-gather.11.cloned.1.call-done), kind=kOutput, calls=%fused_computation.1 | convolution fusion | flops 8669626368 | bytes 44793856 | tf_op jit(solution)/shard_map/dot_general | solution.py:35
  836.4 90.3 %reduce-scatter.13.cloned.1.call-done = bf16[384,2048]{1,0:T(8,128)(2,1)} async-done(((bf16[3072,2048]{1,0:T(8,128)(2,1)}), bf16[384,2048]{1,0:T(8,128)(2,1)}) %reduce-scatter.13.cloned.1.call-update) | async-done | bytes 1572880 | tf_op jit(solution)/shard_map/reduce_scatter | solution.py:713
  935.6 14.3 convolution_convert_fusion.4
  950.1 14.5 convolution_convert_fusion.2
  964.8 14.3 convolution_convert_fusion.3
  979.4 28.4 %all-gather.17.cloned.1.call-done = bf16[3072,2048]{1,0:T(8,128)(2,1)} async-done(((bf16[384,2048]{1,0:T(8,128)(2,1)}), bf16[3072,2048]{1,0:T(8,128)(2,1)}) %all-gather.17.cloned.1.call-update) | async-done | bytes 12582928 | tf_op jit(solution)/shard_map/all_gather | solution.py:723
  1007.8 8.2 convolution_convert_fusion.1
  1109.1 9.5 convolution_convert_fusion.8
  1127.7 9.8 convolution_convert_fusion.7
  1137.7 12.0 fusion.155
  1168.9 9.9 convolution_convert_fusion.6
  1178.8 11.9 fusion.153
  1190.7 22.7 %add_convert_fusion = bf16[3072,2048]{1,0:T(8,128)(2,1)} fusion(f32[3072,2048]{1,0:T(8,128)} %fusion.155, f32[3072,2048]{1,0:T(8,128)} %fusion.153, bf16[2048,768]{1,0:T(8,128)(2,1)S(1)} %get-tuple-element.183, bf16[3072,256]{0,1:T(8,128)(2,1)} %copy-done.30), kind=kOutput, calls=%fused_computation | convolution fusion | flops 3240099840 | bytes 65536000 | tf_op jit(solution)/shard_map/dot_general | solution.py:35
  1215.2 14.8 convolution_convert_fusion
  1239.8 11.0 reduce-scatter.17.cloned.1.call-done
  1252.5 26.2 %reduce-scatter.21.cloned.1.call-done = bf16[512,256]{1,0:T(8,128)(2,1)} async-done(((bf16[2048,256]{1,0:T(8,128)(2,1)}), bf16[512,256]{1,0:T(8,128)(2,1)}) %reduce-scatter.21.cloned.1.call-update) | async-done | bytes 262160 | tf_op jit(solution)/shard_map/reduce_scatter | solution.py:800
  1280.5 26.3 %reduce-scatter.19.cloned.1.call-done = bf16[512,256]{1,0:T(8,128)(2,1)} async-done(((bf16[2048,256]{1,0:T(8,128)(2,1)}), bf16[512,256]{1,0:T(8,128)(2,1)}) %reduce-scatter.19.cloned.1.call-update) | async-done | bytes 262160 | tf_op jit(solution)/shard_map/reduce_scatter | solution.py:797
  1308.6 92.7 %reduce-scatter.15.cloned.1.call-done = bf16[384,2048]{1,0:T(8,128)(2,1)} async-done(((bf16[3072,2048]{1,0:T(8,128)(2,1)}), bf16[384,2048]{1,0:T(8,128)(2,1)}) %reduce-scatter.15.cloned.1.call-update) | async-done | bytes 1572880 | tf_op jit(solution)/shard_map/reduce_scatter | solution.py:781
  1403.8 39.8 %all-reduce.4 = (f32[2048]{0:T(1024)S(1)}, f32[2048]{0:T(1024)S(1)}) all-reduce(f32[2048]{0:T(1024)S(1)} %get-tuple-element.187, f32[2048]{0:T(1024)S(1)} %copy-done.85), channel_id=5, replica_groups=mesh['seq'=4,'head'=8] {'seq','head'}, use_global_device_ids=true, to_apply=%region_28.29.clone | all-reduce | flops 4096 | bytes 32768
  1444.7 52.9 %reduce-scatter.11.cloned.1.call-done = bf16[384,2048]{1,0:T(8,128)(2,1)} async-done(((bf16[3072,2048]{1,0:T(8,128)(2,1)}), bf16[384,2048]{1,0:T(8,128)(2,1)}) %reduce-scatter.11.cloned.1.call-update) | async-done | bytes 1572880 | tf_op jit(solution)/shard_map/reduce_scatter | solution.py:702
  (426 shorter events, 280.6 us)
Async XLA Ops:
  7.2 193.2 %all-gather.7.cloned.1.call-start = ((), (), s32[]{:S(2)}) async-start(), calls=%async_computation.10 | async-start | bytes 1310720 | tf_op jit(solution)/shard_map/all_gather | solution.py:646
  7.9 518.0 %all-reduce.7.cloned.1.call-start = ((), (), s32[]{:S(2)}) async-start(), calls=%async_computation.11 | async-start | bytes 50331648 | tf_op jit(solution)/shard_map/psum | solution.py:692
  8.6 133.2 %collective-permute-start.1 = (s32[1024]{0:T(1024)S(1)}, s32[1024]{0:T(1024)S(1)}, u32[]{:S(2)}, u32[]{:S(2)}) collective-permute-start(s32[1024]{0:T(1024)S(1)} %slice.648), channel_id=1, source_target_pairs={{0,8},{8,16},{16,24},{1,9},{9,17},{17,25},{2,10},{10,18},{18,26},{... | collective-permute-start | bytes 12296 | tf_op jit(solution)/shard_map/ppermute | solution.py:21
  18.5 96.7 %copy-start.68 = (s32[3072]{0:T(1024)S(1)}, s32[3072]{0:T(1024)}, u32[]{:S(2)}) copy-start(s32[3072]{0:T(1024)} %param.41) | copy-start | bytes 36868
  111.1 68.1 %collective-permute-start = (bf16[1024,256]{1,0:T(8,128)(2,1)}, bf16[1024,256]{1,0:T(8,128)(2,1)}, u32[]{:S(2)}, u32[]{:S(2)}) collective-permute-start(bf16[1024,256]{1,0:T(8,128)(2,1)} %get-tuple-element.210), channel_id=1, source_target_pairs={{0,8},{8,16},{16,24},{1,9},{9,17},{17,25},{2,10},{10,18},{18,26},{... | collective-permute-start | bytes 1572872 | tf_op jit(solution)/shard_map/ppermute | solution.py:21
  113.1 49.0 %collective-permute-start.2 = (bf16[1024,256]{1,0:T(8,128)(2,1)}, bf16[1024,256]{1,0:T(8,128)(2,1)}, u32[]{:S(2)}, u32[]{:S(2)}) collective-permute-start(bf16[1024,256]{1,0:T(8,128)(2,1)} %get-tuple-element.211), channel_id=1, source_target_pairs={{0,8},{8,16},{16,24},{1,9},{9,17},{17,25},{2,10},{10,18},{18,26},{... | collective-permute-start | bytes 1572872 | tf_op jit(solution)/shard_map/ppermute | solution.py:21
  153.1 39.6 %copy-start.73 = (f32[2,512]{1,0:T(2,128)}, f32[2,512]{1,0:T(2,128)S(1)}, u32[]{:S(2)}) copy-start(f32[2,512]{1,0:T(2,128)S(1)} %get-tuple-element.256) | copy-start | bytes 12292
  218.6 367.1 %all-gather.11.cloned.1.call-start = ((), (), s32[]{:S(2)}) async-start(), calls=%async_computation.13 | async-start | bytes 3522560 | tf_op jit(solution)/shard_map/all_gather | solution.py:648
  219.4 424.7 %all-gather.9.cloned.1.call-start = ((), (), s32[]{:S(2)}) async-start(), calls=%async_computation.12 | async-start | bytes 3522560 | tf_op jit(solution)/shard_map/all_gather | solution.py:647
  220.0 482.5 %all-gather.13.cloned.1.call-start = ((), (), s32[]{:S(2)}) async-start(), calls=%async_computation.14 | async-start | bytes 3522560 | tf_op jit(solution)/shard_map/all_gather | solution.py:649
  220.5 554.7 %all-gather.15.cloned.1.call-start = ((), (), s32[]{:S(2)}) async-start(), calls=%async_computation.16 | async-start | bytes 14155776 | tf_op jit(solution)/shard_map/all_gather | solution.py:706
  221.1 315.4 %copy-start.69 = (f32[2048]{0:T(1024)S(1)}, f32[2048]{0:T(1024)}, u32[]{:S(2)}) copy-start(f32[2048]{0:T(1024)} %param.47) | copy-start | bytes 24580
  221.1 705.6 %reduce-scatter.13.cloned.1.call-start = ((), (), s32[]{:S(2)}) async-start(), calls=%async_computation.17 | async-start | bytes 14155776 | tf_op jit(solution)/shard_map/reduce_scatter | solution.py:713
  834.1 173.7 %all-gather.17.cloned.1.call-start = ((), (), s32[]{:S(2)}) async-start(), calls=%async_computation.18 | async-start | bytes 14155776 | tf_op jit(solution)/shard_map/all_gather | solution.py:723
  836.4 99.1 %copy-start.83 = (f32[384]{0:T(512)}, f32[384]{0:T(512)S(1)}, u32[]{:S(2)}) copy-start(f32[384]{0:T(512)S(1)} %add_rsqrt_fusion.2) | copy-start | bytes 4612
  935.6 295.1 %reduce-scatter.29.cloned.1.call-start = ((), (), s32[]{:S(2)}) async-start(), calls=%async_computation.26 | async-start | bytes 3522560 | tf_op jit(solution)/shard_map/reduce_scatter | solution.py:812
  950.0 283.1 %reduce-scatter.27.cloned.1.call-start = ((), (), s32[]{:S(2)}) async-start(), calls=%async_computation.25 | async-start | bytes 3522560 | tf_op jit(solution)/shard_map/reduce_scatter | solution.py:809
  964.6 271.0 %reduce-scatter.25.cloned.1.call-start = ((), (), s32[]{:S(2)}) async-start(), calls=%async_computation.24 | async-start | bytes 3522560 | tf_op jit(solution)/shard_map/reduce_scatter | solution.py:806
  979.2 258.8 %reduce-scatter.23.cloned.1.call-start = ((), (), s32[]{:S(2)}) async-start(), calls=%async_computation.23 | async-start | bytes 1310720 | tf_op jit(solution)/shard_map/reduce_scatter | solution.py:803
  1062.0 94.3 %collective-permute-start.4 = (bf16[1024,256]{0,1:T(8,128)(2,1)}, bf16[1024,256]{0,1:T(8,128)(2,1)}, u32[]{:S(2)}, u32[]{:S(2)}) collective-permute-start(bf16[1024,256]{0,1:T(8,128)(2,1)} %bitcast.38), channel_id=1, source_target_pairs={{8,0},{16,8},{24,16},{9,1},{17,9},{25,17},{10,2},{18,10},{26,18},{... | collective-permute-start | bytes 1572872 | tf_op jit(solution)/shard_map/ppermute | solution.py:21
  1102.0 64.5 %collective-permute-start.3 = (bf16[1024,256]{0,1:T(8,128)(2,1)}, bf16[1024,256]{0,1:T(8,128)(2,1)}, u32[]{:S(2)}, u32[]{:S(2)}) collective-permute-start(bf16[1024,256]{0,1:T(8,128)(2,1)} %bitcast.29), channel_id=1, source_target_pairs={{8,0},{16,8},{24,16},{9,1},{17,9},{25,17},{10,2},{18,10},{26,18},{... | collective-permute-start | bytes 1572872 | tf_op jit(solution)/shard_map/ppermute | solution.py:21
  1118.6 132.2 %reduce-scatter.17.cloned.1.call-start = ((), (), s32[]{:S(2)}) async-start(), calls=%async_computation.20 | async-start | bytes 1310720 | tf_op jit(solution)/shard_map/reduce_scatter | solution.py:794
  1137.5 141.3 %reduce-scatter.21.cloned.1.call-start = ((), (), s32[]{:S(2)}) async-start(), calls=%async_computation.22 | async-start | bytes 1310720 | tf_op jit(solution)/shard_map/reduce_scatter | solution.py:800
  1166.5 140.3 %reduce-scatter.19.cloned.1.call-start = ((), (), s32[]{:S(2)}) async-start(), calls=%async_computation.21 | async-start | bytes 1310720 | tf_op jit(solution)/shard_map/reduce_scatter | solution.py:797
  1190.7 210.6 %reduce-scatter.15.cloned.1.call-start = ((), (), s32[]{:S(2)}) async-start(), calls=%async_computation.19 | async-start | bytes 14155776 | tf_op jit(solution)/shard_map/reduce_scatter | solution.py:781
  1213.4 284.2 %reduce-scatter.11.cloned.1.call-start = ((), (), s32[]{:S(2)}) async-start(), calls=%async_computation.15 | async-start | bytes 14155776 | tf_op jit(solution)/shard_map/reduce_scatter | solution.py:702
  1233.1 168.2 %copy-start.2 = (bf16[384,2048]{1,0:T(8,128)(2,1)S(1)}, bf16[384,2048]{1,0:T(8,128)(2,1)}, u32[]{:S(2)}) copy-start(bf16[384,2048]{1,0:T(8,128)(2,1)} %tokens.1) | copy-start | bytes 4718596
  1233.1 168.2 %copy-start.4 = (f32[2048]{0:T(1024)S(1)}, f32[2048]{0:T(1024)}, u32[]{:S(2)}) copy-start(f32[2048]{0:T(1024)} %param.42) | copy-start | bytes 24580
  1235.6 168.2 %copy-start.85 = (f32[2048]{0:T(1024)S(1)}, f32[2048]{0:T(1024)}, u32[]{:S(2)}) copy-start(f32[2048]{0:T(1024)} %get-tuple-element.185) | copy-start | bytes 24580
  1235.6 262.1 %copy-start.70 = (f32[2048]{0:T(1024)S(1)}, f32[2048]{0:T(1024)}, u32[]{:S(2)}) copy-start(f32[2048]{0:T(1024)} %param.47) | copy-start | bytes 24580
  1235.6 262.1 %copy-start.84 = (f32[384]{0:T(512)S(1)}, f32[384]{0:T(512)}, u32[]{:S(2)}) copy-start(f32[384]{0:T(512)} %copy-done.83) | copy-start | bytes 4612
  1235.6 262.1 %copy-start.87 = (f32[384]{0:T(512)S(1)}, f32[384]{0:T(512)}, u32[]{:S(2)}) copy-start(f32[384]{0:T(512)} %copy-done.86) | copy-start | bytes 4612
  (115 other events, 867.1 us)
Sparse Core Ops, SparseCore 0:
  9.6 43.8 all-gather.6
  218.8 307.0 all-reduce.6
  527.6 58.1 all-gather.10
  587.3 56.7 all-gather.8
  645.6 56.7 all-gather.12
  704.3 70.8 all-gather.14
  834.3 92.3 reduce-scatter.12
  935.7 72.1 all-gather.16
  1010.3 55.1 reduce-scatter.28
  1067.6 68.7 reduce-scatter.26
  1138.9 54.4 reduce-scatter.24
  1195.6 26.9 reduce-scatter.22
  1224.9 25.7 reduce-scatter.16
  1252.9 25.7 reduce-scatter.20
  1281.0 25.7 reduce-scatter.18
  1310.2 91.0 reduce-scatter.14
  1404.6 92.9 reduce-scatter.10

commit v2 on v1

--- a/solution.py
+++ b/solution.py
@@ -357,7 +357,7 @@
 class HeadGather:
     SEMS = 7
 
-    def __init__(self, place, block, send, recv):
+    def __init__(self, place, block, send, recv, own=None):
         p = place
         self.p = p
         plan = (
@@ -370,7 +370,13 @@
             (p.across, p.core, p.across + p.turn),
         )
         self.out = [
-            remote(block(j), block(j), send.at[i], recv.at[i], p.at(to))
+            remote(
+                block(j) if own is None or i > 2 else own,
+                block(j),
+                send.at[i],
+                recv.at[i],
+                p.at(to),
+            )
             for i, (j, to, _) in enumerate(plan)
         ]
         self.come = [
@@ -413,21 +419,23 @@
 
 
 class LineGather:
-    def __init__(self, place, piece, up_send, up_recv, down_send, down_recv):
-        self.p, self.piece = place, piece
+    def __init__(self, place, piece, up_send, up_recv, down_send, down_recv, own=None):
+        self.p, self.piece, self.own = place, piece, own
         self.up = (up_send, up_recv)
         self.down = (down_send, down_recv)
 
     def _up(self, owner, t):
         p = self.p
+        source = self.own if t == 0 and self.own is not None else self.piece(owner)
         return remote(
-            self.piece(owner), self.piece(owner), self.up[0].at[t], self.up[1].at[t], (p.s + 1, p.h)
+            source, self.piece(owner), self.up[0].at[t], self.up[1].at[t], (p.s + 1, p.h)
         )
 
     def _down(self, owner, t):
         p = self.p
+        source = self.own if t == 0 and self.own is not None else self.piece(owner)
         return remote(
-            self.piece(owner),
+            source,
             self.piece(owner),
             self.down[0].at[t],
             self.down[1].at[t],
@@ -481,6 +489,26 @@
 def norm_rows(rows, gain):
     inverse = lax.rsqrt(jnp.mean(rows * rows, axis=-1, keepdims=True) + EPS)
     return rows * inverse * gain
+
+
+def own_starts(segment):
+    count = segment.shape[1]
+    ids = segment[...]
+    place = lax.broadcasted_iota(jnp.int32, (1, count), 1)
+    starts = jnp.where((place > 0) & (ids != pltpu.roll(ids, 1, 1)), place, -1)
+    shift = 1
+    while shift < count:
+        earlier = jnp.where(place >= shift, pltpu.roll(starts, shift, 1), -1)
+        starts = jnp.maximum(starts, earlier)
+        shift *= 2
+    return starts
+
+
+def turned_over(source, target):
+    width = source.shape[1]
+    for start in range(0, width, 128):
+        stop = min(start + 128, width)
+        target[start:stop, :] = source[:, start:stop].T
 
 
 def project_kernel(
@@ -490,9 +518,15 @@
     wq,
     wk,
     wv,
+    segment,
+    w_gate,
+    w_up,
     normed_out,
     qkv_out,
     weight_out,
+    floor_out,
+    gate_out,
+    up_out,
     normed,
     weight,
     g_send,
@@ -502,10 +536,20 @@
     ds,
     dr,
     keep,
+    seg_halo,
+    seg_sems,
 ):
     p = Place(line)
     rows, width = tokens.shape
     slab, part = wq.shape
+    count = segment.shape[1]
+    seg_copy = remote(
+        segment.at[:, pl.ds(count - WINDOW, WINDOW)],
+        seg_halo,
+        seg_sems.at[0],
+        seg_sems.at[1],
+        (p.s + 1, p.h),
+    )
     weight_own = weight.at[pl.ds(pl.multiple_of(p.s * slab, slab), slab)]
     weight_own[:, 0:part] = wq[...]
     weight_own[:, part : 2 * part] = wk[...]
@@ -517,6 +561,11 @@
     line_gather = LineGather(p, piece, us, ur, ds, dr)
     p.greet()
     line_gather.start(0)
+
+    @pl.when(p.s < line - 1)
+    def _():
+        seg_copy.start()
+
     mine = block(p.h)
     step = 32
 
@@ -545,6 +594,22 @@
         saved.append(copy)
 
     save(p.h)
+    starts = own_starts(segment)
+    for source, target in ((w_gate, gate_out), (w_up, up_out)):
+        turned_over(source, target)
+
+    @pl.when(p.s > 0)
+    def _():
+        seg_copy.wait_recv()
+
+    before = jnp.sum(
+        (seg_halo[...] == segment[:, 0:1]).astype(jnp.int32), axis=1, keepdims=True
+    )
+    before = jnp.where(p.s > 0, before, 0)
+    floor_out[...] = jnp.maximum(
+        lax.broadcasted_iota(jnp.int32, (1, count), 1),
+        jnp.where(starts >= 0, starts + WINDOW, WINDOW - before),
+    )
     gather.got_core()
     save(p.core)
     line_gather.step(0)
@@ -571,6 +636,11 @@
     multiply(p.across + p.turn)
     gather.finish()
     line_gather.finish()
+
+    @pl.when(p.s < line - 1)
+    def _():
+        seg_copy.wait_send()
+
     for copy in saved:
         copy.wait()
     out_copy.wait()
@@ -584,7 +654,7 @@
     return pl.BlockSpec(memory_space=pltpu.VMEM)
 
 
-def project(line, tokens, gain, wq, wk, wv):
+def project(line, tokens, gain, wq, wk, wv, segment, w_gate, w_up):
     rows, width = tokens.shape
     slab, part = wq.shape
     full = rows * 8
@@ -594,9 +664,12 @@
             jax.ShapeDtypeStruct((full, width), BF16),
             jax.ShapeDtypeStruct((full, 3 * part), BF16),
             jax.ShapeDtypeStruct((slab * line, 3 * part), BF16),
+            jax.ShapeDtypeStruct((1, full), jnp.int32),
+            jax.ShapeDtypeStruct((w_gate.shape[1], slab), BF16),
+            jax.ShapeDtypeStruct((w_gate.shape[1], slab), BF16),
         ),
-        in_specs=[vmem_spec()] * 5,
-        out_specs=(any_spec(), vmem_spec(), any_spec()),
+        in_specs=[vmem_spec()] * 8,
+        out_specs=(any_spec(), vmem_spec(), any_spec(), vmem_spec(), vmem_spec(), vmem_spec()),
         scratch_shapes=[
             pltpu.VMEM((full, width), BF16),
             pltpu.VMEM((slab * line, 3 * part), BF16),
@@ -604,6 +677,8 @@
             pltpu.SemaphoreType.DMA((7,)),
             *line_sems(line),
             pltpu.SemaphoreType.DMA((9,)),
+            pltpu.VMEM((1, WINDOW), jnp.int32),
+            pltpu.SemaphoreType.DMA((2,)),
         ],
         compiler_params=pltpu.CompilerParams(
             collective_id=1, has_side_effects=True, vmem_limit_bytes=48 * MIB
@@ -611,7 +686,637 @@
         cost_estimate=pl.CostEstimate(
             flops=2 * full * width * 3 * part, bytes_accessed=40 * MIB, transcendentals=0
         ),
-    )(tokens, gain.reshape(1, width), wq, wk, wv)
+    )(tokens, gain.reshape(1, width), wq, wk, wv, segment.reshape(1, full), w_gate, w_up)
+
+
+LOG2E = 1.4426950408889634
+TILE = 256
+CHUNKS = WINDOW // TILE + 1
+
+
+def tile_scores(tile, head, q, k_ext, floor):
+    start = pl.multiple_of(tile * TILE, TILE)
+    cols = slice(head * HEAD_DIM, (head + 1) * HEAD_DIM)
+    queries = q[pl.ds(start, TILE), cols]
+    row = lax.broadcasted_iota(jnp.int32, (TILE, TILE), 0)
+    lane = lax.broadcasted_iota(jnp.int32, (TILE, TILE), 1)
+    lowest = floor[:, pl.ds(start, TILE)] - start
+    found = []
+    for i in range(CHUNKS):
+        keys = k_ext[pl.ds(start + i * TILE, TILE), cols]
+        scores = product_nt(keys, queries)
+        visible = row >= lowest - i * TILE
+        if i == CHUNKS - 1:
+            visible = visible & (row <= lane)
+        found.append((scores, visible))
+    return found
+
+
+def forward_tile(tile, q, k_ext, v_t, floor, attended, logs):
+    start = pl.multiple_of(tile * TILE, TILE)
+    sharp = HEAD_DIM ** (-0.5) * LOG2E
+    for head in range(q.shape[1] // HEAD_DIM):
+        cols = slice(head * HEAD_DIM, (head + 1) * HEAD_DIM)
+        found = [
+            jnp.where(visible, scores, NEG)
+            for scores, visible in tile_scores(tile, head, q, k_ext, floor)
+        ]
+        highest = functools.reduce(
+            jnp.maximum, [jnp.max(scores, axis=0, keepdims=True) for scores in found]
+        )
+        total = jnp.zeros((1, TILE), F32)
+        mixed = jnp.zeros((HEAD_DIM, TILE), F32)
+        for i, scores in enumerate(found):
+            weights = jnp.exp2((scores - highest) * sharp)
+            total = total + jnp.sum(weights, axis=0, keepdims=True)
+            mixed = mixed + product(
+                v_t[cols, pl.ds(start + i * TILE, TILE)], weights.astype(BF16)
+            )
+        attended[pl.ds(start, TILE), cols] = (mixed / total).astype(BF16).T
+        logs[head : head + 1, pl.ds(start, TILE)] = highest * sharp + jnp.log2(total)
+
+
+def attend_kernel(
+    line,
+    qkv,
+    floor,
+    cot,
+    w_out,
+    gate_a,
+    attended,
+    logs,
+    halo_out,
+    cot_out,
+    w_out_full,
+    gate_full,
+    q,
+    k_ext,
+    v_ext,
+    v_t,
+    g_send,
+    g_recv,
+    *sems,
+):
+    p = Place(line)
+    out_sems, gate_sems, halo_send, halo_recv, keep = sems[0:4], sems[4:8], *sems[8:11]
+    rows = cot.shape[0]
+    count, part = q.shape
+    p.greet()
+    block = lambda j: cot_out.at[pl.ds(pl.multiple_of(j * rows, rows), rows)]
+    gather = HeadGather(p, block, g_send, g_recv, own=cot)
+    halo = [
+        remote(
+            qkv.at[pl.ds(count - WINDOW, WINDOW), pl.ds((1 + i) * part, part)],
+            ext.at[pl.ds(0, WINDOW)],
+            halo_send.at[i],
+            halo_recv.at[i],
+            (p.s + 1, p.h),
+        )
+        for i, ext in enumerate((k_ext, v_ext))
+    ]
+
+    @pl.when(p.s < line - 1)
+    def _():
+        halo[0].start()
+        halo[1].start()
+
+    gather.start()
+    loads = [
+        pltpu.make_async_copy(qkv.at[:, pl.ds(0, part)], q, keep.at[0]),
+        pltpu.make_async_copy(
+            qkv.at[:, pl.ds(part, part)], k_ext.at[pl.ds(WINDOW, count)], keep.at[1]
+        ),
+        pltpu.make_async_copy(
+            qkv.at[:, pl.ds(2 * part, part)], v_ext.at[pl.ds(WINDOW, count)], keep.at[2]
+        ),
+    ]
+    for copy in loads:
+        copy.start()
+    out_gather = LineGather(p, lambda d: w_out_full.at[d], *out_sems, own=w_out)
+    gate_gather = LineGather(p, lambda d: gate_full.at[d], *gate_sems, own=gate_a)
+    out_gather.start(0)
+    own = [
+        pltpu.make_async_copy(cot, block(p.h), keep.at[3]),
+        pltpu.make_async_copy(w_out, w_out_full.at[p.s], keep.at[4]),
+        pltpu.make_async_copy(gate_a, gate_full.at[p.s], keep.at[5]),
+    ]
+    for copy in own:
+        copy.start()
+
+    @pl.when(p.s == 0)
+    def _():
+        k_ext[0:WINDOW, :] = jnp.zeros((WINDOW, part), BF16)
+        v_ext[0:WINDOW, :] = jnp.zeros((WINDOW, part), BF16)
+
+    for copy in loads:
+        copy.wait()
+
+    def turn(first, last):
+        @pl.loop(first, last)
+        def _(i):
+            at = pl.ds(pl.multiple_of(i * TILE, TILE), TILE)
+            v_t[:, at] = v_ext[at, :].T
+
+    def tiles(first, last):
+        @pl.loop(first, last)
+        def _(tile):
+            forward_tile(tile, q, k_ext, v_t, floor, attended, logs)
+
+    ahead = WINDOW // TILE
+    turn(ahead, ahead + count // TILE)
+    tiles(ahead, count // TILE)
+    out_gather.step(0)
+    gate_gather.start(0)
+
+    @pl.when(p.s > 0)
+    def _():
+        halo[0].wait_recv()
+        halo[1].wait_recv()
+
+    turn(0, ahead)
+    tiles(0, ahead)
+    saves = [
+        pltpu.make_async_copy(ext.at[pl.ds(0, WINDOW)], halo_out.at[i], keep.at[6 + i])
+        for i, ext in enumerate((k_ext, v_ext))
+    ]
+    for copy in saves:
+        copy.start()
+    out_gather.step(1)
+    gate_gather.step(0)
+    gather.got_core()
+    gather.got_first()
+    gather.got_second()
+    gather.got_core_second()
+    gather.got_core_first()
+    out_gather.step(2)
+    gate_gather.step(1)
+    gather.got_across()
+    gather.got_core_across()
+    gate_gather.step(2)
+    gather.finish()
+    out_gather.finish()
+    gate_gather.finish()
+
+    @pl.when(p.s < line - 1)
+    def _():
+        halo[0].wait_send()
+        halo[1].wait_send()
+
+    for copy in own + saves:
+        copy.wait()
+
+
+def attend(line, qkv, floor, cot, w_out, gate_a):
+    count = qkv.shape[0]
+    part = qkv.shape[1] // 3
+    heads = part // HEAD_DIM
+    rows, width = cot.shape
+    return pl.pallas_call(
+        functools.partial(attend_kernel, line),
+        out_shape=(
+            jax.ShapeDtypeStruct((count, part), BF16),
+            jax.ShapeDtypeStruct((heads, count), F32),
+            jax.ShapeDtypeStruct((2, WINDOW, part), BF16),
+            jax.ShapeDtypeStruct((rows * 8, width), BF16),
+            jax.ShapeDtypeStruct((line, *w_out.shape), BF16),
+            jax.ShapeDtypeStruct((line, *gate_a.shape), BF16),
+        ),
+        in_specs=[any_spec(), vmem_spec(), any_spec(), any_spec(), any_spec()],
+        out_specs=(vmem_spec(), vmem_spec(), any_spec(), any_spec(), any_spec(), any_spec()),
+        scratch_shapes=[
+            pltpu.VMEM((count, part), BF16),
+            pltpu.VMEM((WINDOW + count, part), BF16),
+            pltpu.VMEM((WINDOW + count, part), BF16),
+            pltpu.VMEM((part, WINDOW + count), BF16),
+            pltpu.SemaphoreType.DMA((7,)),
+            pltpu.SemaphoreType.DMA((7,)),
+            *line_sems(line, 2),
+            pltpu.SemaphoreType.DMA((2,)),
+            pltpu.SemaphoreType.DMA((2,)),
+            pltpu.SemaphoreType.DMA((8,)),
+        ],
+        compiler_params=pltpu.CompilerParams(
+            collective_id=2, has_side_effects=True, vmem_limit_bytes=48 * MIB
+        ),
+        cost_estimate=pl.CostEstimate(
+            flops=5 * 2**31, bytes_accessed=40 * MIB, transcendentals=0
+        ),
+    )(qkv, floor, cot, w_out, gate_a)
+
+
+class HeadReduce:
+    def __init__(self, place, out, into, send, recv):
+        p = place
+        self.p, self.out, self.into = p, out, into
+        goes = (p.core, p.core, p.core, p.core, p.first, p.first, p.second)
+        self.copies = [
+            remote(out.at[i], into.at[i], send.at[i], recv.at[i], p.at(to))
+            for i, to in enumerate(goes)
+        ]
+        self.for_core = (p.second + p.turn, p.across + p.turn, p.first + p.turn, p.core)
+        self.mine = (p.first, p.across, p.second, p.h)
+
+    def send(self, i):
+        self.copies[i].start()
+
+    def got(self, i):
+        self.copies[i].wait_recv()
+
+    def finish(self):
+        for copy in self.copies:
+            copy.wait_send()
+
+
+def reduce_scratch(rows, width):
+    return [
+        pltpu.VMEM((7, rows, width), BF16),
+        pltpu.VMEM((7, rows, width), BF16),
+        pltpu.SemaphoreType.DMA((7,)),
+        pltpu.SemaphoreType.DMA((7,)),
+    ]
+
+
+def branch_kernel(
+    line,
+    attended,
+    w_out,
+    tokens,
+    gate_b,
+    up,
+    middle,
+    gate_full,
+    up_full,
+    out,
+    into,
+    r_send,
+    r_recv,
+    *sems,
+):
+    p = Place(line)
+    gate_sems, up_sems, keep = sems[0:4], sems[4:8], sems[8]
+    rows, width = tokens.shape
+    slab = w_out.shape[2]
+    p.greet()
+    gate_gather = LineGather(p, lambda d: gate_full.at[d], *gate_sems, own=gate_b)
+    up_gather = LineGather(p, lambda d: up_full.at[d], *up_sems, own=up)
+    gate_gather.start(0)
+    own = [
+        pltpu.make_async_copy(gate_b, gate_full.at[p.s], keep.at[0]),
+        pltpu.make_async_copy(up, up_full.at[p.s], keep.at[1]),
+    ]
+    for copy in own:
+        copy.start()
+    reduce = HeadReduce(p, out, into, r_send, r_recv)
+
+    def emit(j, target, *more):
+        start = pl.multiple_of(j * rows, rows)
+
+        @pl.loop(0, line)
+        def _(n):
+            cols = pl.ds(pl.multiple_of(n * slab, slab), slab)
+            value = product(attended[pl.ds(start, rows), :], w_out[n])
+            for other in more:
+                value = value + other[:, cols].astype(F32)
+            target[:, cols] = value.astype(target.dtype)
+
+    for i in range(4):
+        emit(reduce.for_core[i], out.at[i])
+        reduce.send(i)
+    for i in range(2):
+        reduce.got(i)
+        emit(reduce.mine[i], out.at[4 + i], into.at[i])
+        reduce.send(4 + i)
+    reduce.got(3)
+    emit(p.h, middle, into.at[3], tokens)
+    reduce.got(2)
+    gate_gather.step(0)
+    up_gather.start(0)
+    gate_gather.step(1)
+    reduce.got(5)
+    emit(p.second, out.at[6], into.at[2], into.at[5])
+    reduce.send(6)
+    gate_gather.step(2)
+    up_gather.step(0)
+    reduce.got(4)
+    up_gather.step(1)
+    reduce.got(6)
+
+    @pl.loop(0, line)
+    def _(n):
+        cols = pl.ds(pl.multiple_of(n * slab, slab), slab)
+        middle[:, cols] += into[4, :, cols].astype(F32) + into[6, :, cols].astype(F32)
+
+    up_gather.step(2)
+    reduce.finish()
+    gate_gather.finish()
+    up_gather.finish()
+    for copy in own:
+        copy.wait()
+
+
+def branch(line, attended, w_out, tokens, gate_b, up):
+    rows, width = tokens.shape
+    return pl.pallas_call(
+        functools.partial(branch_kernel, line),
+        out_shape=(
+            jax.ShapeDtypeStruct((rows, width), F32),
+            jax.ShapeDtypeStruct((line, *gate_b.shape), BF16),
+            jax.ShapeDtypeStruct((line, *up.shape), BF16),
+        ),
+        in_specs=[vmem_spec(), vmem_spec(), vmem_spec(), any_spec(), any_spec()],
+        out_specs=(vmem_spec(), any_spec(), any_spec()),
+        scratch_shapes=[
+            *reduce_scratch(rows, width),
+            *line_sems(line, 2),
+            pltpu.SemaphoreType.DMA((2,)),
+        ],
+        compiler_params=pltpu.CompilerParams(
+            collective_id=3, has_side_effects=True, vmem_limit_bytes=48 * MIB
+        ),
+        cost_estimate=pl.CostEstimate(
+            flops=3 * 2**30, bytes_accessed=40 * MIB, transcendentals=0
+        ),
+    )(attended, w_out, tokens, gate_b, up)
+
+
+def strips(width, most=256):
+    return [(start, min(start + most, width)) for start in range(0, width, most)]
+
+
+def feed_kernel(
+    line,
+    middle,
+    gain,
+    cot,
+    gate_a,
+    gate_b,
+    up,
+    down,
+    normed_out,
+    hidden_out,
+    grad_gate_out,
+    grad_up_out,
+    grad_out,
+    down_out,
+    normed,
+    w_gate,
+    w_up,
+    w_down,
+    gates,
+    ups,
+    cot_block,
+    hidden,
+    grad_gate,
+    grad_up,
+    out,
+    into,
+    r_send,
+    r_recv,
+    g_send,
+    g_recv,
+    *sems,
+):
+    p = Place(line)
+    down_sems, loads, saves, stage = sems[0:4], sems[4], sems[5], sems[6]
+    rows, width = grad_out.shape
+    units = w_down.shape[1]
+    slab = w_down.shape[2]
+    cut = gate_a.shape[1]
+    block = lambda j: normed.at[pl.ds(pl.multiple_of(j * rows, rows), rows)]
+    rows_of = lambda ref, j: ref.at[pl.ds(pl.multiple_of(j * rows, rows), rows)]
+    gather = HeadGather(p, block, g_send, g_recv)
+    down_gather = LineGather(p, lambda d: w_down.at[d], *down_sems, own=down)
+    p.greet()
+    down_gather.start(0)
+    started = [
+        pltpu.make_async_copy(middle, grad_out, loads.at[0]),
+        pltpu.make_async_copy(gate_a, w_gate.at[:, pl.ds(0, cut)], loads.at[1]),
+        pltpu.make_async_copy(gate_b, w_gate.at[:, pl.ds(cut, units - cut)], loads.at[2]),
+        pltpu.make_async_copy(up, w_up, loads.at[3]),
+        pltpu.make_async_copy(down, w_down.at[p.s], loads.at[4]),
+    ]
+    for copy in started:
+        copy.start()
+    started[0].wait()
+    mine = block(p.h)
+    step = 32
+
+    @pl.loop(0, rows // step)
+    def _(i):
+        at = pl.ds(pl.multiple_of(i * step, step), step)
+        mine[at] = norm_rows(grad_out[at], gain[...]).astype(BF16)
+
+    gather.start()
+    saved = []
+
+    def save(j):
+        copy = pltpu.make_async_copy(block(j), rows_of(normed_out, j), saves.at[len(saved)])
+        copy.start()
+        saved.append(copy)
+
+    def open_up(j, slot):
+        rows_in = normed.at[pl.ds(pl.multiple_of(j * rows, rows), rows)]
+        for weight, kept in ((w_gate, gates), (w_up, ups)):
+            for first, last in strips(units):
+                value = product_nt(rows_in[:, 0:slab], weight[0, first:last, :])
+                for d in range(1, line):
+                    value = value + product_nt(
+                        rows_in[:, d * slab : (d + 1) * slab], weight[d, first:last, :]
+                    )
+                kept[slot, :, first:last] = value
+
+    order = (
+        p.second + p.turn,
+        p.first,
+        p.across + p.turn,
+        p.across,
+        p.first + p.turn,
+        p.second,
+        p.core,
+        p.h,
+    )
+    fetches = [
+        pltpu.make_async_copy(rows_of(cot, j), cot_block, stage.at[6]) for j in order
+    ]
+    stores = [
+        [
+            pltpu.make_async_copy(held.at[n % 2], rows_of(home, j), stage.at[3 * (n % 2) + i])
+            for i, (held, home) in enumerate(
+                ((hidden, hidden_out), (grad_gate, grad_gate_out), (grad_up, grad_up_out))
+            )
+        ]
+        for n, j in enumerate(order)
+    ]
+
+    def close(n, slot):
+        fetches[n].wait()
+        if n > 1:
+            for copy in stores[n - 2]:
+                copy.wait()
+        turn = n % 2
+        for first, last in strips(units):
+            grad = product_nt(cot_block[:, 0:slab], w_down[0, first:last, :])
+            for d in range(1, line):
+                grad = grad + product_nt(
+                    cot_block[:, d * slab : (d + 1) * slab], w_down[d, first:last, :]
+                )
+            gate = gates[slot, :, first:last]
+            lift = ups[slot, :, first:last]
+            sigmoid = jax.nn.sigmoid(gate)
+            active = gate * sigmoid
+            hidden[turn, :, first:last] = (active * lift).astype(BF16)
+            grad_up[turn, :, first:last] = (grad * active).astype(BF16)
+            grad_gate[turn, :, first:last] = (
+                grad * lift * (sigmoid * (1.0 + gate * (1.0 - sigmoid)))
+            ).astype(BF16)
+        if n + 1 < len(order):
+            fetches[n + 1].start()
+        for copy in stores[n]:
+            copy.start()
+
+    def back(n, target, *more):
+        turn = n % 2
+
+        @pl.loop(0, line)
+        def _(d):
+            cols = pl.ds(pl.multiple_of(d * slab, slab), slab)
+            value = product(grad_gate[turn], w_gate[d]) + product(grad_up[turn], w_up[d])
+            for other in more:
+                value = value + other[:, cols].astype(F32)
+            target[:, cols] = value.astype(target.dtype)
+
+    goes = (p.core, p.core, p.core, p.core, p.first, p.first, p.second)
+    slots = (0, 1, 0, 1, 2, 3, 4)
+    copies = [
+        remote(out.at[slots[i]], into.at[i], r_send.at[i], r_recv.at[i], p.at(to))
+        for i, to in enumerate(goes)
+    ]
+    fetches[0].start()
+    for copy in started[1:4]:
+        copy.wait()
+    save(p.h)
+    open_up(p.h, 0)
+    gather.got_core()
+    save(p.core)
+    open_up(p.core, 1)
+    down_gather.step(0)
+    gather.got_first()
+    gather.got_second()
+    save(p.first)
+    save(p.second)
+    down_gather.step(1)
+    open_up(p.first, 2)
+    gather.got_core_second()
+    gather.got_core_first()
+    save(p.second + p.turn)
+    save(p.first + p.turn)
+    open_up(p.second + p.turn, 3)
+    down_gather.step(2)
+    started[4].wait()
+    down_save = pltpu.make_async_copy(w_down, down_out, loads.at[5])
+    down_save.start()
+    close(0, 3)
+    back(0, out.at[0])
+    copies[0].start()
+    gather.got_across()
+    save(p.across)
+    close(1, 2)
+    copies[0].wait_recv()
+    back(1, out.at[2], into.at[0])
+    copies[4].start()
+    gather.got_core_across()
+    save(p.across + p.turn)
+    open_up(p.across + p.turn, 3)
+    close(2, 3)
+    back(2, out.at[1])
+    copies[1].start()
+    open_up(p.across, 3)
+    close(3, 3)
+    copies[1].wait_recv()
+    back(3, out.at[3], into.at[1])
+    copies[5].start()
+    open_up(p.first + p.turn, 3)
+    close(4, 3)
+    copies[0].wait_send()
+    back(4, out.at[0])
+    copies[2].start()
+    open_up(p.second, 3)
+    close(5, 3)
+    copies[2].wait_recv()
+    copies[5].wait_recv()
+    back(5, out.at[4], into.at[2], into.at[5])
+    copies[6].start()
+    close(6, 1)
+    copies[1].wait_send()
+    back(6, out.at[1])
+    copies[3].start()
+    close(7, 0)
+    copies[3].wait_recv()
+    back(7, grad_out, into.at[3])
+    copies[4].wait_recv()
+    copies[6].wait_recv()
+
+    @pl.loop(0, line)
+    def _(d):
+        cols = pl.ds(pl.multiple_of(d * slab, slab), slab)
+        grad_out[:, cols] += into[4, :, cols].astype(F32) + into[6, :, cols].astype(F32)
+
+    for i in range(2, 7):
+        copies[i].wait_send()
+    gather.finish()
+    down_gather.finish()
+    for copy in saved:
+        copy.wait()
+    for copy in stores[6] + stores[7]:
+        copy.wait()
+    down_save.wait()
+
+
+def feed(line, middle, gain, cot, gate_a, gate_b, up, down):
+    rows, width = middle.shape
+    units, slab = down.shape
+    full = rows * 8
+    return pl.pallas_call(
+        functools.partial(feed_kernel, line),
+        out_shape=(
+            jax.ShapeDtypeStruct((full, width), BF16),
+            jax.ShapeDtypeStruct((full, units), BF16),
+            jax.ShapeDtypeStruct((full, units), BF16),
+            jax.ShapeDtypeStruct((full, units), BF16),
+            jax.ShapeDtypeStruct((rows, width), F32),
+            jax.ShapeDtypeStruct((line, units, slab), BF16),
+        ),
+        in_specs=[any_spec(), vmem_spec()] + [any_spec()] * 5,
+        out_specs=(any_spec(), any_spec(), any_spec(), any_spec(), vmem_spec(), any_spec()),
+        scratch_shapes=[
+            pltpu.VMEM((full, width), BF16),
+            pltpu.VMEM((line, units, slab), BF16),
+            pltpu.VMEM((line, units, slab), BF16),
+            pltpu.VMEM((line, units, slab), BF16),
+            pltpu.VMEM((4, rows, units), F32),
+            pltpu.VMEM((4, rows, units), F32),
+            pltpu.VMEM((rows, width), BF16),
+            pltpu.VMEM((2, rows, units), BF16),
+            pltpu.VMEM((2, rows, units), BF16),
+            pltpu.VMEM((2, rows, units), BF16),
+            pltpu.VMEM((5, rows, width), BF16),
+            pltpu.VMEM((7, rows, width), BF16),
+            pltpu.SemaphoreType.DMA((7,)),
+            pltpu.SemaphoreType.DMA((7,)),
+            pltpu.SemaphoreType.DMA((7,)),
+            pltpu.SemaphoreType.DMA((7,)),
+            *line_sems(line),
+            pltpu.SemaphoreType.DMA((6,)),
+            pltpu.SemaphoreType.DMA((8,)),
+            pltpu.SemaphoreType.DMA((7,)),
+        ],
+        compiler_params=pltpu.CompilerParams(
+            collective_id=4, has_side_effects=True, vmem_limit_bytes=60 * MIB
+        ),
+        cost_estimate=pl.CostEstimate(
+            flops=50 * 2**30, bytes_accessed=80 * MIB, transcendentals=0
+        ),
+    )(middle, gain.reshape(1, width), cot, gate_a, gate_b, up, down)
 
 
 def fused(
@@ -637,17 +1342,29 @@
     scale = HEAD_DIM ** (-0.5)
     line = lax.axis_size("seq")
     part = query_weight.shape[1]
-    normed_full, qkv, w_qkv = project(
-        line, tokens, attn_gain, query_weight, key_weight, value_weight
-    )
+    normed_full, qkv, w_qkv, floor, gate_t, up_t = project(
+        line,
+        tokens,
+        attn_gain,
+        query_weight,
+        key_weight,
+        value_weight,
+        segment,
+        gate_weight,
+        up_weight,
+    )
+    cut = gate_t.shape[0] // 32 * 16 + 16
+    attended, logs, halo_kv, grad_out, w_out_parts, gate_a = attend(
+        line, qkv, floor, cotangent, out_weight, gate_t[:cut]
+    )
+    middle, gate_b, up_all = branch(line, attended, w_out_parts, tokens, gate_t[cut:], up_t)
+    normed_two_full, hidden, grad_gate, grad_up, grad_normed_two, down_parts = feed(
+        line, middle, ffn_gain, grad_out, gate_a, gate_b, up_all, down_weight
+    )
+    w_down = down_parts.transpose(1, 0, 2).reshape(down_weight.shape[0], -1)
+    w_out = w_out_parts.transpose(1, 0, 2).reshape(part, -1)
     w_query, w_key, w_value = (w_qkv[:, i * part : (i + 1) * part] for i in range(3))
     queries, keys, values = (qkv[:, i * part : (i + 1) * part] for i in range(3))
-    w_out, w_gate, w_up, w_down = (
-        lax.all_gather(out_weight, "seq", axis=1, tiled=True),
-        lax.all_gather(gate_weight, "seq", axis=0, tiled=True),
-        lax.all_gather(up_weight, "seq", axis=0, tiled=True),
-        lax.all_gather(down_weight, "seq", axis=1, tiled=True),
-    )
     inputs = tokens.astype(jnp.float32)
     unit_one, inverse_one = normalize(inputs)
     halo_keys, halo_values, halo_segs = ([], [], [])
@@ -667,55 +1384,18 @@
     query_heads = queries.reshape(group, heads_here, HEAD_DIM)
     key_heads = keys_ext.reshape(WINDOW + group, heads_here, HEAD_DIM)
     value_heads = values_ext.reshape(WINDOW + group, heads_here, HEAD_DIM)
-    outputs, logsums = ([], [])
-    for start in range(0, group, block):
-        scores = block_scores(query_heads, key_heads, segment, segs_ext, valid, start, block)
-        highest = jnp.max(scores, axis=-1, keepdims=True)
-        weights = jnp.exp(scores - highest)
-        total = jnp.sum(weights, axis=-1, keepdims=True)
-        probs = (weights / total).astype(jnp.bfloat16)
-        outputs.append(
-            jnp.einsum(
-                "hqk,khd->qhd",
-                probs,
-                value_heads[start : start + block + WINDOW],
-                preferred_element_type=jnp.float32,
-            )
-        )
-        logsums.append(highest + jnp.log(total))
-    attended = (
-        jnp.concatenate(outputs, axis=0).reshape(group, heads_here * HEAD_DIM).astype(jnp.bfloat16)
-    )
-    partial_out = product(attended, w_out)
-    own_part = lax.dynamic_slice_in_dim(partial_out, offset, own_rows, 0)
-    placed = lax.dynamic_update_slice_in_dim(partial_out, own_part + inputs, offset, 0)
-    middle_full = lax.psum(placed, "head")
-    middle = lax.dynamic_slice_in_dim(middle_full, offset, own_rows, 0)
-    unit_full, inverse_full = normalize(middle_full)
-    normed_two_full = (unit_full * ffn_gain).astype(jnp.bfloat16)
+    logsums = [
+        logs[:, start : start + block, None] * 0.6931471805599453
+        for start in range(0, group, block)
+    ]
     unit_two, inverse_two = normalize(middle)
-    gate = product(normed_two_full, w_gate)
-    up = product(normed_two_full, w_up)
-    sigmoid = jax.nn.sigmoid(gate)
-    activated = gate * sigmoid
-    hidden = (activated * up).astype(jnp.bfloat16)
     ffn_out = lax.psum_scatter(
         product(hidden, w_down).astype(jnp.bfloat16), "head", scatter_dimension=0, tiled=True
     ).astype(jnp.float32)
     result = middle + ffn_out
-    grad_out = lax.all_gather(cotangent, "head", axis=0, tiled=True)
-    grad_hidden = product_nt(grad_out, w_down)
-    grad_gate = (grad_hidden * up * sigmoid * (1.0 + gate * (1.0 - sigmoid))).astype(jnp.bfloat16)
-    grad_up = (grad_hidden * activated).astype(jnp.bfloat16)
     down_grad = product_tn(hidden, grad_out)
     gate_grad = product_tn(normed_two_full, grad_gate)
     up_grad = product_tn(normed_two_full, grad_up)
-    grad_normed_two = lax.psum_scatter(
-        (product_nt(grad_gate, w_gate) + product_nt(grad_up, w_up)).astype(jnp.bfloat16),
-        "head",
-        scatter_dimension=0,
-        tiled=True,
-    ).astype(jnp.float32)
     ffn_gain_part = jnp.sum(grad_normed_two * unit_two, axis=0)
     grad_middle = cotangent.astype(jnp.float32) + norm_back(
         unit_two, inverse_two, ffn_gain, grad_normed_two

time: 1520 us -> 927 us (0.61)
  waiting for transfers between devices: 833 us -> 139 us
  Pallas kernels: 90.1 us -> 355 us
  matrix products: 339 us -> 215 us
  other arithmetic: 99.9 us -> 62.7 us
    psum x1 -> x0, waiting for transfers between devices: 305 us -> none  [fused(): middle_full = lax.psum(placed, 'head')]
    pallas_call x0 -> x3, Pallas kernels: none -> 280 us  [the longest x1 127 us: feed(): pl.pallas_call(functools.partial(feed_kernel, line), out_shape=(jax.Shape...]
    all_gather x5 -> x0, waiting for transfers between devices: 197 us -> none  [the longest x1 72.8 us: fused(): grad_out = lax.all_gather(cotangent, 'head', axis=0, tiled=True)]
    reduce_scatter x1 -> x0, waiting for transfers between devices: 90.3 us -> none  [fused(): lax.psum_scatter((product_nt(grad_gate, w_gate) + product_nt(grad_up, w_u...]
    dot_general x7 -> x4, matrix products: 114 us -> 58.2 us  [product_nt(): lax.dot_general(left, right, (((1,), (1,)), ((), ())), preferred_element_...]
    dot_general x4 -> x1, matrix products: 58.1 us -> 14.6 us  [product(): return jnp.dot(left, right, preferred_element_type=jnp.float32)]
    all_gather x1, waiting for transfers between devices: 28.4 us -> 0.01 us  [fused(): lax.all_gather(grad_middle.astype(jnp.bfloat16), 'head', axis=0, tiled=True)]
    reduce_scatter x1, waiting for transfers between devices: 26.3 us -> 0.01 us  [fused(): lax.psum_scatter(key_grad.astype(jnp.bfloat16), 'seq', scatter_dimension=...]
  transfers between devices with their start and end apart: 22 -> 15, of which waited for: 12 -> 2; matrix products, arithmetic and copies ran while one was open for 26% -> 34% of each run, Pallas kernels for 6% -> 0%
where the time goes in v2:
time: 927 us; the launch traced here: 918 us
  Pallas kernels  355 us (38%)
  matrix products  215 us (23%)
  waiting for transfers between devices  139 us (15%)
  local copies, waits for them, and re-layouts  75.4 us (8%)
  other arithmetic  62.7 us (7%)
  blocking collectives  39.8 us (4%)
  between operations  17.4 us (2%)
  starting transfers between devices  13.1 us (1%)
    pallas_call x1, Pallas kernels, feed(): pl.pallas_call(functools.partial(feed_kernel, line), out_shape=(jax.Shape...  127 us
    reduce_scatter x1, waiting for transfers between devices, fused(): lax.psum_scatter((product_nt(grad_queries, w_query) + product_nt(grad_key...  85.1 us
    pallas_call x1, Pallas kernels, branch(): pl.pallas_call(functools.partial(branch_kernel, line), out_shape=(jax.Sha...  81.7 us
    dot_general x7, matrix products, product_tn(): lax.dot_general(left, right, (((0,), (0,)), ((), ())), preferred_element_...  79.6 us
    pallas_call x1, Pallas kernels, project(): pl.pallas_call(functools.partial(project_kernel, line), out_shape=(jax.Sh...  75 us
    pallas_call x1, Pallas kernels, attend(): pl.pallas_call(functools.partial(attend_kernel, line), out_shape=(jax.Sha...  72 us
    dot_general x4, matrix products, product_nt(): lax.dot_general(left, right, (((1,), (1,)), ((), ())), preferred_element_...  58.2 us
    reduce_scatter x1, waiting for transfers between devices, fused(): lax.psum_scatter(product(hidden, w_down).astype(jnp.bfloat16), 'head', sc...  53.2 us
  transfers between devices with their start and end apart: 15, of which 2 were waited for; matrix products, arithmetic and copies ran while one was open for 34% of the time, Pallas kernels for 0%

profile of v2, /device:TPU:0, one launch (start us, length us, event | category | flops | bytes accessed | tf_op | source)
XLA Modules:
  0.0 917.6 jit_solution(7407797785075907001)
XLA Ops:
  16.5 75.0 %shard_map.203 = (bf16[3072,2048]{1,0:T(8,128)(2,1)}, bf16[3072,768]{1,0:T(8,128)(2,1)}, bf16[2048,768]{1,0:T(8,128)(2,1)}, s32[1,3072]{1,0:T(1,128)S(1)}, bf16[...) custom-call(bf16[384,2048]{1,0:T(8,128)(2,1)S(1)} %copy-done, f32[1,2048]{1,0:T(1,128)S(1)} %bitcast.220, ...), custom_call_target="tpu_custom_call" | custom-call | flops 9663676416 | bytes 41943040 | tf_op jit(solution)/shard_map/pallas_call | solution.py:661
  91.5 72.0 %shard_map.204 = (bf16[3072,256]{1,0:T(8,128)(2,1)S(1)}, f32[2,3072]{1,0:T(2,128)S(1)}, bf16[2,1024,256]{2,1,0:T(8,128)(2,1)}, bf16[3072,2048]{1,0:T(8,128)(2,1)...) custom-call(bf16[3072,768]{1,0:T(8,128)(2,1)} %get-tuple-element.199.qkv, ...), custom_call_target="tpu_custom_call" | custom-call | flops 10737418240 | bytes 41943040 | tf_op jit(solution)/shard_map/pallas_call | solution.py:874
  163.6 81.7 %shard_map.205 = (f32[384,2048]{1,0:T(8,128)}, bf16[4,336,512]{2,1,0:T(8,128)(2,1)S(1)}, bf16[4,688,512]{2,1,0:T(8,128)(2,1)}) custom-call(bf16[3072,256]{1,0:T(8,128)(2,1)S(1)} %get-tuple-element.202.attended, bf16[4,256,512]{2,1,0:T(8,128)(2,1)S(1)} %get-tuple-element.203.w_out, bf16[384,2048]{1,0:T(8,128)(2,1)} %tokens.3, ...), custom_call_target="tpu_custom_call" | custom-call | flops 3221225472 | bytes 41943040 | tf_op jit(solution)/shard_map/pallas_call | solution.py:1019
  248.6 126.7 %shard_map.206 = (bf16[3072,2048]{1,0:T(8,128)(2,1)}, bf16[3072,688]{1,0:T(8,128)(2,1)}, bf16[3072,688]{1,0:T(8,128)(2,1)}, bf16[3072,688]{1,0:T(8,128)(2,1)}, f...) custom-call(f32[384,2048]{1,0:T(8,128)} %get-tuple-element.205.middle, f32[1,2048]{1,0:T(1,128)} %bitcast.262, ...), custom_call_target="tpu_custom_call" | custom-call | flops 53687091200 | bytes 83886080 | tf_op jit(solution)/shard_map/pallas_call | solution.py:1279
  375.3 4.4 multiply_reduce_fusion.6
  382.5 14.7 %convolution_convert_fusion.4 = bf16[688,2048]{1,0:T(8,128)(2,1)} fusion(bf16[3072,688]{1,0:T(8,128)(2,1)} %get-tuple-element.210, bf16[3072,2048]{1,0:T(8,128)(2,1)} %get-tuple-element.206.cot), kind=kOutput, calls=%fused_computation.30 | convolution fusion | flops 8658452480 | bytes 19628032 | tf_op jit(solution)/shard_map/dot_general | solution.py:29
  397.3 14.5 %convolution_convert_fusion.3 = bf16[2048,688]{0,1:T(8,128)(2,1)} fusion(bf16[3072,2048]{1,0:T(8,128)(2,1)} %get-tuple-element.216, bf16[3072,688]{1,0:T(8,128)(2,1)} %get-tuple-element.217), kind=kOutput, calls=%fused_computation.29 | convolution fusion | flops 8658452480 | bytes 19628032 | tf_op jit(solution)/shard_map/dot_general | solution.py:29
  420.8 3.6 collective-permute-start
  424.4 15.1 %convolution_convert_fusion.2 = bf16[2048,688]{0,1:T(8,128)(2,1)} fusion(bf16[3072,2048]{1,0:T(8,128)(2,1)} %get-tuple-element.216, bf16[3072,688]{1,0:T(8,128)(2,1)} %get-tuple-element.218), kind=kOutput, calls=%fused_computation.28 | convolution fusion | flops 8658452480 | bytes 19628032 | tf_op jit(solution)/shard_map/dot_general | solution.py:29
  443.0 4.0 fusion.132
  447.0 5.6 slice_bitcast_fusion
  469.6 6.3 and_and_fusion
  483.6 8.3 convolution_convert_fusion.1
  534.0 3.4 fusion.26
  537.4 3.8 fusion.29
  559.1 3.5 multiply_convert_fusion.1
  562.6 4.3 fusion.35
  566.9 3.4 multiply_convert_fusion
  570.4 3.4 fusion.37
  586.6 7.8 convolution_convert_fusion.8
  601.6 9.9 %convolution_convert_fusion.7 = bf16[2048,256]{1,0:T(8,128)(2,1)} fusion(bf16[3072,2048]{1,0:T(8,128)(2,1)} %get-tuple-element.215, bf16[3072,256]{0,1:T(8,128)(2,1)} %bitcast.18), kind=kOutput, calls=%fused_computation.101 | convolution fusion | flops 3221749760 | bytes 15204352 | tf_op jit(solution)/shard_map/dot_general | solution.py:29
  611.8 13.7 %fusion.104 = f32[3072,2048]{1,0:T(8,128)} fusion(bf16[3072,256]{0,1:T(8,128)(2,1)} %bitcast.18, bf16[2048,768]{1,0:T(8,128)(2,1)} %get-tuple-element.214), kind=kOutput, calls=%fused_computation.134 | convolution fusion | flops 3221225472 | bytes 27787264 | tf_op jit(solution)/shard_map/dot_general | solution.py:35
  627.7 3.2 slice.749
  632.1 7.9 convolution_convert_fusion.5
  642.4 9.8 %convolution_convert_fusion.6 = bf16[2048,256]{1,0:T(8,128)(2,1)} fusion(bf16[3072,2048]{1,0:T(8,128)(2,1)} %get-tuple-element.215, bf16[3072,256]{0,1:T(8,128)(2,1)} %constant_dynamic-update-slice_fusion.4), kind=kOutput, calls=%fused_computation.100 | convolution fusion | flops 3221749760 | bytes 15204352 | tf_op jit(solution)/shard_map/dot_general | solution.py:29
  652.1 13.7 %fusion.102 = f32[3072,2048]{1,0:T(8,128)} fusion(bf16[2048,768]{1,0:T(8,128)(2,1)} %get-tuple-element.214, bf16[3072,256]{0,1:T(8,128)(2,1)} %constant_dynamic-update-slice_fusion.4), kind=kOutput, calls=%fused_computation.132 | convolution fusion | flops 3221225472 | bytes 27787264 | tf_op jit(solution)/shard_map/dot_general | solution.py:35
  665.9 22.5 %add_convert_fusion = bf16[3072,2048]{1,0:T(8,128)(2,1)} fusion(f32[3072,2048]{1,0:T(8,128)} %fusion.104, f32[3072,2048]{1,0:T(8,128)} %fusion.102, bf16[2048,768]{1,0:T(8,128)(2,1)} %get-tuple-element.214, bf16[3072,256]{0,1:T(8,128)(2,1)S(1)} %constant_dynamic-update-slice_fusion.2), kind=kOutput, calls=%fused_computation | convolution fusion | flops 3240099840 | bytes 65536000 | tf_op jit(solution)/shard_map/dot_general | solution.py:35
  690.6 14.6 %convolution_convert_fusion = bf16[3072,2048]{1,0:T(8,128)(2,1)} fusion(bf16[3072,688]{1,0:T(8,128)(2,1)} %get-tuple-element.210, bf16[688,2048]{1,0:T(8,128)(2,1)S(1)} %bitcast.236), kind=kOutput, calls=%fused_computation.1 | convolution fusion | flops 8663334912 | bytes 19628032 | tf_op jit(solution)/shard_map/dot_general | solution.py:25
  721.6 85.1 %reduce-scatter.12.cloned.1.call-done = bf16[384,2048]{1,0:T(8,128)(2,1)} async-done(((bf16[3072,2048]{1,0:T(8,128)(2,1)}), bf16[384,2048]{1,0:T(8,128)(2,1)}) %reduce-scatter.12.cloned.1.call-update) | async-done | bytes 1572880 | tf_op jit(solution)/shard_map/reduce_scatter | solution.py:1461
  809.3 39.8 %all-reduce.4 = (f32[2048]{0:T(1024)S(1)}, f32[2048]{0:T(1024)S(1)}) all-reduce(f32[2048]{0:T(1024)S(1)} %get-tuple-element.221, f32[2048]{0:T(1024)S(1)} %copy-done.78), channel_id=4, replica_groups=mesh['seq'=4,'head'=8] {'seq','head'}, use_global_device_ids=true, to_apply=%region_13.14.clone | all-reduce | flops 4096 | bytes 32768
  850.2 53.2 %reduce-scatter.10.cloned.1.call-done = bf16[384,2048]{1,0:T(8,128)(2,1)} async-done(((bf16[3072,2048]{1,0:T(8,128)(2,1)}), bf16[384,2048]{1,0:T(8,128)(2,1)}) %reduce-scatter.10.cloned.1.call-update) | async-done | bytes 1572880 | tf_op jit(solution)/shard_map/reduce_scatter | solution.py:1392
  903.4 6.1 fusion.4
  (334 shorter events, 159.4 us)
Async XLA Ops:
  8.0 475.6 %all-gather.2.cloned.1.call-start = ((), (), s32[]{:S(2)}) async-start(), calls=%async_computation.10 | async-start | bytes 14155776 | tf_op jit(solution)/shard_map/all_gather | solution.py:1403
  16.5 75.0 %copy-start.11 = (bf16[256,512]{1,0:T(8,128)(2,1)S(1)}, bf16[256,512]{1,0:T(8,128)(2,1)}, u32[]{:S(2)}) copy-start(bf16[256,512]{1,0:T(8,128)(2,1)} %w_out.1) | copy-start | bytes 786436
  163.6 81.7 %copy-start.2 = (bf16[3072,256]{1,0:T(8,128)(2,1)}, bf16[3072,256]{1,0:T(8,128)(2,1)S(1)}, u32[]{:S(2)}) copy-start(bf16[3072,256]{1,0:T(8,128)(2,1)S(1)} %get-tuple-element.202.attended) | copy-start | bytes 4718596
  163.6 81.7 %copy-start.13 = (bf16[4,352,512]{2,1,0:T(8,128)(2,1)}, bf16[4,352,512]{2,1,0:T(8,128)(2,1)S(1)}, u32[]{:S(2)}) copy-start(bf16[4,352,512]{2,1,0:T(8,128)(2,1)S(1)} %get-tuple-element.207.gate_a) | copy-start | bytes 4325380
  248.6 131.1 %copy-start.76 = (f32[384]{0:T(512)}, f32[384]{0:T(512)S(1)}, u32[]{:S(2)}) copy-start(f32[384]{0:T(512)S(1)} %add_rsqrt_fusion.1) | copy-start | bytes 4612
  248.6 126.7 %copy-start.74 = (f32[2048]{0:T(1024)S(1)}, f32[2048]{0:T(1024)}, u32[]{:S(2)}) copy-start(f32[2048]{0:T(1024)} %param.47) | copy-start | bytes 24580
  248.6 131.7 %copy-start.44 = (bf16[384,2048]{1,0:T(8,128)(2,1)S(1)}, bf16[384,2048]{1,0:T(8,128)(2,1)}, u32[]{:S(2)}) copy-start(bf16[384,2048]{1,0:T(8,128)(2,1)} %cot.1) | copy-start | bytes 4718596
  382.5 324.6 %reduce-scatter.26.cloned.1.call-start = ((), (), s32[]{:S(2)}) async-start(), calls=%async_computation.18 | async-start | bytes 3522560 | tf_op jit(solution)/shard_map/reduce_scatter | solution.py:1492
  397.2 312.2 %reduce-scatter.22.cloned.1.call-start = ((), (), s32[]{:S(2)}) async-start(), calls=%async_computation.16 | async-start | bytes 3522560 | tf_op jit(solution)/shard_map/reduce_scatter | solution.py:1486
  397.3 14.6 %copy-start.5 = (s32[3072]{0:T(1024)S(1)}, s32[3072]{0:T(1024)}, u32[]{:S(2)}) copy-start(s32[3072]{0:T(1024)} %param.41) | copy-start | bytes 36868
  411.8 300.0 %reduce-scatter.24.cloned.1.call-start = ((), (), s32[]{:S(2)}) async-start(), calls=%async_computation.17 | async-start | bytes 3522560 | tf_op jit(solution)/shard_map/reduce_scatter | solution.py:1489
  412.5 56.2 %collective-permute-start.1 = (s32[1024]{0:T(1024)}, s32[1024]{0:T(1024)}, u32[]{:S(2)}, u32[]{:S(2)}) collective-permute-start(s32[1024]{0:T(1024)} %slice.638), channel_id=1, source_target_pairs={{0,8},{8,16},{16,24},{1,9},{9,17},{17,25},{2,10},{10,18},{18,26},{... | collective-permute-start | bytes 12296 | tf_op jit(solution)/shard_map/ppermute | solution.py:21
  418.1 62.6 %collective-permute-start.2 = (bf16[1024,256]{1,0:T(8,128)(2,1)}, bf16[1024,256]{1,0:T(8,128)(2,1)}, u32[]{:S(2)}, u32[]{:S(2)}) collective-permute-start(bf16[1024,256]{1,0:T(8,128)(2,1)} %get-tuple-element.239), channel_id=1, source_target_pairs={{0,8},{8,16},{16,24},{1,9},{9,17},{17,25},{2,10},{10,18},{18,26},{... | collective-permute-start | bytes 1572872 | tf_op jit(solution)/shard_map/ppermute | solution.py:21
  420.8 55.2 %collective-permute-start = (bf16[1024,256]{1,0:T(8,128)(2,1)}, bf16[1024,256]{1,0:T(8,128)(2,1)}, u32[]{:S(2)}, u32[]{:S(2)}) collective-permute-start(bf16[1024,256]{1,0:T(8,128)(2,1)} %get-tuple-element.240), channel_id=1, source_target_pairs={{0,8},{8,16},{16,24},{1,9},{9,17},{17,25},{2,10},{10,18},{18,26},{... | collective-permute-start | bytes 1572872 | tf_op jit(solution)/shard_map/ppermute | solution.py:21
  439.6 274.7 %reduce-scatter.20.cloned.1.call-start = ((), (), s32[]{:S(2)}) async-start(), calls=%async_computation.15 | async-start | bytes 1310720 | tf_op jit(solution)/shard_map/reduce_scatter | solution.py:1483
  461.2 85.3 %copy-start.33 = (bf16[1536,256]{0,1:T(8,128)(2,1)}, bf16[1536,256]{0,1:T(8,128)(2,1)S(1)}, u32[]{:S(2)}) copy-start(bf16[1536,256]{0,1:T(8,128)(2,1)S(1)} %copy.157) | copy-start | bytes 2359300
  461.2 8.3 copy-start.79
  461.2 8.3 copy-start.80
  480.7 13.8 %copy-start.42 = (bf16[1536,256]{0,1:T(8,128)(2,1)}, bf16[1536,256]{0,1:T(8,128)(2,1)S(1)}, u32[]{:S(2)}) copy-start(bf16[1536,256]{0,1:T(8,128)(2,1)S(1)} %copy.147) | copy-start | bytes 2359300
  578.2 62.1 %collective-permute-start.3 = (bf16[1024,256]{0,1:T(8,128)(2,1)}, bf16[1024,256]{0,1:T(8,128)(2,1)}, u32[]{:S(2)}, u32[]{:S(2)}) collective-permute-start(bf16[1024,256]{0,1:T(8,128)(2,1)} %bitcast.27), channel_id=1, source_target_pairs={{8,0},{16,8},{24,16},{9,1},{17,9},{25,17},{10,2},{18,10},{26,18},{... | collective-permute-start | bytes 1572872 | tf_op jit(solution)/shard_map/ppermute | solution.py:21
  579.5 51.4 %collective-permute-start.4 = (bf16[1024,256]{0,1:T(8,128)(2,1)}, bf16[1024,256]{0,1:T(8,128)(2,1)}, u32[]{:S(2)}, u32[]{:S(2)}) collective-permute-start(bf16[1024,256]{0,1:T(8,128)(2,1)} %bitcast.36), channel_id=1, source_target_pairs={{8,0},{16,8},{24,16},{9,1},{17,9},{25,17},{10,2},{18,10},{26,18},{... | collective-permute-start | bytes 1572872 | tf_op jit(solution)/shard_map/ppermute | solution.py:21
  594.4 121.8 %reduce-scatter.14.cloned.1.call-start = ((), (), s32[]{:S(2)}) async-start(), calls=%async_computation.12 | async-start | bytes 1310720 | tf_op jit(solution)/shard_map/reduce_scatter | solution.py:1474
  611.5 106.5 %reduce-scatter.18.cloned.1.call-start = ((), (), s32[]{:S(2)}) async-start(), calls=%async_computation.14 | async-start | bytes 1310720 | tf_op jit(solution)/shard_map/reduce_scatter | solution.py:1480
  640.0 79.7 %reduce-scatter.16.cloned.1.call-start = ((), (), s32[]{:S(2)}) async-start(), calls=%async_computation.13 | async-start | bytes 1310720 | tf_op jit(solution)/shard_map/reduce_scatter | solution.py:1477
  665.9 140.9 %reduce-scatter.12.cloned.1.call-start = ((), (), s32[]{:S(2)}) async-start(), calls=%async_computation.11 | async-start | bytes 14155776 | tf_op jit(solution)/shard_map/reduce_scatter | solution.py:1461
  688.5 214.9 %reduce-scatter.10.cloned.1.call-start = ((), (), s32[]{:S(2)}) async-start(), calls=%async_computation.9 | async-start | bytes 14155776 | tf_op jit(solution)/shard_map/reduce_scatter | solution.py:1392
  711.8 94.9 %copy-start.7 = (f32[2048]{0:T(1024)S(1)}, f32[2048]{0:T(1024)}, u32[]{:S(2)}) copy-start(f32[2048]{0:T(1024)} %param.42) | copy-start | bytes 24580
  714.2 95.0 %copy-start.78 = (f32[2048]{0:T(1024)S(1)}, f32[2048]{0:T(1024)}, u32[]{:S(2)}) copy-start(f32[2048]{0:T(1024)} %get-tuple-element.219) | copy-start | bytes 24580
  714.2 189.1 %copy-start.45 = (bf16[384,2048]{1,0:T(8,128)(2,1)S(1)}, bf16[384,2048]{1,0:T(8,128)(2,1)}, u32[]{:S(2)}) copy-start(bf16[384,2048]{1,0:T(8,128)(2,1)} %cot.1) | copy-start | bytes 4718596
  714.3 189.1 %copy-start.75 = (f32[2048]{0:T(1024)S(1)}, f32[2048]{0:T(1024)}, u32[]{:S(2)}) copy-start(f32[2048]{0:T(1024)} %param.47) | copy-start | bytes 24580
  714.3 189.1 %copy-start.77 = (f32[384]{0:T(512)S(1)}, f32[384]{0:T(512)}, u32[]{:S(2)}) copy-start(f32[384]{0:T(512)} %copy-done.76) | copy-start | bytes 4612
  714.3 189.1 %copy-start.83 = (f32[384]{0:T(512)S(1)}, f32[384]{0:T(512)}, u32[]{:S(2)}) copy-start(f32[384]{0:T(512)} %copy-done.82) | copy-start | bytes 4612
  (87 other events, 334.1 us)
Sparse Core Ops, SparseCore 0:
  382.6 70.4 all-gather.1
Sparse Core Ops, SparseCore 1:
  397.3 73.4 reduce-scatter.25
  473.1 57.1 reduce-scatter.21
  532.5 60.2 reduce-scatter.23
  595.2 32.0 reduce-scatter.19
  630.1 26.0 reduce-scatter.13
  658.6 25.7 reduce-scatter.17
  686.5 25.7 reduce-scatter.15
  716.0 90.7 reduce-scatter.11
  810.5 92.8 reduce-scatter.9

commit v3 on v2

--- a/solution.py
+++ b/solution.py
@@ -1319,6 +1319,908 @@
     )(middle, gain.reshape(1, width), cot, gate_a, gate_b, up, down)
 
 
+class LineReduce:
+    def __init__(self, place, part, up_in, down_in, up_send, up_recv, down_send, down_recv):
+        self.p, self.part = place, part
+        self.up_in, self.down_in = up_in, down_in
+        self.up = (up_send, up_recv)
+        self.down = (down_send, down_recv)
+
+    def _up(self, d, t):
+        p = self.p
+        return remote(
+            self.part(d), self.up_in.at[t], self.up[0].at[t], self.up[1].at[t], (p.s + 1, p.h)
+        )
+
+    def _down(self, d, t):
+        p = self.p
+        return remote(
+            self.part(d),
+            self.down_in.at[t],
+            self.down[0].at[t],
+            self.down[1].at[t],
+            (p.s - 1, p.h),
+        )
+
+    def _sends(self, t):
+        p, last = self.p, self.p.line - 1
+        return (
+            ((p.s <= t) & (p.s < last), self._up, last - t + p.s),
+            ((last - p.s <= t) & (p.s > 0), self._down, t - last + p.s),
+        )
+
+    def start(self, t):
+        p, last = self.p, self.p.line - 1
+        for number, (goes, copy, d) in enumerate(self._sends(t)):
+            came = (self.up_in, self.down_in)[number]
+
+            @pl.when(goes)
+            def _():
+                if t > 0:
+                    inner = p.s > 0 if number == 0 else p.s < last
+
+                    @pl.when(inner)
+                    def _():
+                        add_rows(self.part(d), came.at[t - 1])
+
+                copy(d, t).start()
+
+    def got(self, t):
+        p, last = self.p, self.p.line - 1
+
+        @pl.when((p.s >= 1) & (t >= p.s - 1))
+        def _():
+            self._up(0, t).wait_recv()
+
+        @pl.when((p.s < last) & (t >= last - p.s - 1))
+        def _():
+            self._down(0, t).wait_recv()
+
+    def step(self, t):
+        self.got(t)
+        if t + 1 < self.p.line - 1:
+            self.start(t + 1)
+
+    def end(self):
+        p, last = self.p, self.p.line - 1
+
+        @pl.when(p.s >= 1)
+        def _():
+            add_rows(self.part(p.s), self.up_in.at[last - 1])
+
+        @pl.when(p.s < last)
+        def _():
+            add_rows(self.part(p.s), self.down_in.at[last - 1])
+
+    def total(self, rows):
+        p, last = self.p, self.p.line - 1
+        value = self.part(p.s)[rows, :].astype(F32)
+        value = value + jnp.where(p.s >= 1, self.up_in[last - 1, rows, :].astype(F32), 0.0)
+        return value + jnp.where(p.s < last, self.down_in[last - 1, rows, :].astype(F32), 0.0)
+
+    def finish(self):
+        for t in range(self.p.line - 1):
+            for goes, copy, d in self._sends(t):
+
+                @pl.when(goes)
+                def _():
+                    copy(d, t).wait_send()
+
+
+def add_rows(target, other):
+    step = 16
+
+    @pl.loop(0, target.shape[0] // step)
+    def _(i):
+        at = pl.ds(pl.multiple_of(i * step, step), step)
+        target[at, :] = (target[at, :].astype(F32) + other[at, :].astype(F32)).astype(BF16)
+
+
+def clear_last(reduce):
+    p, last = reduce.p, reduce.p.line - 1
+
+    @pl.when(p.s == 0)
+    def _():
+        reduce.up_in[last - 1] = jnp.zeros(reduce.up_in.shape[1:], BF16)
+
+    @pl.when(p.s == last)
+    def _():
+        reduce.down_in[last - 1] = jnp.zeros(reduce.down_in.shape[1:], BF16)
+
+
+def weight_product(turned, source, piece, strip, sems):
+    depth = turned.shape[1]
+    wide = strip.shape[2]
+    slab = piece(0).shape[1]
+    count = source.shape[1] // wide
+    each = slab // wide
+
+    def fetch(n):
+        cols = pl.ds(pl.multiple_of(n * wide, wide), wide)
+        return pltpu.make_async_copy(
+            source.at[:, cols], strip.at[lax.rem(n, 2)], sems.at[lax.rem(n, 2)]
+        )
+
+    fetch(0).start()
+
+    @pl.loop(0, count)
+    def _(n):
+        @pl.when(n + 1 < count)
+        def _():
+            fetch(n + 1).start()
+
+        fetch(n).wait()
+        cols = pl.ds(pl.multiple_of(lax.rem(n, each) * wide, wide), wide)
+        piece(lax.div(n, each))[:, cols] = product(
+            turned[...], strip[lax.rem(n, 2)]
+        ).astype(BF16)
+
+
+def turn_rows(source, target):
+    step = 256
+
+    @pl.loop(0, source.shape[0] // step)
+    def _(i):
+        at = pl.ds(pl.multiple_of(i * step, step), step)
+        for first, last in strips(source.shape[1], 128):
+            target[first:last, at] = source[at, first:last].T
+
+
+def return_kernel(
+    line,
+    cut,
+    grad_normed,
+    middle,
+    cot_own,
+    gain,
+    attended,
+    w_out,
+    hidden,
+    grad_gate,
+    grad_up,
+    cot,
+    normed,
+    grad_middle,
+    gain_part,
+    grad_attended,
+    inner,
+    down_grad,
+    up_low,
+    up_high,
+    gate_parts,
+    out_parts,
+    branch,
+    units_in,
+    turned,
+    strip,
+    down_parts,
+    up_parts,
+    other_parts,
+    down_up_in,
+    down_down_in,
+    up_up_in,
+    up_down_in,
+    att_turned,
+    out_sum,
+    g_send,
+    g_recv,
+    *sems,
+):
+    p = Place(line)
+    down_sems, up_sems, loads, strips_sem, saves = sems[0:4], sems[4:8], *sems[8:11]
+    rows, width = grad_normed.shape
+    slab = w_out.shape[2]
+    part = attended.shape[1]
+    block = lambda j: branch.at[pl.ds(pl.multiple_of(j * rows, rows), rows)]
+    gather = HeadGather(p, block, g_send, g_recv)
+    down_reduce = LineReduce(
+        p, lambda d: down_parts.at[d], down_up_in, down_down_in, *down_sems
+    )
+    up_reduce = LineReduce(
+        p, lambda d: up_parts.at[d, pl.ds(0, cut)], up_up_in, up_down_in, *up_sems
+    )
+    load = [
+        pltpu.make_async_copy(source, units_in, loads.at[i])
+        for i, source in enumerate((hidden, grad_up, grad_gate))
+    ]
+    load[0].start()
+    p.greet()
+    mine = block(p.h)
+    gain_part[...] = jnp.zeros_like(gain_part)
+    step = 32
+
+    @pl.loop(0, rows // step)
+    def _(i):
+        at = pl.ds(pl.multiple_of(i * step, step), step)
+        value = middle[at]
+        inverse = lax.rsqrt(jnp.mean(value * value, axis=-1, keepdims=True) + EPS)
+        unit = value * inverse
+        grad = grad_normed[at]
+        gain_part[...] += jnp.sum(grad * unit, axis=0, keepdims=True)
+        result = cot_own[at].astype(F32) + norm_back(unit, inverse, gain[...], grad)
+        grad_middle[at] = result
+        mine[at] = result.astype(BF16)
+
+    gather.start()
+    clear_last(down_reduce)
+    clear_last(up_reduce)
+    load[0].wait()
+    turn_rows(units_in, turned)
+    load[1].start()
+    weight_product(turned, cot, lambda d: down_parts.at[d], strip, strips_sem)
+    down_reduce.start(0)
+    load[1].wait()
+    turn_rows(units_in, turned)
+    load[2].start()
+    gather.got_core()
+    weight_product(turned, normed, lambda d: up_parts.at[d], strip, strips_sem)
+    up_reduce.start(0)
+    down_reduce.step(0)
+    gather.got_first()
+    gather.got_second()
+    save_up = pltpu.make_async_copy(
+        up_parts.at[:, pl.ds(cut, up_parts.shape[1] - cut)], up_high, saves.at[0]
+    )
+    save_up.start()
+    load[2].wait()
+    turn_rows(units_in, turned)
+    weight_product(turned, normed, lambda d: other_parts.at[d], strip, strips_sem)
+    save_gate = pltpu.make_async_copy(other_parts, gate_parts, saves.at[1])
+    save_gate.start()
+    turn_rows(attended, att_turned)
+    down_reduce.step(1)
+    gather.got_core_second()
+    gather.got_core_first()
+    out_sum[...] = jnp.zeros_like(out_sum)
+
+    def take(j):
+        start = pl.multiple_of(j * rows, rows)
+        at = pl.ds(start, rows)
+        total = product_nt(branch[at, 0:slab], w_out[0])
+        for d in range(1, line):
+            total = total + product_nt(branch[at, d * slab : (d + 1) * slab], w_out[d])
+        low = total.astype(BF16)
+        grad_attended[at, :] = low
+        for head in range(part // HEAD_DIM):
+            cols = slice(head * HEAD_DIM, (head + 1) * HEAD_DIM)
+            both = low[:, cols].astype(F32) * attended[at, cols].astype(F32)
+            inner[head : head + 1, at] = jnp.sum(both.T, axis=0, keepdims=True)
+
+        @pl.loop(0, line)
+        def _(d):
+            cols = pl.ds(pl.multiple_of(d * slab, slab), slab)
+            out_sum[d] += product(att_turned[:, at], branch[at, cols])
+
+    for j in (p.h, p.core, p.first, p.second):
+        take(j)
+    up_reduce.step(0)
+    for j in (p.second + p.turn, p.first + p.turn):
+        take(j)
+    gather.got_across()
+    take(p.across)
+    gather.got_core_across()
+    take(p.across + p.turn)
+    for d in range(line):
+        out_parts[d] = out_sum[d].astype(BF16)
+    down_reduce.step(2)
+    for first, last in strips(down_grad.shape[0], 128):
+        down_grad[first:last, :] = down_reduce.total(slice(first, last))
+    up_reduce.step(1)
+    up_reduce.step(2)
+    for first, last in strips(cut, 128):
+        up_low[:, first:last] = up_reduce.total(slice(first, last)).T
+    gather.finish()
+    down_reduce.finish()
+    up_reduce.finish()
+    save_up.wait()
+    save_gate.wait()
+
+
+def give_back(line, cut, grad_normed, middle, cot_own, gain, attended, w_out, hidden, grad_gate, grad_up, cot, normed):
+    rows, width = middle.shape
+    full, units = hidden.shape
+    part = attended.shape[1]
+    slab = w_out.shape[2]
+    heads = part // HEAD_DIM
+    return pl.pallas_call(
+        functools.partial(return_kernel, line, cut),
+        out_shape=(
+            jax.ShapeDtypeStruct((rows, width), F32),
+            jax.ShapeDtypeStruct((1, width), F32),
+            jax.ShapeDtypeStruct((full, part), BF16),
+            jax.ShapeDtypeStruct((heads, full), F32),
+            jax.ShapeDtypeStruct((units, slab), F32),
+            jax.ShapeDtypeStruct((slab, cut), F32),
+            jax.ShapeDtypeStruct((line, units - cut, slab), BF16),
+            jax.ShapeDtypeStruct((line, units, slab), BF16),
+            jax.ShapeDtypeStruct((line, part, slab), BF16),
+        ),
+        in_specs=[vmem_spec()] * 6 + [any_spec()] * 5,
+        out_specs=(
+            vmem_spec(),
+            vmem_spec(),
+            vmem_spec(),
+            vmem_spec(),
+            vmem_spec(),
+            vmem_spec(),
+            any_spec(),
+            any_spec(),
+            vmem_spec(),
+        ),
+        scratch_shapes=[
+            pltpu.VMEM((full, width), BF16),
+            pltpu.VMEM((full, units), BF16),
+            pltpu.VMEM((units, full), BF16),
+            pltpu.VMEM((2, full, 256), BF16),
+            pltpu.VMEM((line, units, slab), BF16),
+            pltpu.VMEM((line, units, slab), BF16),
+            pltpu.VMEM((line, units, slab), BF16),
+            pltpu.VMEM((line - 1, units, slab), BF16),
+            pltpu.VMEM((line - 1, units, slab), BF16),
+            pltpu.VMEM((line - 1, cut, slab), BF16),
+            pltpu.VMEM((line - 1, cut, slab), BF16),
+            pltpu.VMEM((part, full), BF16),
+            pltpu.VMEM((line, part, slab), F32),
+            pltpu.SemaphoreType.DMA((7,)),
+            pltpu.SemaphoreType.DMA((7,)),
+            *line_sems(line, 2),
+            pltpu.SemaphoreType.DMA((3,)),
+            pltpu.SemaphoreType.DMA((2,)),
+            pltpu.SemaphoreType.DMA((2,)),
+        ],
+        compiler_params=pltpu.CompilerParams(
+            collective_id=5, has_side_effects=True, vmem_limit_bytes=62 * MIB
+        ),
+        cost_estimate=pl.CostEstimate(
+            flops=35 * 2**30, bytes_accessed=80 * MIB, transcendentals=0
+        ),
+    )(
+        grad_normed,
+        middle,
+        cot_own,
+        gain.reshape(1, width),
+        attended,
+        w_out,
+        hidden,
+        grad_gate,
+        grad_up,
+        cot,
+        normed,
+    )
+
+
+def backward_tile(tile, q, k_ext, v_ext, k_t, floor, logs, inner, grad, key_sum, value_sum):
+    start = pl.multiple_of(tile * TILE, TILE)
+    mine = pl.ds(start, TILE)
+    scale = HEAD_DIM ** (-0.5)
+    for head in range(q.shape[1] // HEAD_DIM):
+        cols = slice(head * HEAD_DIM, (head + 1) * HEAD_DIM)
+        queries = q[mine, cols]
+        grads = grad[mine, cols]
+        log = logs[head : head + 1, mine]
+        middle = inner[head : head + 1, mine]
+        turned = jnp.zeros((HEAD_DIM, TILE), F32)
+        for i, (scores, visible) in enumerate(tile_scores(tile, head, q, k_ext, floor)):
+            at = pl.ds(start + i * TILE, TILE)
+            probs = jnp.where(visible, jnp.exp2(scores * (scale * LOG2E) - log), 0.0)
+            grad_probs = product_nt(v_ext[at, cols], grads)
+            grad_scores = (probs * (grad_probs - middle)).astype(BF16)
+            value_sum[at, cols] += product(probs.astype(BF16), grads)
+            key_sum[at, cols] += product(grad_scores, queries)
+            turned = turned + product(k_t[cols, at], grad_scores)
+        q[mine, cols] = (turned * scale).astype(BF16).T
+
+
+def block_reduce(place, out, into, r_send, r_recv):
+    p = place
+    goes = (p.core, p.core, p.core, p.core, p.first, p.first, p.second)
+    slots = (0, 1, 0, 1, 2, 3, 4)
+    return [
+        remote(out.at[slots[i]], into.at[i], r_send.at[i], r_recv.at[i], p.at(to))
+        for i, to in enumerate(goes)
+    ]
+
+
+def attend_back_kernel(
+    line,
+    qkv,
+    halo_kv,
+    floor,
+    logs,
+    grad,
+    inner,
+    hidden,
+    w_down,
+    middle,
+    gate_in,
+    grads_out,
+    result,
+    gate_grad,
+    q,
+    k_ext,
+    v_ext,
+    k_t,
+    key_sum,
+    value_sum,
+    halo_out,
+    halo_in,
+    gate_parts,
+    gate_up_in,
+    gate_down_in,
+    out,
+    into,
+    total,
+    hidden_block,
+    r_send,
+    r_recv,
+    *sems,
+):
+    p = Place(line)
+    gate_sems, loads, halo_send, halo_recv, stage, saves = sems[0:4], *sems[4:9]
+    rows, width = result.shape
+    slab = w_down.shape[2]
+    count, part = q.shape
+    scale = HEAD_DIM ** (-0.5)
+    rows_of = lambda ref, j: ref.at[pl.ds(pl.multiple_of(j * rows, rows), rows)]
+    gate_reduce = LineReduce(
+        p, lambda d: gate_parts.at[d], gate_up_in, gate_down_in, *gate_sems
+    )
+    started = [
+        pltpu.make_async_copy(gate_in, gate_parts, loads.at[0]),
+        pltpu.make_async_copy(qkv.at[:, pl.ds(0, part)], q, loads.at[1]),
+        pltpu.make_async_copy(
+            qkv.at[:, pl.ds(part, part)], k_ext.at[pl.ds(WINDOW, count)], loads.at[2]
+        ),
+        pltpu.make_async_copy(
+            qkv.at[:, pl.ds(2 * part, part)], v_ext.at[pl.ds(WINDOW, count)], loads.at[3]
+        ),
+        pltpu.make_async_copy(halo_kv.at[0], k_ext.at[pl.ds(0, WINDOW)], loads.at[4]),
+        pltpu.make_async_copy(halo_kv.at[1], v_ext.at[pl.ds(0, WINDOW)], loads.at[5]),
+        pltpu.make_async_copy(middle, total, loads.at[6]),
+    ]
+    halo = [
+        remote(
+            halo_out.at[i], halo_in.at[i], halo_send.at[i], halo_recv.at[i], (p.s - 1, p.h)
+        )
+        for i in range(2)
+    ]
+    order = (
+        p.second + p.turn,
+        p.across + p.turn,
+        p.first,
+        p.first + p.turn,
+        p.across,
+        p.core,
+        p.h,
+        p.second,
+    )
+    fetches = [
+        pltpu.make_async_copy(rows_of(hidden, j), hidden_block.at[n % 2], stage.at[n % 2])
+        for n, j in enumerate(order)
+    ]
+    copies = block_reduce(p, out, into, r_send, r_recv)
+
+    def emit(n, target, *more):
+        fetches[n].wait()
+        if n + 1 < len(order):
+            fetches[n + 1].start()
+
+        @pl.loop(0, line)
+        def _(d):
+            cols = pl.ds(pl.multiple_of(d * slab, slab), slab)
+            value = product(hidden_block[n % 2], w_down[d])
+            for other in more:
+                value = value + other[:, cols].astype(F32)
+            target[:, cols] = value.astype(target.dtype)
+
+    def tiles(first, last):
+        @pl.loop(first, last)
+        def _(tile):
+            backward_tile(
+                tile, q, k_ext, v_ext, k_t, floor, logs, inner, grad, key_sum, value_sum
+            )
+
+    for copy in started:
+        copy.start()
+    fetches[0].start()
+    p.greet()
+    started[0].wait()
+    gate_reduce.start(0)
+    clear_last(gate_reduce)
+    emit(0, out.at[0])
+    copies[0].start()
+    emit(1, out.at[1])
+    copies[1].start()
+    copies[0].wait_recv()
+    emit(2, out.at[2], into.at[0])
+    copies[4].start()
+    copies[0].wait_send()
+    emit(3, out.at[0])
+    copies[2].start()
+    copies[1].wait_recv()
+    emit(4, out.at[3], into.at[1])
+    copies[5].start()
+    copies[1].wait_send()
+    emit(5, out.at[1])
+    copies[3].start()
+    for copy in started[1:]:
+        copy.wait()
+
+    @pl.loop(0, (WINDOW + count) // TILE)
+    def _(i):
+        at = pl.ds(pl.multiple_of(i * TILE, TILE), TILE)
+        k_t[:, at] = k_ext[at, :].T
+        key_sum[at, :] = jnp.zeros((TILE, part), F32)
+        value_sum[at, :] = jnp.zeros((TILE, part), F32)
+
+    ahead = WINDOW // TILE
+    last = count // TILE
+    tiles(0, ahead)
+
+    @pl.when(p.s > 0)
+    def _():
+        @pl.loop(0, ahead)
+        def _(i):
+            at = pl.ds(pl.multiple_of(i * TILE, TILE), TILE)
+            halo_out[0, at, :] = (key_sum[at, :] * scale).astype(BF16)
+            halo_out[1, at, :] = value_sum[at, :].astype(BF16)
+
+        halo[0].start()
+        halo[1].start()
+
+    gate_reduce.step(0)
+    tiles(ahead, ahead + 4)
+    copies[3].wait_recv()
+    emit(6, total, into.at[3], total)
+    copies[2].wait_recv()
+    copies[5].wait_recv()
+    emit(7, out.at[4], into.at[2], into.at[5])
+    copies[6].start()
+    gate_reduce.step(1)
+    tiles(ahead + 4, last)
+
+    @pl.when(p.s < line - 1)
+    def _():
+        halo[0].wait_recv()
+        halo[1].wait_recv()
+
+    @pl.loop(0, last)
+    def _(i):
+        here = pl.ds(pl.multiple_of(i * TILE, TILE), TILE)
+        at = pl.ds(pl.multiple_of(i * TILE + WINDOW, TILE), TILE)
+        key_value = key_sum[at, :] * scale
+        value_value = value_sum[at, :]
+        k_ext[here, :] = key_value.astype(BF16)
+        v_ext[here, :] = value_value.astype(BF16)
+
+    @pl.when(p.s < line - 1)
+    def _():
+        @pl.loop(0, ahead)
+        def _(i):
+            here = pl.ds(pl.multiple_of(i * TILE, TILE), TILE)
+            near = pl.ds(pl.multiple_of(i * TILE + count, TILE), TILE)
+            there = pl.ds(pl.multiple_of(i * TILE + count - WINDOW, TILE), TILE)
+            k_ext[there, :] = (
+                key_sum[near, :] * scale + halo_in[0, here, :].astype(F32)
+            ).astype(BF16)
+            v_ext[there, :] = (value_sum[near, :] + halo_in[1, here, :].astype(F32)).astype(BF16)
+
+    save = [
+        pltpu.make_async_copy(
+            ref.at[pl.ds(0, count)], grads_out.at[:, pl.ds(i * part, part)], saves.at[i]
+        )
+        for i, ref in enumerate((q, k_ext, v_ext))
+    ]
+    for copy in save:
+        copy.start()
+    copies[4].wait_recv()
+    copies[6].wait_recv()
+
+    @pl.loop(0, line)
+    def _(d):
+        cols = pl.ds(pl.multiple_of(d * slab, slab), slab)
+        value = total[:, cols] + into[4, :, cols].astype(F32) + into[6, :, cols].astype(F32)
+        result[:, cols] = value.astype(BF16)
+
+    gate_reduce.step(2)
+    for first, stop in strips(gate_grad.shape[1], 128):
+        gate_grad[:, first:stop] = gate_reduce.total(slice(first, stop)).T
+    for i in range(2, 7):
+        copies[i].wait_send()
+    gate_reduce.finish()
+
+    @pl.when(p.s > 0)
+    def _():
+        halo[0].wait_send()
+        halo[1].wait_send()
+
+    for copy in save:
+        copy.wait()
+
+
+def attend_back(line, qkv, halo_kv, floor, logs, grad, inner, hidden, w_down, middle, gate_parts):
+    rows, width = middle.shape
+    count = qkv.shape[0]
+    part = qkv.shape[1] // 3
+    units, slab = w_down.shape[1:]
+    return pl.pallas_call(
+        functools.partial(attend_back_kernel, line),
+        out_shape=(
+            jax.ShapeDtypeStruct((count, 3 * part), BF16),
+            jax.ShapeDtypeStruct((rows, width), BF16),
+            jax.ShapeDtypeStruct((slab, units), F32),
+        ),
+        in_specs=[any_spec()] * 2
+        + [vmem_spec()] * 4
+        + [any_spec(), vmem_spec(), any_spec(), any_spec()],
+        out_specs=(any_spec(), vmem_spec(), vmem_spec()),
+        scratch_shapes=[
+            pltpu.VMEM((count, part), BF16),
+            pltpu.VMEM((WINDOW + count, part), BF16),
+            pltpu.VMEM((WINDOW + count, part), BF16),
+            pltpu.VMEM((part, WINDOW + count), BF16),
+            pltpu.VMEM((WINDOW + count, part), F32),
+            pltpu.VMEM((WINDOW + count, part), F32),
+            pltpu.VMEM((2, WINDOW, part), BF16),
+            pltpu.VMEM((2, WINDOW, part), BF16),
+            pltpu.VMEM((line, units, slab), BF16),
+            pltpu.VMEM((line - 1, units, slab), BF16),
+            pltpu.VMEM((line - 1, units, slab), BF16),
+            pltpu.VMEM((5, rows, width), BF16),
+            pltpu.VMEM((7, rows, width), BF16),
+            pltpu.VMEM((rows, width), F32),
+            pltpu.VMEM((2, rows, units), BF16),
+            pltpu.SemaphoreType.DMA((7,)),
+            pltpu.SemaphoreType.DMA((7,)),
+            *line_sems(line),
+            pltpu.SemaphoreType.DMA((7,)),
+            pltpu.SemaphoreType.DMA((2,)),
+            pltpu.SemaphoreType.DMA((2,)),
+            pltpu.SemaphoreType.DMA((2,)),
+            pltpu.SemaphoreType.DMA((3,)),
+        ],
+        compiler_params=pltpu.CompilerParams(
+            collective_id=6, has_side_effects=True, vmem_limit_bytes=62 * MIB
+        ),
+        cost_estimate=pl.CostEstimate(
+            flops=20 * 2**30, bytes_accessed=60 * MIB, transcendentals=0
+        ),
+    )(qkv, halo_kv, floor, logs, grad, inner, hidden, w_down, middle, gate_parts)
+
+
+def finish_kernel(
+    line,
+    grads,
+    weight,
+    normed,
+    tokens,
+    gain,
+    grad_middle,
+    up_high,
+    up_low,
+    out_given,
+    ffn_gain_part,
+    input_grad,
+    gain_sums,
+    query_grad,
+    key_grad,
+    value_grad,
+    out_grad,
+    up_grad,
+    turned,
+    strip,
+    parts,
+    parts_up_in,
+    parts_down_in,
+    up_parts,
+    up_up_in,
+    up_down_in,
+    out_parts,
+    out_up_in,
+    out_down_in,
+    out,
+    into,
+    total,
+    gain_line,
+    gain_in,
+    r_send,
+    r_recv,
+    *sems,
+):
+    p = Place(line)
+    part_sems, up_sems, out_sems, gain_sems = sems[0:4], sems[4:8], sems[8:12], sems[12:16]
+    loads, strip_sems, gain_send, gain_recv = sems[16:20]
+    rows, width = tokens.shape
+    slab = width // line
+    part = query_grad.shape[1]
+    cut = up_low.shape[1]
+    part_reduce = LineReduce(p, lambda d: parts.at[d], parts_up_in, parts_down_in, *part_sems)
+    up_reduce = LineReduce(p, lambda d: up_parts.at[d], up_up_in, up_down_in, *up_sems)
+    out_reduce = LineReduce(p, lambda d: out_parts.at[d], out_up_in, out_down_in, *out_sems)
+    started = [
+        pltpu.make_async_copy(up_high, up_parts, loads.at[0]),
+        pltpu.make_async_copy(out_given, out_parts, loads.at[1]),
+        pltpu.make_async_copy(up_low, up_grad.at[:, pl.ds(0, cut)], loads.at[2]),
+        pltpu.make_async_copy(grad_middle, input_grad, loads.at[3]),
+    ]
+    for copy in started:
+        copy.start()
+    p.greet()
+    started[0].wait()
+    up_reduce.start(0)
+    started[1].wait()
+    out_reduce.start(0)
+    for reduce in (part_reduce, up_reduce, out_reduce):
+        clear_last(reduce)
+    copies = block_reduce(p, out, into, r_send, r_recv)
+
+    def emit(j, target, *more):
+        at = pl.ds(pl.multiple_of(j * rows, rows), rows)
+
+        @pl.loop(0, line)
+        def _(d):
+            cols = pl.ds(pl.multiple_of(d * slab, slab), slab)
+            value = product_nt(grads[at, :], weight[cols, :])
+            for other in more:
+                value = value + other[:, cols].astype(F32)
+            target[:, cols] = value.astype(target.dtype)
+
+    emit(p.second + p.turn, out.at[0])
+    copies[0].start()
+    emit(p.across + p.turn, out.at[1])
+    copies[1].start()
+    copies[0].wait_recv()
+    emit(p.first, out.at[2], into.at[0])
+    copies[4].start()
+    copies[0].wait_send()
+    emit(p.first + p.turn, out.at[0])
+    copies[2].start()
+    copies[1].wait_recv()
+    emit(p.across, out.at[3], into.at[1])
+    copies[5].start()
+    copies[1].wait_send()
+    emit(p.core, out.at[1])
+    copies[3].start()
+    turn_rows(grads, turned)
+    up_reduce.step(0)
+    out_reduce.step(0)
+    weight_product(turned, normed, lambda d: parts.at[d], strip, strip_sems)
+    part_reduce.start(0)
+    copies[3].wait_recv()
+    emit(p.h, total, into.at[3])
+    up_reduce.step(1)
+    out_reduce.step(1)
+    copies[2].wait_recv()
+    copies[5].wait_recv()
+    emit(p.second, out.at[4], into.at[2], into.at[5])
+    copies[6].start()
+    up_reduce.step(2)
+    out_reduce.step(2)
+    part_reduce.step(0)
+    started[2].wait()
+    for first, last in strips(up_parts.shape[1], 128):
+        up_grad[:, cut + first : cut + last] = up_reduce.total(slice(first, last)).T
+    for first, last in strips(part, 128):
+        out_grad[first:last, :] = out_reduce.total(slice(first, last))
+    copies[4].wait_recv()
+    copies[6].wait_recv()
+    started[3].wait()
+    gain_own = gain_line.at[p.s]
+    gain_own[...] = jnp.zeros(gain_own.shape, F32)
+    gain_own[1:2, :] = ffn_gain_part[...]
+    step = 32
+
+    @pl.loop(0, rows // step)
+    def _(i):
+        at = pl.ds(pl.multiple_of(i * step, step), step)
+        grad = total[at] + into[4, at].astype(F32) + into[6, at].astype(F32)
+        unit, inverse = normalize(tokens[at].astype(F32))
+        gain_own[0:1, :] += jnp.sum(grad * unit, axis=0, keepdims=True)
+        input_grad[at] += norm_back(unit, inverse, gain[...], grad)
+
+    part_reduce.step(1)
+    for i, head in enumerate((p.core, p.first, p.second)):
+        copy = remote(gain_own, gain_in.at[i], gain_send.at[i], gain_recv.at[i], p.at(head))
+        copy.start()
+        copy.wait()
+        gain_own[...] += gain_in[i]
+    gain_gather = LineGather(p, lambda d: gain_line.at[d], *gain_sems)
+    gain_gather.start(0)
+    for t in range(line - 1):
+        gain_gather.step(t)
+    summed = gain_line[0]
+    for d in range(1, line):
+        summed = summed + gain_line[d]
+    gain_sums[...] = summed
+    part_reduce.step(2)
+    for i, target in enumerate((query_grad, key_grad, value_grad)):
+        for first, last in strips(part, 128):
+            target[:, first:last] = part_reduce.total(
+                slice(i * part + first, i * part + last)
+            ).T
+    for i in range(2, 7):
+        copies[i].wait_send()
+    gain_gather.finish()
+    for reduce in (part_reduce, up_reduce, out_reduce):
+        reduce.finish()
+
+
+def finish(line, grads, weight, normed, tokens, gain, grad_middle, up_high, up_low, out_parts, ffn_gain_part):
+    rows, width = tokens.shape
+    full = grads.shape[0]
+    part = grads.shape[1] // 3
+    slab = width // line
+    rest = up_high.shape[1]
+    units = up_low.shape[1] + rest
+    return pl.pallas_call(
+        functools.partial(finish_kernel, line),
+        out_shape=(
+            jax.ShapeDtypeStruct((rows, width), F32),
+            jax.ShapeDtypeStruct((8, width), F32),
+            jax.ShapeDtypeStruct((slab, part), F32),
+            jax.ShapeDtypeStruct((slab, part), F32),
+            jax.ShapeDtypeStruct((slab, part), F32),
+            jax.ShapeDtypeStruct((part, slab), F32),
+            jax.ShapeDtypeStruct((slab, units), F32),
+        ),
+        in_specs=[
+            vmem_spec(),
+            vmem_spec(),
+            any_spec(),
+            vmem_spec(),
+            vmem_spec(),
+            any_spec(),
+            any_spec(),
+            any_spec(),
+            any_spec(),
+            vmem_spec(),
+        ],
+        out_specs=(vmem_spec(),) * 7,
+        scratch_shapes=[
+            pltpu.VMEM((3 * part, full), BF16),
+            pltpu.VMEM((2, full, 256), BF16),
+            pltpu.VMEM((line, 3 * part, slab), BF16),
+            pltpu.VMEM((line - 1, 3 * part, slab), BF16),
+            pltpu.VMEM((line - 1, 3 * part, slab), BF16),
+            pltpu.VMEM((line, rest, slab), BF16),
+            pltpu.VMEM((line - 1, rest, slab), BF16),
+            pltpu.VMEM((line - 1, rest, slab), BF16),
+            pltpu.VMEM((line, part, slab), BF16),
+            pltpu.VMEM((line - 1, part, slab), BF16),
+            pltpu.VMEM((line - 1, part, slab), BF16),
+            pltpu.VMEM((5, rows, width), BF16),
+            pltpu.VMEM((7, rows, width), BF16),
+            pltpu.VMEM((rows, width), F32),
+            pltpu.VMEM((line, 8, width), F32),
+            pltpu.VMEM((3, 8, width), F32),
+            pltpu.SemaphoreType.DMA((7,)),
+            pltpu.SemaphoreType.DMA((7,)),
+            *line_sems(line, 4),
+            pltpu.SemaphoreType.DMA((4,)),
+            pltpu.SemaphoreType.DMA((2,)),
+            pltpu.SemaphoreType.DMA((3,)),
+            pltpu.SemaphoreType.DMA((3,)),
+        ],
+        compiler_params=pltpu.CompilerParams(
+            collective_id=7, has_side_effects=True, vmem_limit_bytes=62 * MIB
+        ),
+        cost_estimate=pl.CostEstimate(
+            flops=20 * 2**30, bytes_accessed=60 * MIB, transcendentals=0
+        ),
+    )(
+        grads,
+        weight,
+        normed,
+        tokens,
+        gain.reshape(1, width),
+        grad_middle,
+        up_high,
+        up_low,
+        out_parts,
+        ffn_gain_part,
+    )
+
+
 def fused(
     tokens,
     segment,
@@ -1333,16 +2235,8 @@
     down_weight,
     cotangent,
 ):
-    own_rows = tokens.shape[0]
-    group = own_rows * lax.axis_size("head")
-    heads_here = query_weight.shape[1] // HEAD_DIM
-    offset = lax.axis_index("head") * own_rows
-    seq_index = lax.axis_index("seq")
-    block = min(512, group)
-    scale = HEAD_DIM ** (-0.5)
     line = lax.axis_size("seq")
-    part = query_weight.shape[1]
-    normed_full, qkv, w_qkv, floor, gate_t, up_t = project(
+    normed_one, qkv, w_qkv, floor, gate_t, up_t = project(
         line,
         tokens,
         attn_gain,
@@ -1353,162 +2247,70 @@
         gate_weight,
         up_weight,
     )
-    cut = gate_t.shape[0] // 32 * 16 + 16
-    attended, logs, halo_kv, grad_out, w_out_parts, gate_a = attend(
+    cut = gate_t.shape[0] // 256 * 128 + 128
+    attended, logs, halo_kv, cot_full, w_out, gate_a = attend(
         line, qkv, floor, cotangent, out_weight, gate_t[:cut]
     )
-    middle, gate_b, up_all = branch(line, attended, w_out_parts, tokens, gate_t[cut:], up_t)
-    normed_two_full, hidden, grad_gate, grad_up, grad_normed_two, down_parts = feed(
-        line, middle, ffn_gain, grad_out, gate_a, gate_b, up_all, down_weight
-    )
-    w_down = down_parts.transpose(1, 0, 2).reshape(down_weight.shape[0], -1)
-    w_out = w_out_parts.transpose(1, 0, 2).reshape(part, -1)
-    w_query, w_key, w_value = (w_qkv[:, i * part : (i + 1) * part] for i in range(3))
-    queries, keys, values = (qkv[:, i * part : (i + 1) * part] for i in range(3))
-    inputs = tokens.astype(jnp.float32)
-    unit_one, inverse_one = normalize(inputs)
-    halo_keys, halo_values, halo_segs = ([], [], [])
-    hop = 1
-    take = min(group, WINDOW - (hop - 1) * group)
-    got_keys, got_values, got_segs = from_behind(
-        (keys[group - take :], values[group - take :], segment[group - take :]), "seq", hop
-    )
-    halo_keys.append(got_keys)
-    halo_values.append(got_values)
-    halo_segs.append(got_segs)
-    keys_ext = jnp.concatenate(halo_keys + [keys], axis=0)
-    values_ext = jnp.concatenate(halo_values + [values], axis=0)
-    segs_ext = jnp.concatenate(halo_segs + [segment], axis=0)
-    positions = seq_index * group - WINDOW + jnp.arange(WINDOW + group)
-    valid = positions >= 0
-    query_heads = queries.reshape(group, heads_here, HEAD_DIM)
-    key_heads = keys_ext.reshape(WINDOW + group, heads_here, HEAD_DIM)
-    value_heads = values_ext.reshape(WINDOW + group, heads_here, HEAD_DIM)
-    logsums = [
-        logs[:, start : start + block, None] * 0.6931471805599453
-        for start in range(0, group, block)
-    ]
-    unit_two, inverse_two = normalize(middle)
-    ffn_out = lax.psum_scatter(
-        product(hidden, w_down).astype(jnp.bfloat16), "head", scatter_dimension=0, tiled=True
-    ).astype(jnp.float32)
-    result = middle + ffn_out
-    down_grad = product_tn(hidden, grad_out)
-    gate_grad = product_tn(normed_two_full, grad_gate)
-    up_grad = product_tn(normed_two_full, grad_up)
-    ffn_gain_part = jnp.sum(grad_normed_two * unit_two, axis=0)
-    grad_middle = cotangent.astype(jnp.float32) + norm_back(
-        unit_two, inverse_two, ffn_gain, grad_normed_two
-    )
-    grad_branch = lax.all_gather(grad_middle.astype(jnp.bfloat16), "head", axis=0, tiled=True)
-    out_grad = product_tn(attended, grad_branch)
-    grad_attended = product_nt(grad_branch, w_out).astype(jnp.bfloat16)
-    grad_heads = grad_attended.reshape(group, heads_here, HEAD_DIM)
-    grad_query_list = []
-    grad_keys_ext = jnp.zeros((WINDOW + group, heads_here, HEAD_DIM), jnp.float32)
-    grad_values_ext = jnp.zeros((WINDOW + group, heads_here, HEAD_DIM), jnp.float32)
-    for number, start in enumerate(range(0, group, block)):
-        scores = block_scores(query_heads, key_heads, segment, segs_ext, valid, start, block)
-        probs = jnp.exp(scores - logsums[number])
-        probs_low = probs.astype(jnp.bfloat16)
-        key_part = key_heads[start : start + block + WINDOW]
-        value_part = value_heads[start : start + block + WINDOW]
-        query_part = query_heads[start : start + block]
-        grad_part = grad_heads[start : start + block]
-        grad_probs = jnp.einsum(
-            "qhd,khd->hqk", grad_part, value_part, preferred_element_type=jnp.float32
-        )
-        inner = jnp.sum(probs * grad_probs, axis=-1, keepdims=True)
-        grad_scores = (probs * (grad_probs - inner)).astype(jnp.bfloat16)
-        grad_query_list.append(
-            jnp.einsum("hqk,khd->qhd", grad_scores, key_part, preferred_element_type=jnp.float32)
-            * scale
-        )
-        key_term = (
-            jnp.einsum("hqk,qhd->khd", grad_scores, query_part, preferred_element_type=jnp.float32)
-            * scale
-        )
-        value_term = jnp.einsum(
-            "hqk,qhd->khd", probs_low, grad_part, preferred_element_type=jnp.float32
-        )
-        grad_keys_ext = grad_keys_ext.at[start : start + block + WINDOW].add(key_term)
-        grad_values_ext = grad_values_ext.at[start : start + block + WINDOW].add(value_term)
-    grad_keys_ext = grad_keys_ext.reshape(WINDOW + group, heads_here * HEAD_DIM)
-    grad_values_ext = grad_values_ext.reshape(WINDOW + group, heads_here * HEAD_DIM)
-    grad_keys = grad_keys_ext[WINDOW:]
-    grad_values = grad_values_ext[WINDOW:]
-    cursor = 0
-    hop = 1
-    take = min(group, WINDOW - (hop - 1) * group)
-    back_keys = from_behind(
-        grad_keys_ext[cursor : cursor + take].astype(jnp.bfloat16), "seq", -hop
-    ).astype(jnp.float32)
-    back_values = from_behind(
-        grad_values_ext[cursor : cursor + take].astype(jnp.bfloat16), "seq", -hop
-    ).astype(jnp.float32)
-    grad_keys = grad_keys.at[group - take :].add(back_keys)
-    grad_values = grad_values.at[group - take :].add(back_values)
-    grad_queries = (
-        jnp.concatenate(grad_query_list, axis=0)
-        .reshape(group, heads_here * HEAD_DIM)
-        .astype(jnp.bfloat16)
-    )
-    grad_keys = grad_keys.astype(jnp.bfloat16)
-    grad_values = grad_values.astype(jnp.bfloat16)
-    query_grad = product_tn(normed_full, grad_queries)
-    key_grad = product_tn(normed_full, grad_keys)
-    value_grad = product_tn(normed_full, grad_values)
-    grad_normed_one = lax.psum_scatter(
-        (
-            product_nt(grad_queries, w_query)
-            + product_nt(grad_keys, w_key)
-            + product_nt(grad_values, w_value)
-        ).astype(jnp.bfloat16),
-        "head",
-        scatter_dimension=0,
-        tiled=True,
-    ).astype(jnp.float32)
-    attn_gain_part = jnp.sum(grad_normed_one * unit_one, axis=0)
-    input_grad = grad_middle + norm_back(unit_one, inverse_one, attn_gain, grad_normed_one)
-    summed = (
-        lax.psum_scatter(
-            query_grad.astype(jnp.bfloat16), "seq", scatter_dimension=0, tiled=True
-        ).astype(jnp.float32),
-        lax.psum_scatter(
-            key_grad.astype(jnp.bfloat16), "seq", scatter_dimension=0, tiled=True
-        ).astype(jnp.float32),
-        lax.psum_scatter(
-            value_grad.astype(jnp.bfloat16), "seq", scatter_dimension=0, tiled=True
-        ).astype(jnp.float32),
-        lax.psum_scatter(
-            out_grad.astype(jnp.bfloat16), "seq", scatter_dimension=1, tiled=True
-        ).astype(jnp.float32),
-        lax.psum_scatter(
-            gate_grad.astype(jnp.bfloat16), "seq", scatter_dimension=0, tiled=True
-        ).astype(jnp.float32),
-        lax.psum_scatter(
-            up_grad.astype(jnp.bfloat16), "seq", scatter_dimension=0, tiled=True
-        ).astype(jnp.float32),
-        lax.psum_scatter(
-            down_grad.astype(jnp.bfloat16), "seq", scatter_dimension=1, tiled=True
-        ).astype(jnp.float32),
-    )
-    gain_grads = (
-        lax.psum_scatter(attn_gain_part, ("seq", "head"), scatter_dimension=0, tiled=True),
-        lax.psum_scatter(ffn_gain_part, ("seq", "head"), scatter_dimension=0, tiled=True),
-    )
+    middle, gate_b, w_up = branch(line, attended, w_out, tokens, gate_t[cut:], up_t)
+    normed_two, hidden, grad_gate, grad_up, grad_normed_two, w_down = feed(
+        line, middle, ffn_gain, cot_full, gate_a, gate_b, w_up, down_weight
+    )
+    (
+        grad_middle,
+        ffn_gain_part,
+        grad_attended,
+        inner,
+        down_grad,
+        up_low,
+        up_high,
+        gate_parts,
+        out_parts,
+    ) = give_back(
+        line,
+        cut,
+        grad_normed_two,
+        middle,
+        cotangent,
+        ffn_gain,
+        attended,
+        w_out,
+        hidden,
+        grad_gate,
+        grad_up,
+        cot_full,
+        normed_two,
+    )
+    grads, result, gate_grad = attend_back(
+        line, qkv, halo_kv, floor, logs, grad_attended, inner, hidden, w_down, middle, gate_parts
+    )
+    input_grad, gain_sums, query_grad, key_grad, value_grad, out_grad, up_grad = finish(
+        line,
+        grads,
+        w_qkv,
+        normed_one,
+        tokens,
+        attn_gain,
+        grad_middle,
+        up_high,
+        up_low,
+        out_parts,
+        ffn_gain_part,
+    )
+    share = tokens.shape[1] // (line * lax.axis_size("head"))
+    place = (lax.axis_index("seq") * lax.axis_size("head") + lax.axis_index("head")) * share
+    gain_grads = lax.dynamic_slice(gain_sums, (0, place), (2, share))
     return (
-        result.astype(jnp.bfloat16),
+        result,
         input_grad,
         gain_grads[0],
-        summed[0],
-        summed[1],
-        summed[2],
-        summed[3],
+        query_grad,
+        key_grad,
+        value_grad,
+        out_grad,
         gain_grads[1],
-        summed[4],
-        summed[5],
-        summed[6],
+        gate_grad,
+        up_grad,
+        down_grad,
     )
 
 

time: 927 us -> 688 us (0.74)
  Pallas kernels: 355 us -> 657 us
  matrix products: 215 us -> 0 us
  waiting for transfers between devices: 139 us -> 0 us
  other arithmetic: 62.7 us -> 0 us
  local copies, waits for them, and re-layouts: 75.4 us -> 21.6 us
  blocking collectives: 39.8 us -> 0 us
  between operations: 17.4 us -> 1.35 us
  starting transfers between devices: 13.1 us -> 0 us
    pallas_call x0 -> x3, Pallas kernels: none -> 301 us  [the longest x1 112 us: finish(): pl.pallas_call(functools.partial(finish_kernel, line), out_shape=(jax.Sha...]
    dot_general x42 -> x0, matrix products: 215 us -> none  [the longest x7 79.6 us: product_tn(): lax.dot_general(left, right, (((0,), (0,)), ((), ())), preferred_element_...]
    reduce_scatter x9 -> x0, waiting for transfers between devices: 138 us -> none  [the longest x1 85.1 us: fused(): lax.psum_scatter((product_nt(grad_queries, w_query) + product_nt(grad_key...]
    unnamed x1 -> x0, blocking collectives: 39.8 us -> none
    slice x25 -> x0, local copies, waits for them, and re-layouts: 36.6 us -> none  [the longest x6 9.97 us: fused(): key_part = key_heads[start:start + block + WINDOW]]
    convert_element_type x14 -> x0, other arithmetic: 31.4 us -> none  [the longest x6 14.7 us: fused(): grad_scores = (probs * (grad_probs - inner)).astype(jnp.bfloat16)]
    unnamed x210 -> x53, local copies, waits for them, and re-layouts: 32.6 us -> 20.3 us
    ppermute x5 -> x0, starting transfers between devices: 11.9 us -> none  [from_behind(): return lax.ppermute(value, axis, pairs)]
  transfers between devices with their start and end apart: 15 -> 0, of which waited for: 2 -> 0; matrix products, arithmetic and copies ran while one was open for 34% -> 0% of each run, Pallas kernels for 0% -> 0%
where the time goes in v3:
time: 688 us; the launch traced here: 680 us
  Pallas kernels  657 us (95%)
  local copies, waits for them, and re-layouts  21.6 us (3%)
    pallas_call x1, Pallas kernels, feed(): pl.pallas_call(functools.partial(feed_kernel, line), out_shape=(jax.Shape...  127 us
    pallas_call x1, Pallas kernels, finish(): pl.pallas_call(functools.partial(finish_kernel, line), out_shape=(jax.Sha...  112 us
    pallas_call x1, Pallas kernels, give_back(): pl.pallas_call(functools.partial(return_kernel, line, cut), out_shape=(ja...  99.6 us
    pallas_call x1, Pallas kernels, attend_back(): pl.pallas_call(functools.partial(attend_back_kernel, line), out_shape=(ja...  89.1 us
    pallas_call x1, Pallas kernels, branch(): pl.pallas_call(functools.partial(branch_kernel, line), out_shape=(jax.Sha...  81.7 us
    pallas_call x1, Pallas kernels, project(): pl.pallas_call(functools.partial(project_kernel, line), out_shape=(jax.Sh...  75 us
    pallas_call x1, Pallas kernels, attend(): pl.pallas_call(functools.partial(attend_kernel, line), out_shape=(jax.Sha...  72.7 us
    unnamed x53, local copies, waits for them, and re-layouts  20.3 us

profile of v3, /device:TPU:0, one launch (start us, length us, event | category | flops | bytes accessed | tf_op | source)
XLA Modules:
  0.0 679.9 jit_solution(4872280432318781923)
XLA Ops:
  0.6 0.0 copy-start
  0.7 0.0 copy-start.6
  0.7 1.5 copy.23.w_gate
  2.2 1.4 copy.24.w_up
  3.6 0.0 copy-done
  3.6 0.0 copy-done.6
  3.6 0.0 copy-start.2
  3.6 0.9 copy-done.2
  4.6 0.9 copy-done.3
  5.5 75.0 %shard_map.203 = (bf16[3072,2048]{1,0:T(8,128)(2,1)}, bf16[3072,768]{1,0:T(8,128)(2,1)}, bf16[2048,768]{1,0:T(8,128)(2,1)}, s32[1,3072]{1,0:T(1,128)S(1)}, bf16[...) custom-call(bf16[384,2048]{1,0:T(8,128)(2,1)S(1)} %copy-done, f32[1,2048]{1,0:T(1,128)S(1)} %bitcast.9, ...), custom_call_target="tpu_custom_call" | custom-call | flops 9663676416 | bytes 41943040 | tf_op jit(solution)/shard_map/pallas_call | solution.py:661
  80.5 0.0 copy-start.13
  80.6 72.7 %shard_map.204 = (bf16[3072,256]{1,0:T(8,128)(2,1)S(1)}, f32[2,3072]{1,0:T(2,128)S(1)}, bf16[2,1024,256]{2,1,0:T(8,128)(2,1)S(1)}, bf16[3072,2048]{1,0:T(8,128)(...) custom-call(bf16[3072,768]{1,0:T(8,128)(2,1)} %get-tuple-element.51.qkv, ...), custom_call_target="tpu_custom_call" | custom-call | flops 10737418240 | bytes 41943040 | tf_op jit(solution)/shard_map/pallas_call | solution.py:874
  153.3 0.0 copy-start.10
  153.3 1.1 copy-done.10
  154.5 81.7 %shard_map.205 = (f32[384,2048]{1,0:T(8,128)}, bf16[4,304,512]{2,1,0:T(8,128)(2,1)S(1)}, bf16[4,688,512]{2,1,0:T(8,128)(2,1)}) custom-call(bf16[3072,256]{1,0:T(8,128)(2,1)S(1)} %get-tuple-element.56.attended, bf16[4,256,512]{2,1,0:T(8,128)(2,1)S(1)} %get-tuple-element.57.w_out, bf16[384,2048]{1,0:T(8,128)(2,1)} %tokens.5, ...), custom_call_target="tpu_custom_call" | custom-call | flops 3221225472 | bytes 41943040 | tf_op jit(solution)/shard_map/pallas_call | solution.py:1019
  236.2 0.0 copy-start.8
  236.2 1.0 copy-done.8
  237.3 126.5 %shard_map.206 = (bf16[3072,2048]{1,0:T(8,128)(2,1)}, bf16[3072,688]{1,0:T(8,128)(2,1)}, bf16[3072,688]{1,0:T(8,128)(2,1)}, bf16[3072,688]{1,0:T(8,128)(2,1)}, f...) custom-call(f32[384,2048]{1,0:T(8,128)} %get-tuple-element.59.middle, f32[1,2048]{1,0:T(1,128)} %bitcast.10, ...), custom_call_target="tpu_custom_call" | custom-call | flops 53687091200 | bytes 83886080 | tf_op jit(solution)/shard_map/pallas_call | solution.py:1279
  363.8 99.6 %shard_map.207 = (f32[384,2048]{1,0:T(8,128)}, f32[1,2048]{1,0:T(1,128)}, bf16[3072,256]{1,0:T(8,128)(2,1)}, f32[2,3072]{1,0:T(2,128)}, f32[688,512]{1,0:T(8,128...) custom-call(f32[384,2048]{1,0:T(8,128)} %get-tuple-element.64.grad_n, ...), custom_call_target="tpu_custom_call" | custom-call | flops 37580963840 | bytes 83886080 | tf_op jit(solution)/shard_map/pallas_call | solution.py:1625
  463.4 89.1 %shard_map.208 = (bf16[3072,768]{1,0:T(8,128)(2,1)}, bf16[384,2048]{1,0:T(8,128)(2,1)}, f32[512,688]{1,0:T(8,128)}) custom-call(bf16[3072,768]{1,0:T(8,128)(2,1)} %get-tuple-element.51.qkv, bf16[2,1024,256]{2,1,0:T(8,128)(2,1)} %copy-done.11, s32[1,3072]{1,0:T(1,128)} %copy-done.13, f32[2,3072]{1,0:T(2,128)} %copy-done.12, ...), custom_call_target="tpu_custom_call" | custom-call | flops 21474836480 | bytes 62914560 | tf_op jit(solution)/shard_map/pallas_call | solution.py:1946
  552.5 112.3 %shard_map.209 = (f32[384,2048]{1,0:T(8,128)}, f32[8,2048]{1,0:T(8,128)}, f32[512,256]{1,0:T(8,128)}, f32[512,256]{1,0:T(8,128)}, f32[512,256]{1,0:T(8,128)}, /*index=5*/f32[256,512]{1,0:T(8,128)}, f32[512,688]{1,0:T(8,128)}) custom-call(bf16[3072,768]{1,0:T(8,128)(2,1)} %get-tuple-element.74.grads, bf16[2048,768]{1,0:T(8,128)(2,1)} %get-tuple-element.75.weight, ...), custom_call_target="tpu_custom_call" | custom-call | flops 21474836480 | bytes 62914560 | tf_op jit(solution)/shard_map/pallas_call | solution.py:2155
  664.9 0.8 constant_dynamic-slice_fusion
  665.7 0.5 slice_bitcast_fusion
  666.2 1.5 copy.25
  667.7 3.1 copy.26
  670.8 2.7 copy.34
  673.6 1.7 copy.35
  675.2 0.8 copy.36
  676.0 0.8 copy.37
  676.8 0.8 copy.38
  677.6 0.8 copy.39
  678.4 1.1 copy.40
  (32 shorter events, 0.1 us)
Async XLA Ops:
  0.6 2.9 copy-start
  0.7 2.9 copy-start.6
  0.7 2.9 copy-start.1
  0.7 2.9 copy-start.5
  3.6 1.0 copy-start.2
  4.6 0.9 copy-start.3
  5.5 75.0 %copy-start.4 = (bf16[256,512]{1,0:T(8,128)(2,1)S(1)}, bf16[256,512]{1,0:T(8,128)(2,1)}, u32[]{:S(2)}) copy-start(bf16[256,512]{1,0:T(8,128)(2,1)} %w_out.1) | copy-start | bytes 786436
  80.5 72.8 %copy-start.13 = (s32[1,3072]{1,0:T(1,128)}, s32[1,3072]{1,0:T(1,128)S(1)}, u32[]{:S(2)}) copy-start(s32[1,3072]{1,0:T(1,128)S(1)} %get-tuple-element.52.floor) | copy-start | bytes 36868
  153.3 1.1 copy-start.10
  154.5 81.7 %copy-start.7 = (bf16[3072,256]{1,0:T(8,128)(2,1)}, bf16[3072,256]{1,0:T(8,128)(2,1)S(1)}, u32[]{:S(2)}) copy-start(bf16[3072,256]{1,0:T(8,128)(2,1)S(1)} %get-tuple-element.56.attended) | copy-start | bytes 4718596
  154.5 81.7 %copy-start.9 = (bf16[4,256,512]{2,1,0:T(8,128)(2,1)}, bf16[4,256,512]{2,1,0:T(8,128)(2,1)S(1)}, u32[]{:S(2)}) copy-start(bf16[4,256,512]{2,1,0:T(8,128)(2,1)S(1)} %get-tuple-element.57.w_out) | copy-start | bytes 3145732
  154.5 81.7 %copy-start.11 = (bf16[2,1024,256]{2,1,0:T(8,128)(2,1)}, bf16[2,1024,256]{2,1,0:T(8,128)(2,1)S(1)}, u32[]{:S(2)}) copy-start(bf16[2,1024,256]{2,1,0:T(8,128)(2,1)S(1)} %get-tuple-element.54.halo_kv) | copy-start | bytes 3145732
  154.5 81.7 %copy-start.12 = (f32[2,3072]{1,0:T(2,128)}, f32[2,3072]{1,0:T(2,128)S(1)}, u32[]{:S(2)}) copy-start(f32[2,3072]{1,0:T(2,128)S(1)} %get-tuple-element.55.logs) | copy-start | bytes 73732
  236.2 1.0 copy-start.8
  552.5 113.6 %copy-start.15 = (f32[512,688]{1,0:T(8,128)S(1)}, f32[512,688]{1,0:T(8,128)}, u32[]{:S(2)}) copy-start(f32[512,688]{1,0:T(8,128)} %get-tuple-element.99) | copy-start | bytes 4227076
  667.7 5.8 copy-start.14
  673.5 1.7 copy-start.20
  673.5 2.5 copy-start.19
  673.6 3.3 copy-start.18
  675.2 2.4 copy-start.17
  675.2 3.2 copy-start.16

commit v4 on v3

--- a/solution.py
+++ b/solution.py
@@ -504,189 +504,12 @@
     return starts
 
 
-def turned_over(source, target):
-    width = source.shape[1]
-    for start in range(0, width, 128):
-        stop = min(start + 128, width)
-        target[start:stop, :] = source[:, start:stop].T
-
-
-def project_kernel(
-    line,
-    tokens,
-    gain,
-    wq,
-    wk,
-    wv,
-    segment,
-    w_gate,
-    w_up,
-    normed_out,
-    qkv_out,
-    weight_out,
-    floor_out,
-    gate_out,
-    up_out,
-    normed,
-    weight,
-    g_send,
-    g_recv,
-    us,
-    ur,
-    ds,
-    dr,
-    keep,
-    seg_halo,
-    seg_sems,
-):
-    p = Place(line)
-    rows, width = tokens.shape
-    slab, part = wq.shape
-    count = segment.shape[1]
-    seg_copy = remote(
-        segment.at[:, pl.ds(count - WINDOW, WINDOW)],
-        seg_halo,
-        seg_sems.at[0],
-        seg_sems.at[1],
-        (p.s + 1, p.h),
-    )
-    weight_own = weight.at[pl.ds(pl.multiple_of(p.s * slab, slab), slab)]
-    weight_own[:, 0:part] = wq[...]
-    weight_own[:, part : 2 * part] = wk[...]
-    weight_own[:, 2 * part : 3 * part] = wv[...]
-    block = lambda j: normed.at[pl.ds(pl.multiple_of(j * rows, rows), rows)]
-    home = lambda j: normed_out.at[pl.ds(pl.multiple_of(j * rows, rows), rows)]
-    piece = lambda d: weight.at[pl.ds(pl.multiple_of(d * slab, slab), slab)]
-    gather = HeadGather(p, block, g_send, g_recv)
-    line_gather = LineGather(p, piece, us, ur, ds, dr)
-    p.greet()
-    line_gather.start(0)
-
-    @pl.when(p.s < line - 1)
-    def _():
-        seg_copy.start()
-
-    mine = block(p.h)
-    step = 32
-
-    @pl.loop(0, rows // step)
-    def _(i):
-        at = pl.ds(pl.multiple_of(i * step, step), step)
-        mine[at] = norm_rows(tokens[at].astype(F32), gain[...]).astype(BF16)
-
-    gather.start()
-
-    def multiply(j):
-        start = pl.multiple_of(j * rows, rows)
-
-        @pl.loop(0, 3)
-        def _(n):
-            cols = pl.ds(pl.multiple_of(n * part, part), part)
-            qkv_out[pl.ds(start, rows), cols] = jnp.dot(
-                normed[pl.ds(start, rows), :], weight[:, cols], preferred_element_type=F32
-            ).astype(BF16)
-
-    saved = []
-
-    def save(j):
-        copy = pltpu.make_async_copy(block(j), home(j), keep.at[len(saved)])
-        copy.start()
-        saved.append(copy)
-
-    save(p.h)
-    starts = own_starts(segment)
-    for source, target in ((w_gate, gate_out), (w_up, up_out)):
-        turned_over(source, target)
-
-    @pl.when(p.s > 0)
-    def _():
-        seg_copy.wait_recv()
-
-    before = jnp.sum(
-        (seg_halo[...] == segment[:, 0:1]).astype(jnp.int32), axis=1, keepdims=True
-    )
-    before = jnp.where(p.s > 0, before, 0)
-    floor_out[...] = jnp.maximum(
-        lax.broadcasted_iota(jnp.int32, (1, count), 1),
-        jnp.where(starts >= 0, starts + WINDOW, WINDOW - before),
-    )
-    gather.got_core()
-    save(p.core)
-    line_gather.step(0)
-    gather.got_first()
-    gather.got_second()
-    save(p.first)
-    save(p.second)
-    line_gather.step(1)
-    gather.got_core_second()
-    gather.got_core_first()
-    save(p.second + p.turn)
-    save(p.first + p.turn)
-    line_gather.step(2)
-    out_copy = pltpu.make_async_copy(weight, weight_out, keep.at[8])
-    out_copy.start()
-    for j in (p.h, p.core, p.first, p.second):
-        multiply(j)
-    gather.got_across()
-    save(p.across)
-    for j in (p.second + p.turn, p.first + p.turn, p.across):
-        multiply(j)
-    gather.got_core_across()
-    save(p.across + p.turn)
-    multiply(p.across + p.turn)
-    gather.finish()
-    line_gather.finish()
-
-    @pl.when(p.s < line - 1)
-    def _():
-        seg_copy.wait_send()
-
-    for copy in saved:
-        copy.wait()
-    out_copy.wait()
-
-
 def any_spec():
     return pl.BlockSpec(memory_space=pl.ANY)
 
 
 def vmem_spec():
     return pl.BlockSpec(memory_space=pltpu.VMEM)
-
-
-def project(line, tokens, gain, wq, wk, wv, segment, w_gate, w_up):
-    rows, width = tokens.shape
-    slab, part = wq.shape
-    full = rows * 8
-    return pl.pallas_call(
-        functools.partial(project_kernel, line),
-        out_shape=(
-            jax.ShapeDtypeStruct((full, width), BF16),
-            jax.ShapeDtypeStruct((full, 3 * part), BF16),
-            jax.ShapeDtypeStruct((slab * line, 3 * part), BF16),
-            jax.ShapeDtypeStruct((1, full), jnp.int32),
-            jax.ShapeDtypeStruct((w_gate.shape[1], slab), BF16),
-            jax.ShapeDtypeStruct((w_gate.shape[1], slab), BF16),
-        ),
-        in_specs=[vmem_spec()] * 8,
-        out_specs=(any_spec(), vmem_spec(), any_spec(), vmem_spec(), vmem_spec(), vmem_spec()),
-        scratch_shapes=[
-            pltpu.VMEM((full, width), BF16),
-            pltpu.VMEM((slab * line, 3 * part), BF16),
-            pltpu.SemaphoreType.DMA((7,)),
-            pltpu.SemaphoreType.DMA((7,)),
-            *line_sems(line),
-            pltpu.SemaphoreType.DMA((9,)),
-            pltpu.VMEM((1, WINDOW), jnp.int32),
-            pltpu.SemaphoreType.DMA((2,)),
-        ],
-        compiler_params=pltpu.CompilerParams(
-            collective_id=1, has_side_effects=True, vmem_limit_bytes=48 * MIB
-        ),
-        cost_estimate=pl.CostEstimate(
-            flops=2 * full * width * 3 * part, bytes_accessed=40 * MIB, transcendentals=0
-        ),
-    )(tokens, gain.reshape(1, width), wq, wk, wv, segment.reshape(1, full), w_gate, w_up)
 
 
 LOG2E = 1.4426950408889634
@@ -736,37 +559,83 @@
         logs[head : head + 1, pl.ds(start, TILE)] = highest * sharp + jnp.log2(total)
 
 
-def attend_kernel(
+def block_reduce(place, out, into, r_send, r_recv):
+    p = place
+    goes = (p.core, p.core, p.core, p.core, p.first, p.first, p.second)
+    slots = (0, 1, 0, 1, 2, 3, 4)
+    return [
+        remote(out.at[slots[i]], into.at[i], r_send.at[i], r_recv.at[i], p.at(to))
+        for i, to in enumerate(goes)
+    ]
+
+
+def forward_kernel(
     line,
-    qkv,
-    floor,
+    tokens,
+    gain,
+    wq,
+    wk,
+    wv,
+    segment,
     cot,
     w_out,
-    gate_a,
+    w_gate,
+    w_up,
+    normed_out,
+    qkv_out,
+    weight_out,
+    floor,
     attended,
     logs,
     halo_out,
     cot_out,
-    w_out_full,
+    w_out_out,
     gate_full,
+    up_full,
+    middle,
+    normed,
+    weight,
     q,
     k_ext,
     v_ext,
     v_t,
+    w_out_full,
+    seg_halo,
+    out,
+    into,
     g_send,
     g_recv,
+    c_send,
+    c_recv,
+    r_send,
+    r_recv,
+    halo_send,
+    halo_recv,
+    seg_sems,
+    keep,
     *sems,
 ):
     p = Place(line)
-    out_sems, gate_sems, halo_send, halo_recv, keep = sems[0:4], sems[4:8], *sems[8:11]
-    rows = cot.shape[0]
-    count, part = q.shape
-    p.greet()
-    block = lambda j: cot_out.at[pl.ds(pl.multiple_of(j * rows, rows), rows)]
-    gather = HeadGather(p, block, g_send, g_recv, own=cot)
+    qkv_sems, out_sems, gate_sems, up_sems = sems[0:4], sems[4:8], sems[8:12], sems[12:16]
+    rows, width = tokens.shape
+    slab, part = wq.shape
+    count = segment.shape[1]
+    rows_of = lambda ref, j: ref.at[pl.ds(pl.multiple_of(j * rows, rows), rows)]
+    slab_of = lambda d: weight.at[pl.ds(pl.multiple_of(d * slab, slab), slab)]
+    weight_own = slab_of(p.s)
+    weight_own[:, 0:part] = wq[...]
+    weight_own[:, part : 2 * part] = wk[...]
+    weight_own[:, 2 * part : 3 * part] = wv[...]
+    seg_copy = remote(
+        segment.at[:, pl.ds(count - WINDOW, WINDOW)],
+        seg_halo,
+        seg_sems.at[0],
+        seg_sems.at[1],
+        (p.s + 1, p.h),
+    )
     halo = [
         remote(
-            qkv.at[pl.ds(count - WINDOW, WINDOW), pl.ds((1 + i) * part, part)],
+            ext.at[pl.ds(count, WINDOW)],
             ext.at[pl.ds(0, WINDOW)],
             halo_send.at[i],
             halo_recv.at[i],
@@ -774,42 +643,107 @@
         )
         for i, ext in enumerate((k_ext, v_ext))
     ]
+    gather = HeadGather(p, lambda j: rows_of(normed, j), g_send, g_recv)
+    cot_gather = HeadGather(p, lambda j: rows_of(cot_out, j), c_send, c_recv, own=cot)
+    qkv_gather = LineGather(p, slab_of, *qkv_sems)
+    out_gather = LineGather(p, lambda d: w_out_full.at[d], *out_sems, own=w_out)
+    gate_gather = LineGather(p, lambda d: gate_full.at[d], *gate_sems, own=w_gate)
+    up_gather = LineGather(p, lambda d: up_full.at[d], *up_sems, own=w_up)
+    p.greet()
+    qkv_gather.start(0)
+
+    @pl.when(p.s < line - 1)
+    def _():
+        seg_copy.start()
+
+    mine = rows_of(normed, p.h)
+    step = 32
+
+    @pl.loop(0, rows // step)
+    def _(i):
+        at = pl.ds(pl.multiple_of(i * step, step), step)
+        mine[at] = norm_rows(tokens[at].astype(F32), gain[...]).astype(BF16)
+
+    gather.start()
+    saved = []
+
+    def save(source, target):
+        copy = pltpu.make_async_copy(source, target, keep.at[len(saved)])
+        copy.start()
+        saved.append(copy)
+
+    def save_block(j):
+        save(rows_of(normed, j), rows_of(normed_out, j))
+
+    save_block(p.h)
+    save(cot, rows_of(cot_out, p.h))
+    save(w_out, w_out_full.at[p.s])
+    own_w_out = saved[-1]
+    save(w_gate, gate_full.at[p.s])
+    save(w_up, up_full.at[p.s])
+    starts = own_starts(segment)
+
+    @pl.when(p.s == 0)
+    def _():
+        k_ext[0:WINDOW, :] = jnp.zeros((WINDOW, part), BF16)
+        v_ext[0:WINDOW, :] = jnp.zeros((WINDOW, part), BF16)
+
+    @pl.when(p.s > 0)
+    def _():
+        seg_copy.wait_recv()
+
+    before = jnp.sum(
+        (seg_halo[...] == segment[:, 0:1]).astype(jnp.int32), axis=1, keepdims=True
+    )
+    before = jnp.where(p.s > 0, before, 0)
+    floor[...] = jnp.maximum(
+        lax.broadcasted_iota(jnp.int32, (1, count), 1),
+        jnp.where(starts >= 0, starts + WINDOW, WINDOW - before),
+    )
+    gather.got_core()
+    save_block(p.core)
+    qkv_gather.step(0)
+    gather.got_first()
+    gather.got_second()
+    cot_gather.start()
+    save_block(p.first)
+    save_block(p.second)
+    qkv_gather.step(1)
+    out_gather.start(0)
+    gather.got_core_second()
+    gather.got_core_first()
+    save_block(p.second + p.turn)
+    save_block(p.first + p.turn)
+    qkv_gather.step(2)
+    gather.got_across()
+    save_block(p.across)
+    gather.got_core_across()
+    save_block(p.across + p.turn)
+    save(weight, weight_out)
+
+    def multiply(first, last):
+        @pl.loop(first, last)
+        def _(n):
+            start = pl.multiple_of((count // rows - 1 - n) * rows, rows)
+            value = product(normed[pl.ds(start, rows), :], weight[...]).astype(BF16)
+            q[pl.ds(start, rows), :] = value[:, 0:part]
+            k_ext[pl.ds(start + WINDOW, rows), :] = value[:, part : 2 * part]
+            v_ext[pl.ds(start + WINDOW, rows), :] = value[:, 2 * part : 3 * part]
+
+    late = (WINDOW + rows - 1) // rows
+    multiply(0, late)
 
     @pl.when(p.s < line - 1)
     def _():
         halo[0].start()
         halo[1].start()
 
-    gather.start()
-    loads = [
-        pltpu.make_async_copy(qkv.at[:, pl.ds(0, part)], q, keep.at[0]),
-        pltpu.make_async_copy(
-            qkv.at[:, pl.ds(part, part)], k_ext.at[pl.ds(WINDOW, count)], keep.at[1]
-        ),
-        pltpu.make_async_copy(
-            qkv.at[:, pl.ds(2 * part, part)], v_ext.at[pl.ds(WINDOW, count)], keep.at[2]
-        ),
-    ]
-    for copy in loads:
-        copy.start()
-    out_gather = LineGather(p, lambda d: w_out_full.at[d], *out_sems, own=w_out)
-    gate_gather = LineGather(p, lambda d: gate_full.at[d], *gate_sems, own=gate_a)
-    out_gather.start(0)
-    own = [
-        pltpu.make_async_copy(cot, block(p.h), keep.at[3]),
-        pltpu.make_async_copy(w_out, w_out_full.at[p.s], keep.at[4]),
-        pltpu.make_async_copy(gate_a, gate_full.at[p.s], keep.at[5]),
-    ]
-    for copy in own:
-        copy.start()
-
-    @pl.when(p.s == 0)
-    def _():
-        k_ext[0:WINDOW, :] = jnp.zeros((WINDOW, part), BF16)
-        v_ext[0:WINDOW, :] = jnp.zeros((WINDOW, part), BF16)
-
-    for copy in loads:
-        copy.wait()
+    out_gather.step(0)
+    gate_gather.start(0)
+    multiply(late, count // rows)
+    save(q, qkv_out.at[:, pl.ds(0, part)])
+    save(k_ext.at[pl.ds(WINDOW, count)], qkv_out.at[:, pl.ds(part, part)])
+    save(v_ext.at[pl.ds(WINDOW, count)], qkv_out.at[:, pl.ds(2 * part, part)])
 
     def turn(first, last):
         @pl.loop(first, last)
@@ -824,9 +758,17 @@
 
     ahead = WINDOW // TILE
     turn(ahead, ahead + count // TILE)
-    tiles(ahead, count // TILE)
-    out_gather.step(0)
-    gate_gather.start(0)
+    tiles(ahead, ahead + 1)
+    out_gather.step(1)
+    up_gather.start(0)
+    tiles(ahead + 1, ahead + 4)
+    cot_gather.got_core()
+    cot_gather.got_first()
+    cot_gather.got_second()
+    tiles(ahead + 4, ahead + 5)
+    out_gather.step(2)
+    tiles(ahead + 5, count // TILE)
+    gate_gather.step(0)
 
     @pl.when(p.s > 0)
     def _():
@@ -834,139 +776,17 @@
         halo[1].wait_recv()
 
     turn(0, ahead)
-    tiles(0, ahead)
-    saves = [
-        pltpu.make_async_copy(ext.at[pl.ds(0, WINDOW)], halo_out.at[i], keep.at[6 + i])
-        for i, ext in enumerate((k_ext, v_ext))
-    ]
-    for copy in saves:
-        copy.start()
-    out_gather.step(1)
-    gate_gather.step(0)
-    gather.got_core()
-    gather.got_first()
-    gather.got_second()
-    gather.got_core_second()
-    gather.got_core_first()
-    out_gather.step(2)
-    gate_gather.step(1)
-    gather.got_across()
-    gather.got_core_across()
-    gate_gather.step(2)
-    gather.finish()
-    out_gather.finish()
-    gate_gather.finish()
-
-    @pl.when(p.s < line - 1)
-    def _():
-        halo[0].wait_send()
-        halo[1].wait_send()
-
-    for copy in own + saves:
-        copy.wait()
-
-
-def attend(line, qkv, floor, cot, w_out, gate_a):
-    count = qkv.shape[0]
-    part = qkv.shape[1] // 3
-    heads = part // HEAD_DIM
-    rows, width = cot.shape
-    return pl.pallas_call(
-        functools.partial(attend_kernel, line),
-        out_shape=(
-            jax.ShapeDtypeStruct((count, part), BF16),
-            jax.ShapeDtypeStruct((heads, count), F32),
-            jax.ShapeDtypeStruct((2, WINDOW, part), BF16),
-            jax.ShapeDtypeStruct((rows * 8, width), BF16),
-            jax.ShapeDtypeStruct((line, *w_out.shape), BF16),
-            jax.ShapeDtypeStruct((line, *gate_a.shape), BF16),
-        ),
-        in_specs=[any_spec(), vmem_spec(), any_spec(), any_spec(), any_spec()],
-        out_specs=(vmem_spec(), vmem_spec(), any_spec(), any_spec(), any_spec(), any_spec()),
-        scratch_shapes=[
-            pltpu.VMEM((count, part), BF16),
-            pltpu.VMEM((WINDOW + count, part), BF16),
-            pltpu.VMEM((WINDOW + count, part), BF16),
-            pltpu.VMEM((part, WINDOW + count), BF16),
-            pltpu.SemaphoreType.DMA((7,)),
-            pltpu.SemaphoreType.DMA((7,)),
-            *line_sems(line, 2),
-            pltpu.SemaphoreType.DMA((2,)),
-            pltpu.SemaphoreType.DMA((2,)),
-            pltpu.SemaphoreType.DMA((8,)),
-        ],
-        compiler_params=pltpu.CompilerParams(
-            collective_id=2, has_side_effects=True, vmem_limit_bytes=48 * MIB
-        ),
-        cost_estimate=pl.CostEstimate(
-            flops=5 * 2**31, bytes_accessed=40 * MIB, transcendentals=0
-        ),
-    )(qkv, floor, cot, w_out, gate_a)
-
-
-class HeadReduce:
-    def __init__(self, place, out, into, send, recv):
-        p = place
-        self.p, self.out, self.into = p, out, into
-        goes = (p.core, p.core, p.core, p.core, p.first, p.first, p.second)
-        self.copies = [
-            remote(out.at[i], into.at[i], send.at[i], recv.at[i], p.at(to))
-            for i, to in enumerate(goes)
-        ]
-        self.for_core = (p.second + p.turn, p.across + p.turn, p.first + p.turn, p.core)
-        self.mine = (p.first, p.across, p.second, p.h)
-
-    def send(self, i):
-        self.copies[i].start()
-
-    def got(self, i):
-        self.copies[i].wait_recv()
-
-    def finish(self):
-        for copy in self.copies:
-            copy.wait_send()
-
-
-def reduce_scratch(rows, width):
-    return [
-        pltpu.VMEM((7, rows, width), BF16),
-        pltpu.VMEM((7, rows, width), BF16),
-        pltpu.SemaphoreType.DMA((7,)),
-        pltpu.SemaphoreType.DMA((7,)),
-    ]
-
-
-def branch_kernel(
-    line,
-    attended,
-    w_out,
-    tokens,
-    gate_b,
-    up,
-    middle,
-    gate_full,
-    up_full,
-    out,
-    into,
-    r_send,
-    r_recv,
-    *sems,
-):
-    p = Place(line)
-    gate_sems, up_sems, keep = sems[0:4], sems[4:8], sems[8]
-    rows, width = tokens.shape
-    slab = w_out.shape[2]
-    p.greet()
-    gate_gather = LineGather(p, lambda d: gate_full.at[d], *gate_sems, own=gate_b)
-    up_gather = LineGather(p, lambda d: up_full.at[d], *up_sems, own=up)
-    gate_gather.start(0)
-    own = [
-        pltpu.make_async_copy(gate_b, gate_full.at[p.s], keep.at[0]),
-        pltpu.make_async_copy(up, up_full.at[p.s], keep.at[1]),
-    ]
-    for copy in own:
-        copy.start()
-    reduce = HeadReduce(p, out, into, r_send, r_recv)
+    tiles(0, 2)
+    cot_gather.got_core_second()
+    cot_gather.got_core_first()
+    cot_gather.got_across()
+    tiles(2, ahead)
+    up_gather.step(0)
+    for i, ext in enumerate((k_ext, v_ext)):
+        save(ext.at[pl.ds(0, WINDOW)], halo_out.at[i])
+    own_w_out.wait()
+    save(w_out_full, w_out_out)
+    copies = block_reduce(p, out, into, r_send, r_recv)
 
     def emit(j, target, *more):
         start = pl.multiple_of(j * rows, rows)
@@ -974,69 +794,131 @@
         @pl.loop(0, line)
         def _(n):
             cols = pl.ds(pl.multiple_of(n * slab, slab), slab)
-            value = product(attended[pl.ds(start, rows), :], w_out[n])
+            value = product(attended[pl.ds(start, rows), :], w_out_full[n])
             for other in more:
                 value = value + other[:, cols].astype(F32)
             target[:, cols] = value.astype(target.dtype)
 
-    for i in range(4):
-        emit(reduce.for_core[i], out.at[i])
-        reduce.send(i)
-    for i in range(2):
-        reduce.got(i)
-        emit(reduce.mine[i], out.at[4 + i], into.at[i])
-        reduce.send(4 + i)
-    reduce.got(3)
+    emit(p.second + p.turn, out.at[0])
+    copies[0].start()
+    emit(p.across + p.turn, out.at[1])
+    copies[1].start()
+    copies[0].wait_recv()
+    emit(p.first, out.at[2], into.at[0])
+    copies[4].start()
+    copies[0].wait_send()
+    emit(p.first + p.turn, out.at[0])
+    copies[2].start()
+    copies[1].wait_recv()
+    emit(p.across, out.at[3], into.at[1])
+    copies[5].start()
+    copies[1].wait_send()
+    emit(p.core, out.at[1])
+    copies[3].start()
+    gate_gather.step(1)
+    copies[3].wait_recv()
     emit(p.h, middle, into.at[3], tokens)
-    reduce.got(2)
-    gate_gather.step(0)
-    up_gather.start(0)
-    gate_gather.step(1)
-    reduce.got(5)
-    emit(p.second, out.at[6], into.at[2], into.at[5])
-    reduce.send(6)
+    copies[2].wait_recv()
+    cot_gather.got_core_across()
+    copies[5].wait_recv()
+    emit(p.second, out.at[4], into.at[2], into.at[5])
+    copies[6].start()
+    up_gather.step(1)
     gate_gather.step(2)
-    up_gather.step(0)
-    reduce.got(4)
-    up_gather.step(1)
-    reduce.got(6)
+    copies[4].wait_recv()
+    up_gather.step(2)
+    copies[6].wait_recv()
 
     @pl.loop(0, line)
     def _(n):
         cols = pl.ds(pl.multiple_of(n * slab, slab), slab)
         middle[:, cols] += into[4, :, cols].astype(F32) + into[6, :, cols].astype(F32)
 
-    up_gather.step(2)
-    reduce.finish()
-    gate_gather.finish()
-    up_gather.finish()
-    for copy in own:
-        copy.wait()
-
-
-def branch(line, attended, w_out, tokens, gate_b, up):
+    for i in range(2, 7):
+        copies[i].wait_send()
+    gather.finish()
+    cot_gather.finish()
+    for each in (qkv_gather, out_gather, gate_gather, up_gather):
+        each.finish()
+
+    @pl.when(p.s < line - 1)
+    def _():
+        seg_copy.wait_send()
+        halo[0].wait_send()
+        halo[1].wait_send()
+
+    for copy in saved:
+        if copy is not own_w_out:
+            copy.wait()
+
+
+def forward(line, tokens, gain, wq, wk, wv, segment, cot, w_out, w_gate, w_up):
     rows, width = tokens.shape
+    slab, part = wq.shape
+    full = rows * 8
+    units = w_gate.shape[0]
+    heads = part // HEAD_DIM
     return pl.pallas_call(
-        functools.partial(branch_kernel, line),
+        functools.partial(forward_kernel, line),
         out_shape=(
+            jax.ShapeDtypeStruct((full, width), BF16),
+            jax.ShapeDtypeStruct((full, 3 * part), BF16),
+            jax.ShapeDtypeStruct((width, 3 * part), BF16),
+            jax.ShapeDtypeStruct((1, full), jnp.int32),
+            jax.ShapeDtypeStruct((full, part), BF16),
+            jax.ShapeDtypeStruct((heads, full), F32),
+            jax.ShapeDtypeStruct((2, WINDOW, part), BF16),
+            jax.ShapeDtypeStruct((full, width), BF16),
+            jax.ShapeDtypeStruct((line, part, slab), BF16),
+            jax.ShapeDtypeStruct((line, units, slab), BF16),
+            jax.ShapeDtypeStruct((line, units, slab), BF16),
             jax.ShapeDtypeStruct((rows, width), F32),
-            jax.ShapeDtypeStruct((line, *gate_b.shape), BF16),
-            jax.ShapeDtypeStruct((line, *up.shape), BF16),
         ),
-        in_specs=[vmem_spec(), vmem_spec(), vmem_spec(), any_spec(), any_spec()],
-        out_specs=(vmem_spec(), any_spec(), any_spec()),
+        in_specs=[vmem_spec()] * 10,
+        out_specs=(
+            any_spec(),
+            any_spec(),
+            any_spec(),
+            vmem_spec(),
+            vmem_spec(),
+            vmem_spec(),
+            any_spec(),
+            any_spec(),
+            any_spec(),
+            any_spec(),
+            any_spec(),
+            vmem_spec(),
+        ),
         scratch_shapes=[
-            *reduce_scratch(rows, width),
-            *line_sems(line, 2),
+            pltpu.VMEM((full, width), BF16),
+            pltpu.VMEM((width, 3 * part), BF16),
+            pltpu.VMEM((full, part), BF16),
+            pltpu.VMEM((WINDOW + full, part), BF16),
+            pltpu.VMEM((WINDOW + full, part), BF16),
+            pltpu.VMEM((part, WINDOW + full), BF16),
+            pltpu.VMEM((line, part, slab), BF16),
+            pltpu.VMEM((1, WINDOW), jnp.int32),
+            pltpu.VMEM((5, rows, width), BF16),
+            pltpu.VMEM((7, rows, width), BF16),
+            pltpu.SemaphoreType.DMA((7,)),
+            pltpu.SemaphoreType.DMA((7,)),
+            pltpu.SemaphoreType.DMA((7,)),
+            pltpu.SemaphoreType.DMA((7,)),
+            pltpu.SemaphoreType.DMA((7,)),
+            pltpu.SemaphoreType.DMA((7,)),
             pltpu.SemaphoreType.DMA((2,)),
+            pltpu.SemaphoreType.DMA((2,)),
+            pltpu.SemaphoreType.DMA((2,)),
+            pltpu.SemaphoreType.DMA((19,)),
+            *line_sems(line, 4),
         ],
         compiler_params=pltpu.CompilerParams(
-            collective_id=3, has_side_effects=True, vmem_limit_bytes=48 * MIB
+            collective_id=1, has_side_effects=True, vmem_limit_bytes=62 * MIB
         ),
         cost_estimate=pl.CostEstimate(
-            flops=3 * 2**30, bytes_accessed=40 * MIB, transcendentals=0
+            flops=20 * 2**30, bytes_accessed=100 * MIB, transcendentals=0
         ),
-    )(attended, w_out, tokens, gate_b, up)
+    )(tokens, gain.reshape(1, width), wq, wk, wv, segment.reshape(1, full), cot, w_out, w_gate, w_up)
 
 
 def strips(width, most=256):
@@ -1048,8 +930,7 @@
     middle,
     gain,
     cot,
-    gate_a,
-    gate_b,
+    gate,
     up,
     down,
     normed_out,
@@ -1058,6 +939,7 @@
     grad_up_out,
     grad_out,
     down_out,
+    down_grad,
     normed,
     w_gate,
     w_up,
@@ -1068,6 +950,9 @@
     hidden,
     grad_gate,
     grad_up,
+    down_parts,
+    down_up_in,
+    down_down_in,
     out,
     into,
     r_send,
@@ -1077,11 +962,10 @@
     *sems,
 ):
     p = Place(line)
-    down_sems, loads, saves, stage = sems[0:4], sems[4], sems[5], sems[6]
+    down_sems, sum_sems, loads, saves, stage, strip_sems = sems[0:4], sems[4:8], *sems[8:12]
     rows, width = grad_out.shape
     units = w_down.shape[1]
     slab = w_down.shape[2]
-    cut = gate_a.shape[1]
     block = lambda j: normed.at[pl.ds(pl.multiple_of(j * rows, rows), rows)]
     rows_of = lambda ref, j: ref.at[pl.ds(pl.multiple_of(j * rows, rows), rows)]
     gather = HeadGather(p, block, g_send, g_recv)
@@ -1090,8 +974,7 @@
     down_gather.start(0)
     started = [
         pltpu.make_async_copy(middle, grad_out, loads.at[0]),
-        pltpu.make_async_copy(gate_a, w_gate.at[:, pl.ds(0, cut)], loads.at[1]),
-        pltpu.make_async_copy(gate_b, w_gate.at[:, pl.ds(cut, units - cut)], loads.at[2]),
+        pltpu.make_async_copy(gate, w_gate, loads.at[1]),
         pltpu.make_async_copy(up, w_up, loads.at[3]),
         pltpu.make_async_copy(down, w_down.at[p.s], loads.at[4]),
     ]
@@ -1114,16 +997,40 @@
         copy.start()
         saved.append(copy)
 
-    def open_up(j, slot):
-        rows_in = normed.at[pl.ds(pl.multiple_of(j * rows, rows), rows)]
-        for weight, kept in ((w_gate, gates), (w_up, ups)):
-            for first, last in strips(units):
-                value = product_nt(rows_in[:, 0:slab], weight[0, first:last, :])
+    opened = (
+        p.h,
+        p.core,
+        p.first,
+        p.second + p.turn,
+        p.across + p.turn,
+        p.across,
+        p.first + p.turn,
+        p.second,
+    )
+    hidden_stores = [
+        pltpu.make_async_copy(hidden.at[m % 2], rows_of(hidden_out, j), stage.at[m % 2])
+        for m, j in enumerate(opened)
+    ]
+
+    def open_up(m, slot):
+        start = pl.multiple_of(opened[m] * rows, rows)
+        if m > 1:
+            hidden_stores[m - 2].wait()
+        for first, last in strips(units):
+            found = []
+            for weight in (w_gate, w_up):
+                value = product_nt(normed[pl.ds(start, rows), 0:slab], weight[0, first:last, :])
                 for d in range(1, line):
                     value = value + product_nt(
-                        rows_in[:, d * slab : (d + 1) * slab], weight[d, first:last, :]
+                        normed[pl.ds(start, rows), d * slab : (d + 1) * slab],
+                        weight[d, first:last, :],
                     )
-                kept[slot, :, first:last] = value
+                found.append(value)
+            value, lift = found
+            gates[slot, :, first:last] = value.astype(BF16)
+            ups[slot, :, first:last] = lift.astype(BF16)
+            hidden[m % 2, :, first:last] = (value * jax.nn.sigmoid(value) * lift).astype(BF16)
+        hidden_stores[m].start()
 
     order = (
         p.second + p.turn,
@@ -1140,9 +1047,11 @@
     ]
     stores = [
         [
-            pltpu.make_async_copy(held.at[n % 2], rows_of(home, j), stage.at[3 * (n % 2) + i])
+            pltpu.make_async_copy(
+                held.at[n % 2], rows_of(home, j), stage.at[2 + 2 * (n % 2) + i]
+            )
             for i, (held, home) in enumerate(
-                ((hidden, hidden_out), (grad_gate, grad_gate_out), (grad_up, grad_up_out))
+                ((grad_gate, grad_gate_out), (grad_up, grad_up_out))
             )
         ]
         for n, j in enumerate(order)
@@ -1160,12 +1069,10 @@
                 grad = grad + product_nt(
                     cot_block[:, d * slab : (d + 1) * slab], w_down[d, first:last, :]
                 )
-            gate = gates[slot, :, first:last]
-            lift = ups[slot, :, first:last]
+            gate = gates[slot, :, first:last].astype(F32)
+            lift = ups[slot, :, first:last].astype(F32)
             sigmoid = jax.nn.sigmoid(gate)
-            active = gate * sigmoid
-            hidden[turn, :, first:last] = (active * lift).astype(BF16)
-            grad_up[turn, :, first:last] = (grad * active).astype(BF16)
+            grad_up[turn, :, first:last] = (grad * gate * sigmoid).astype(BF16)
             grad_gate[turn, :, first:last] = (
                 grad * lift * (sigmoid * (1.0 + gate * (1.0 - sigmoid)))
             ).astype(BF16)
@@ -1185,35 +1092,48 @@
                 value = value + other[:, cols].astype(F32)
             target[:, cols] = value.astype(target.dtype)
 
-    goes = (p.core, p.core, p.core, p.core, p.first, p.first, p.second)
-    slots = (0, 1, 0, 1, 2, 3, 4)
-    copies = [
-        remote(out.at[slots[i]], into.at[i], r_send.at[i], r_recv.at[i], p.at(to))
-        for i, to in enumerate(goes)
-    ]
+    copies = block_reduce(p, out, into, r_send, r_recv)
+    down_reduce = LineReduce(
+        p, lambda d: down_parts.at[d], down_up_in, down_down_in, *sum_sems
+    )
+    wide = 256
+    padded = hidden.shape[2]
+    kept = slice(2 * wide, 2 * wide + units)
+    hidden[:, :, units // 128 * 128 :] = jnp.zeros((2, rows, padded - units // 128 * 128), BF16)
+    multiply = lambda *some: weight_product(
+        lambda rows_in: product_tn(normed[:, kept], rows_in),
+        cot,
+        lambda d: down_parts.at[d],
+        lambda k: normed.at[:, pl.ds(pl.multiple_of(k * wide, wide), wide)],
+        wide,
+        strip_sems,
+        p,
+        *some,
+    )
     fetches[0].start()
-    for copy in started[1:4]:
+    for copy in started[1:3]:
         copy.wait()
     save(p.h)
-    open_up(p.h, 0)
+    open_up(0, 0)
     gather.got_core()
     save(p.core)
-    open_up(p.core, 1)
+    open_up(1, 1)
     down_gather.step(0)
     gather.got_first()
     gather.got_second()
     save(p.first)
     save(p.second)
     down_gather.step(1)
-    open_up(p.first, 2)
+    open_up(2, 2)
     gather.got_core_second()
     gather.got_core_first()
     save(p.second + p.turn)
     save(p.first + p.turn)
-    open_up(p.second + p.turn, 3)
+    open_up(3, 3)
+    clear_last(down_reduce)
     down_gather.step(2)
-    started[4].wait()
-    down_save = pltpu.make_async_copy(w_down, down_out, loads.at[5])
+    started[3].wait()
+    down_save = pltpu.make_async_copy(w_down, down_out, loads.at[4])
     down_save.start()
     close(0, 3)
     back(0, out.at[0])
@@ -1226,26 +1146,39 @@
     copies[4].start()
     gather.got_core_across()
     save(p.across + p.turn)
-    open_up(p.across + p.turn, 3)
-    close(2, 3)
+    open_up(4, 2)
+    open_up(5, 3)
+    open_up(6, 4)
+    open_up(7, 5)
+    gather.finish()
+    for copy in saved:
+        copy.wait()
+    for copy in hidden_stores[6:]:
+        copy.wait()
+    fill = pltpu.make_async_copy(hidden_out, normed.at[:, pl.ds(2 * wide, padded)], loads.at[5])
+    fill.start()
+    fill.wait()
+    multiply(0, 1)
+    down_reduce.start(0)
+    close(2, 2)
     back(2, out.at[1])
     copies[1].start()
-    open_up(p.across, 3)
     close(3, 3)
     copies[1].wait_recv()
     back(3, out.at[3], into.at[1])
     copies[5].start()
-    open_up(p.first + p.turn, 3)
-    close(4, 3)
+    multiply(1, line)
+    down_reduce.step(0)
+    close(4, 4)
     copies[0].wait_send()
     back(4, out.at[0])
     copies[2].start()
-    open_up(p.second, 3)
-    close(5, 3)
+    close(5, 5)
     copies[2].wait_recv()
     copies[5].wait_recv()
     back(5, out.at[4], into.at[2], into.at[5])
     copies[6].start()
+    down_reduce.step(1)
     close(6, 1)
     copies[1].wait_send()
     back(6, out.at[1])
@@ -1261,62 +1194,77 @@
         cols = pl.ds(pl.multiple_of(d * slab, slab), slab)
         grad_out[:, cols] += into[4, :, cols].astype(F32) + into[6, :, cols].astype(F32)
 
+    down_reduce.step(2)
+    for first, last in strips(units, 128):
+        down_grad[first:last, :] = down_reduce.total(slice(first, last))
     for i in range(2, 7):
         copies[i].wait_send()
-    gather.finish()
     down_gather.finish()
-    for copy in saved:
-        copy.wait()
+    down_reduce.finish()
     for copy in stores[6] + stores[7]:
         copy.wait()
     down_save.wait()
 
 
-def feed(line, middle, gain, cot, gate_a, gate_b, up, down):
+def feed(line, middle, gain, cot, gate, up, down):
     rows, width = middle.shape
     units, slab = down.shape
     full = rows * 8
+    padded = (units + 127) // 128 * 128
     return pl.pallas_call(
         functools.partial(feed_kernel, line),
         out_shape=(
             jax.ShapeDtypeStruct((full, width), BF16),
-            jax.ShapeDtypeStruct((full, units), BF16),
+            jax.ShapeDtypeStruct((full, padded), BF16),
             jax.ShapeDtypeStruct((full, units), BF16),
             jax.ShapeDtypeStruct((full, units), BF16),
             jax.ShapeDtypeStruct((rows, width), F32),
             jax.ShapeDtypeStruct((line, units, slab), BF16),
+            jax.ShapeDtypeStruct((units, slab), F32),
         ),
-        in_specs=[any_spec(), vmem_spec()] + [any_spec()] * 5,
-        out_specs=(any_spec(), any_spec(), any_spec(), any_spec(), vmem_spec(), any_spec()),
+        in_specs=[any_spec(), vmem_spec()] + [any_spec()] * 4,
+        out_specs=(
+            any_spec(),
+            any_spec(),
+            any_spec(),
+            any_spec(),
+            vmem_spec(),
+            any_spec(),
+            vmem_spec(),
+        ),
         scratch_shapes=[
             pltpu.VMEM((full, width), BF16),
             pltpu.VMEM((line, units, slab), BF16),
             pltpu.VMEM((line, units, slab), BF16),
             pltpu.VMEM((line, units, slab), BF16),
-            pltpu.VMEM((4, rows, units), F32),
-            pltpu.VMEM((4, rows, units), F32),
+            pltpu.VMEM((6, rows, units), BF16),
+            pltpu.VMEM((6, rows, units), BF16),
             pltpu.VMEM((rows, width), BF16),
+            pltpu.VMEM((2, rows, padded), BF16),
             pltpu.VMEM((2, rows, units), BF16),
             pltpu.VMEM((2, rows, units), BF16),
-            pltpu.VMEM((2, rows, units), BF16),
+            pltpu.VMEM((line, units, slab), BF16),
+            pltpu.VMEM((line - 1, units, slab), BF16),
+            pltpu.VMEM((line - 1, units, slab), BF16),
             pltpu.VMEM((5, rows, width), BF16),
             pltpu.VMEM((7, rows, width), BF16),
             pltpu.SemaphoreType.DMA((7,)),
             pltpu.SemaphoreType.DMA((7,)),
             pltpu.SemaphoreType.DMA((7,)),
             pltpu.SemaphoreType.DMA((7,)),
-            *line_sems(line),
+            *line_sems(line, 2),
             pltpu.SemaphoreType.DMA((6,)),
             pltpu.SemaphoreType.DMA((8,)),
             pltpu.SemaphoreType.DMA((7,)),
+            pltpu.SemaphoreType.DMA((2,)),
         ],
         compiler_params=pltpu.CompilerParams(
-            collective_id=4, has_side_effects=True, vmem_limit_bytes=60 * MIB
+            collective_id=2, has_side_effects=True, vmem_limit_bytes=63 * MIB
         ),
         cost_estimate=pl.CostEstimate(
             flops=50 * 2**30, bytes_accessed=80 * MIB, transcendentals=0
         ),
-    )(middle, gain.reshape(1, width), cot, gate_a, gate_b, up, down)
+    )(middle, gain.reshape(1, width), cot, gate, up, down)
 
 
 class LineReduce:
@@ -1428,32 +1376,33 @@
         reduce.down_in[last - 1] = jnp.zeros(reduce.down_in.shape[1:], BF16)
 
 
-def weight_product(turned, source, piece, strip, sems):
-    depth = turned.shape[1]
-    wide = strip.shape[2]
-    slab = piece(0).shape[1]
-    count = source.shape[1] // wide
-    each = slab // wide
+def weight_product(apply, source, piece, strip, wide, sems, place, first, last):
+    each = piece(0).shape[1] // wide
+    begin, end = first * each, last * each
+
+    def slab(n):
+        d = lax.div(n, each)
+        low = place.s < place.line // 2
+        return jnp.where(low, place.line - 1 - d, d)
 
     def fetch(n):
-        cols = pl.ds(pl.multiple_of(n * wide, wide), wide)
+        at = slab(n) * each + lax.rem(n, each)
+        cols = pl.ds(pl.multiple_of(at * wide, wide), wide)
         return pltpu.make_async_copy(
-            source.at[:, cols], strip.at[lax.rem(n, 2)], sems.at[lax.rem(n, 2)]
+            source.at[:, cols], strip(lax.rem(n, 2)), sems.at[lax.rem(n, 2)]
         )
 
-    fetch(0).start()
-
-    @pl.loop(0, count)
+    fetch(begin).start()
+
+    @pl.loop(begin, end)
     def _(n):
-        @pl.when(n + 1 < count)
+        @pl.when(n + 1 < end)
         def _():
             fetch(n + 1).start()
 
         fetch(n).wait()
         cols = pl.ds(pl.multiple_of(lax.rem(n, each) * wide, wide), wide)
-        piece(lax.div(n, each))[:, cols] = product(
-            turned[...], strip[lax.rem(n, 2)]
-        ).astype(BF16)
+        piece(slab(n))[:, cols] = apply(strip(lax.rem(n, 2))[...]).astype(BF16)
 
 
 def turn_rows(source, target):
@@ -1468,36 +1417,28 @@
 
 def return_kernel(
     line,
-    cut,
     grad_normed,
     middle,
     cot_own,
     gain,
     attended,
     w_out,
-    hidden,
     grad_gate,
     grad_up,
-    cot,
     normed,
     grad_middle,
     gain_part,
     grad_attended,
     inner,
-    down_grad,
-    up_low,
-    up_high,
+    up_grad,
     gate_parts,
     out_parts,
     branch,
     units_in,
     turned,
     strip,
-    down_parts,
     up_parts,
     other_parts,
-    down_up_in,
-    down_down_in,
     up_up_in,
     up_down_in,
     att_turned,
@@ -1507,21 +1448,16 @@
     *sems,
 ):
     p = Place(line)
-    down_sems, up_sems, loads, strips_sem, saves = sems[0:4], sems[4:8], *sems[8:11]
+    up_sems, loads, strips_sem, saves = sems[0:4], *sems[4:7]
     rows, width = grad_normed.shape
     slab = w_out.shape[2]
     part = attended.shape[1]
     block = lambda j: branch.at[pl.ds(pl.multiple_of(j * rows, rows), rows)]
     gather = HeadGather(p, block, g_send, g_recv)
-    down_reduce = LineReduce(
-        p, lambda d: down_parts.at[d], down_up_in, down_down_in, *down_sems
-    )
-    up_reduce = LineReduce(
-        p, lambda d: up_parts.at[d, pl.ds(0, cut)], up_up_in, up_down_in, *up_sems
-    )
+    up_reduce = LineReduce(p, lambda d: up_parts.at[d], up_up_in, up_down_in, *up_sems)
     load = [
         pltpu.make_async_copy(source, units_in, loads.at[i])
-        for i, source in enumerate((hidden, grad_up, grad_gate))
+        for i, source in enumerate((grad_up, grad_gate))
     ]
     load[0].start()
     p.greet()
@@ -1542,33 +1478,34 @@
         mine[at] = result.astype(BF16)
 
     gather.start()
-    clear_last(down_reduce)
     clear_last(up_reduce)
+    multiply = lambda parts, *some: weight_product(
+        lambda rows_in: product(turned[...], rows_in),
+        normed,
+        lambda d: parts.at[d],
+        strip.at.__getitem__,
+        strip.shape[2],
+        strips_sem,
+        p,
+        *some,
+    )
     load[0].wait()
     turn_rows(units_in, turned)
     load[1].start()
-    weight_product(turned, cot, lambda d: down_parts.at[d], strip, strips_sem)
-    down_reduce.start(0)
+    multiply(up_parts, 0, 1)
+    up_reduce.start(0)
+    multiply(up_parts, 1, line)
+    gather.got_core()
     load[1].wait()
     turn_rows(units_in, turned)
-    load[2].start()
-    gather.got_core()
-    weight_product(turned, normed, lambda d: up_parts.at[d], strip, strips_sem)
-    up_reduce.start(0)
-    down_reduce.step(0)
+    up_reduce.step(0)
     gather.got_first()
     gather.got_second()
-    save_up = pltpu.make_async_copy(
-        up_parts.at[:, pl.ds(cut, up_parts.shape[1] - cut)], up_high, saves.at[0]
-    )
-    save_up.start()
-    load[2].wait()
-    turn_rows(units_in, turned)
-    weight_product(turned, normed, lambda d: other_parts.at[d], strip, strips_sem)
+    multiply(other_parts, 0, line)
     save_gate = pltpu.make_async_copy(other_parts, gate_parts, saves.at[1])
     save_gate.start()
     turn_rows(attended, att_turned)
-    down_reduce.step(1)
+    up_reduce.step(1)
     gather.got_core_second()
     gather.got_core_first()
     out_sum[...] = jnp.zeros_like(out_sum)
@@ -1593,7 +1530,6 @@
 
     for j in (p.h, p.core, p.first, p.second):
         take(j)
-    up_reduce.step(0)
     for j in (p.second + p.turn, p.first + p.turn):
         take(j)
     gather.got_across()
@@ -1602,48 +1538,40 @@
     take(p.across + p.turn)
     for d in range(line):
         out_parts[d] = out_sum[d].astype(BF16)
-    down_reduce.step(2)
-    for first, last in strips(down_grad.shape[0], 128):
-        down_grad[first:last, :] = down_reduce.total(slice(first, last))
-    up_reduce.step(1)
     up_reduce.step(2)
-    for first, last in strips(cut, 128):
-        up_low[:, first:last] = up_reduce.total(slice(first, last)).T
+    for first, last in strips(up_grad.shape[0], 128):
+        up_grad[first:last, :] = up_reduce.total(slice(first, last))
     gather.finish()
-    down_reduce.finish()
     up_reduce.finish()
-    save_up.wait()
     save_gate.wait()
 
 
-def give_back(line, cut, grad_normed, middle, cot_own, gain, attended, w_out, hidden, grad_gate, grad_up, cot, normed):
+def give_back(
+    line, grad_normed, middle, cot_own, gain, attended, w_out, grad_gate, grad_up, normed
+):
     rows, width = middle.shape
-    full, units = hidden.shape
+    full, units = grad_up.shape
     part = attended.shape[1]
     slab = w_out.shape[2]
     heads = part // HEAD_DIM
     return pl.pallas_call(
-        functools.partial(return_kernel, line, cut),
+        functools.partial(return_kernel, line),
         out_shape=(
             jax.ShapeDtypeStruct((rows, width), F32),
             jax.ShapeDtypeStruct((1, width), F32),
             jax.ShapeDtypeStruct((full, part), BF16),
             jax.ShapeDtypeStruct((heads, full), F32),
             jax.ShapeDtypeStruct((units, slab), F32),
-            jax.ShapeDtypeStruct((slab, cut), F32),
-            jax.ShapeDtypeStruct((line, units - cut, slab), BF16),
             jax.ShapeDtypeStruct((line, units, slab), BF16),
             jax.ShapeDtypeStruct((line, part, slab), BF16),
         ),
-        in_specs=[vmem_spec()] * 6 + [any_spec()] * 5,
+        in_specs=[vmem_spec()] * 6 + [any_spec()] * 3,
         out_specs=(
             vmem_spec(),
             vmem_spec(),
             vmem_spec(),
             vmem_spec(),
             vmem_spec(),
-            vmem_spec(),
-            any_spec(),
             any_spec(),
             vmem_spec(),
         ),
@@ -1654,25 +1582,22 @@
             pltpu.VMEM((2, full, 256), BF16),
             pltpu.VMEM((line, units, slab), BF16),
             pltpu.VMEM((line, units, slab), BF16),
-            pltpu.VMEM((line, units, slab), BF16),
             pltpu.VMEM((line - 1, units, slab), BF16),
             pltpu.VMEM((line - 1, units, slab), BF16),
-            pltpu.VMEM((line - 1, cut, slab), BF16),
-            pltpu.VMEM((line - 1, cut, slab), BF16),
             pltpu.VMEM((part, full), BF16),
             pltpu.VMEM((line, part, slab), F32),
             pltpu.SemaphoreType.DMA((7,)),
             pltpu.SemaphoreType.DMA((7,)),
-            *line_sems(line, 2),
-            pltpu.SemaphoreType.DMA((3,)),
+            *line_sems(line),
+            pltpu.SemaphoreType.DMA((2,)),
             pltpu.SemaphoreType.DMA((2,)),
             pltpu.SemaphoreType.DMA((2,)),
         ],
         compiler_params=pltpu.CompilerParams(
-            collective_id=5, has_side_effects=True, vmem_limit_bytes=62 * MIB
+            collective_id=3, has_side_effects=True, vmem_limit_bytes=62 * MIB
         ),
         cost_estimate=pl.CostEstimate(
-            flops=35 * 2**30, bytes_accessed=80 * MIB, transcendentals=0
+            flops=25 * 2**30, bytes_accessed=80 * MIB, transcendentals=0
         ),
     )(
         grad_normed,
@@ -1681,10 +1606,8 @@
         gain.reshape(1, width),
         attended,
         w_out,
-        hidden,
         grad_gate,
         grad_up,
-        cot,
         normed,
     )
 
@@ -1709,16 +1632,6 @@
             key_sum[at, cols] += product(grad_scores, queries)
             turned = turned + product(k_t[cols, at], grad_scores)
         q[mine, cols] = (turned * scale).astype(BF16).T
-
-
-def block_reduce(place, out, into, r_send, r_recv):
-    p = place
-    goes = (p.core, p.core, p.core, p.core, p.first, p.first, p.second)
-    slots = (0, 1, 0, 1, 2, 3, 4)
-    return [
-        remote(out.at[slots[i]], into.at[i], r_send.at[i], r_recv.at[i], p.at(to))
-        for i, to in enumerate(goes)
-    ]
 
 
 def attend_back_kernel(
@@ -1808,7 +1721,7 @@
         @pl.loop(0, line)
         def _(d):
             cols = pl.ds(pl.multiple_of(d * slab, slab), slab)
-            value = product(hidden_block[n % 2], w_down[d])
+            value = product(hidden_block[n % 2][:, 0 : w_down.shape[1]], w_down[d])
             for other in more:
                 value = value + other[:, cols].astype(F32)
             target[:, cols] = value.astype(target.dtype)
@@ -1845,6 +1758,7 @@
     copies[3].start()
     for copy in started[1:]:
         copy.wait()
+    gate_reduce.step(0)
 
     @pl.loop(0, (WINDOW + count) // TILE)
     def _(i):
@@ -1868,7 +1782,7 @@
         halo[0].start()
         halo[1].start()
 
-    gate_reduce.step(0)
+    gate_reduce.step(1)
     tiles(ahead, ahead + 4)
     copies[3].wait_recv()
     emit(6, total, into.at[3], total)
@@ -1876,7 +1790,6 @@
     copies[5].wait_recv()
     emit(7, out.at[4], into.at[2], into.at[5])
     copies[6].start()
-    gate_reduce.step(1)
     tiles(ahead + 4, last)
 
     @pl.when(p.s < line - 1)
@@ -1923,8 +1836,8 @@
         result[:, cols] = value.astype(BF16)
 
     gate_reduce.step(2)
-    for first, stop in strips(gate_grad.shape[1], 128):
-        gate_grad[:, first:stop] = gate_reduce.total(slice(first, stop)).T
+    for first, stop in strips(gate_grad.shape[0], 128):
+        gate_grad[first:stop, :] = gate_reduce.total(slice(first, stop))
     for i in range(2, 7):
         copies[i].wait_send()
     gate_reduce.finish()
@@ -1948,7 +1861,7 @@
         out_shape=(
             jax.ShapeDtypeStruct((count, 3 * part), BF16),
             jax.ShapeDtypeStruct((rows, width), BF16),
-            jax.ShapeDtypeStruct((slab, units), F32),
+            jax.ShapeDtypeStruct((units, slab), F32),
         ),
         in_specs=[any_spec()] * 2
         + [vmem_spec()] * 4
@@ -1969,7 +1882,7 @@
             pltpu.VMEM((5, rows, width), BF16),
             pltpu.VMEM((7, rows, width), BF16),
             pltpu.VMEM((rows, width), F32),
-            pltpu.VMEM((2, rows, units), BF16),
+            pltpu.VMEM((2, rows, hidden.shape[1]), BF16),
             pltpu.SemaphoreType.DMA((7,)),
             pltpu.SemaphoreType.DMA((7,)),
             *line_sems(line),
@@ -1980,7 +1893,7 @@
             pltpu.SemaphoreType.DMA((3,)),
         ],
         compiler_params=pltpu.CompilerParams(
-            collective_id=6, has_side_effects=True, vmem_limit_bytes=62 * MIB
+            collective_id=4, has_side_effects=True, vmem_limit_bytes=62 * MIB
         ),
         cost_estimate=pl.CostEstimate(
             flops=20 * 2**30, bytes_accessed=60 * MIB, transcendentals=0
@@ -1996,8 +1909,6 @@
     tokens,
     gain,
     grad_middle,
-    up_high,
-    up_low,
     out_given,
     ffn_gain_part,
     input_grad,
@@ -2006,15 +1917,11 @@
     key_grad,
     value_grad,
     out_grad,
-    up_grad,
     turned,
     strip,
     parts,
     parts_up_in,
     parts_down_in,
-    up_parts,
-    up_up_in,
-    up_down_in,
     out_parts,
     out_up_in,
     out_down_in,
@@ -2028,29 +1935,23 @@
     *sems,
 ):
     p = Place(line)
-    part_sems, up_sems, out_sems, gain_sems = sems[0:4], sems[4:8], sems[8:12], sems[12:16]
-    loads, strip_sems, gain_send, gain_recv = sems[16:20]
+    part_sems, out_sems, gain_sems = sems[0:4], sems[4:8], sems[8:12]
+    loads, strip_sems, gain_send, gain_recv = sems[12:16]
     rows, width = tokens.shape
     slab = width // line
     part = query_grad.shape[1]
-    cut = up_low.shape[1]
     part_reduce = LineReduce(p, lambda d: parts.at[d], parts_up_in, parts_down_in, *part_sems)
-    up_reduce = LineReduce(p, lambda d: up_parts.at[d], up_up_in, up_down_in, *up_sems)
     out_reduce = LineReduce(p, lambda d: out_parts.at[d], out_up_in, out_down_in, *out_sems)
     started = [
-        pltpu.make_async_copy(up_high, up_parts, loads.at[0]),
-        pltpu.make_async_copy(out_given, out_parts, loads.at[1]),
-        pltpu.make_async_copy(up_low, up_grad.at[:, pl.ds(0, cut)], loads.at[2]),
-        pltpu.make_async_copy(grad_middle, input_grad, loads.at[3]),
+        pltpu.make_async_copy(out_given, out_parts, loads.at[0]),
+        pltpu.make_async_copy(grad_middle, input_grad, loads.at[1]),
     ]
     for copy in started:
         copy.start()
     p.greet()
     started[0].wait()
-    up_reduce.start(0)
-    started[1].wait()
     out_reduce.start(0)
-    for reduce in (part_reduce, up_reduce, out_reduce):
+    for reduce in (part_reduce, out_reduce):
         clear_last(reduce)
     copies = block_reduce(p, out, into, r_send, r_recv)
 
@@ -2082,29 +1983,35 @@
     emit(p.core, out.at[1])
     copies[3].start()
     turn_rows(grads, turned)
-    up_reduce.step(0)
+    multiply = lambda *some: weight_product(
+        lambda rows_in: product(turned[...], rows_in),
+        normed,
+        lambda d: parts.at[d],
+        strip.at.__getitem__,
+        strip.shape[2],
+        strip_sems,
+        p,
+        *some,
+    )
     out_reduce.step(0)
-    weight_product(turned, normed, lambda d: parts.at[d], strip, strip_sems)
+    multiply(0, 1)
     part_reduce.start(0)
+    multiply(1, line)
+    out_reduce.step(1)
     copies[3].wait_recv()
     emit(p.h, total, into.at[3])
-    up_reduce.step(1)
-    out_reduce.step(1)
+    part_reduce.step(0)
     copies[2].wait_recv()
     copies[5].wait_recv()
     emit(p.second, out.at[4], into.at[2], into.at[5])
     copies[6].start()
-    up_reduce.step(2)
     out_reduce.step(2)
-    part_reduce.step(0)
-    started[2].wait()
-    for first, last in strips(up_parts.shape[1], 128):
-        up_grad[:, cut + first : cut + last] = up_reduce.total(slice(first, last)).T
     for first, last in strips(part, 128):
         out_grad[first:last, :] = out_reduce.total(slice(first, last))
     copies[4].wait_recv()
+    part_reduce.step(1)
     copies[6].wait_recv()
-    started[3].wait()
+    started[1].wait()
     gain_own = gain_line.at[p.s]
     gain_own[...] = jnp.zeros(gain_own.shape, F32)
     gain_own[1:2, :] = ffn_gain_part[...]
@@ -2118,7 +2025,6 @@
         gain_own[0:1, :] += jnp.sum(grad * unit, axis=0, keepdims=True)
         input_grad[at] += norm_back(unit, inverse, gain[...], grad)
 
-    part_reduce.step(1)
     for i, head in enumerate((p.core, p.first, p.second)):
         copy = remote(gain_own, gain_in.at[i], gain_send.at[i], gain_recv.at[i], p.at(head))
         copy.start()
@@ -2141,17 +2047,15 @@
     for i in range(2, 7):
         copies[i].wait_send()
     gain_gather.finish()
-    for reduce in (part_reduce, up_reduce, out_reduce):
+    for reduce in (part_reduce, out_reduce):
         reduce.finish()
 
 
-def finish(line, grads, weight, normed, tokens, gain, grad_middle, up_high, up_low, out_parts, ffn_gain_part):
+def finish(line, grads, weight, normed, tokens, gain, grad_middle, out_parts, ffn_gain_part):
     rows, width = tokens.shape
     full = grads.shape[0]
     part = grads.shape[1] // 3
     slab = width // line
-    rest = up_high.shape[1]
-    units = up_low.shape[1] + rest
     return pl.pallas_call(
         functools.partial(finish_kernel, line),
         out_shape=(
@@ -2161,7 +2065,6 @@
             jax.ShapeDtypeStruct((slab, part), F32),
             jax.ShapeDtypeStruct((slab, part), F32),
             jax.ShapeDtypeStruct((part, slab), F32),
-            jax.ShapeDtypeStruct((slab, units), F32),
         ),
         in_specs=[
             vmem_spec(),
@@ -2171,20 +2074,15 @@
             vmem_spec(),
             any_spec(),
             any_spec(),
-            any_spec(),
-            any_spec(),
             vmem_spec(),
         ],
-        out_specs=(vmem_spec(),) * 7,
+        out_specs=(vmem_spec(),) * 6,
         scratch_shapes=[
             pltpu.VMEM((3 * part, full), BF16),
             pltpu.VMEM((2, full, 256), BF16),
             pltpu.VMEM((line, 3 * part, slab), BF16),
             pltpu.VMEM((line - 1, 3 * part, slab), BF16),
             pltpu.VMEM((line - 1, 3 * part, slab), BF16),
-            pltpu.VMEM((line, rest, slab), BF16),
-            pltpu.VMEM((line - 1, rest, slab), BF16),
-            pltpu.VMEM((line - 1, rest, slab), BF16),
             pltpu.VMEM((line, part, slab), BF16),
             pltpu.VMEM((line - 1, part, slab), BF16),
             pltpu.VMEM((line - 1, part, slab), BF16),
@@ -2195,14 +2093,14 @@
             pltpu.VMEM((3, 8, width), F32),
             pltpu.SemaphoreType.DMA((7,)),
             pltpu.SemaphoreType.DMA((7,)),
-            *line_sems(line, 4),
-            pltpu.SemaphoreType.DMA((4,)),
+            *line_sems(line, 3),
+            pltpu.SemaphoreType.DMA((2,)),
             pltpu.SemaphoreType.DMA((2,)),
             pltpu.SemaphoreType.DMA((3,)),
             pltpu.SemaphoreType.DMA((3,)),
         ],
         compiler_params=pltpu.CompilerParams(
-            collective_id=7, has_side_effects=True, vmem_limit_bytes=62 * MIB
+            collective_id=5, has_side_effects=True, vmem_limit_bytes=62 * MIB
         ),
         cost_estimate=pl.CostEstimate(
             flops=20 * 2**30, bytes_accessed=60 * MIB, transcendentals=0
@@ -2214,11 +2112,42 @@
         tokens,
         gain.reshape(1, width),
         grad_middle,
-        up_high,
-        up_low,
         out_parts,
         ffn_gain_part,
     )
+
+
+def deliver_kernel(count, *refs):
+    sources, targets, held = refs[:count], refs[count : 2 * count], refs[2 * count : 3 * count]
+    sems = refs[3 * count]
+    loads = [
+        pltpu.make_async_copy(source, keep, sems.at[i])
+        for i, (source, keep) in enumerate(zip(sources, held))
+    ]
+    stores = [
+        pltpu.make_async_copy(keep, target, sems.at[count + i])
+        for i, (keep, target) in enumerate(zip(held, targets))
+    ]
+    for copy in loads:
+        copy.start()
+    for load, store in zip(loads, stores):
+        load.wait()
+        store.start()
+    for copy in stores:
+        copy.wait()
+
+
+def deliver(*arrays):
+    count = len(arrays)
+    return pl.pallas_call(
+        functools.partial(deliver_kernel, count),
+        out_shape=tuple(jax.ShapeDtypeStruct(a.shape, a.dtype) for a in arrays),
+        in_specs=[any_spec()] * count,
+        out_specs=(any_spec(),) * count,
+        scratch_shapes=[pltpu.VMEM(a.shape, a.dtype) for a in arrays]
+        + [pltpu.SemaphoreType.DMA((2 * count,))],
+        compiler_params=pltpu.CompilerParams(vmem_limit_bytes=62 * MIB),
+    )(*arrays)
 
 
 def fused(
@@ -2236,7 +2165,20 @@
     cotangent,
 ):
     line = lax.axis_size("seq")
-    normed_one, qkv, w_qkv, floor, gate_t, up_t = project(
+    (
+        normed_one,
+        qkv,
+        w_qkv,
+        floor,
+        attended,
+        logs,
+        halo_kv,
+        cot_full,
+        w_out,
+        w_gate,
+        w_up,
+        middle,
+    ) = forward(
         line,
         tokens,
         attn_gain,
@@ -2244,46 +2186,30 @@
         key_weight,
         value_weight,
         segment,
-        gate_weight,
-        up_weight,
-    )
-    cut = gate_t.shape[0] // 256 * 128 + 128
-    attended, logs, halo_kv, cot_full, w_out, gate_a = attend(
-        line, qkv, floor, cotangent, out_weight, gate_t[:cut]
-    )
-    middle, gate_b, w_up = branch(line, attended, w_out, tokens, gate_t[cut:], up_t)
-    normed_two, hidden, grad_gate, grad_up, grad_normed_two, w_down = feed(
-        line, middle, ffn_gain, cot_full, gate_a, gate_b, w_up, down_weight
-    )
-    (
-        grad_middle,
-        ffn_gain_part,
-        grad_attended,
-        inner,
-        down_grad,
-        up_low,
-        up_high,
-        gate_parts,
-        out_parts,
-    ) = give_back(
+        cotangent,
+        out_weight,
+        gate_weight.T,
+        up_weight.T,
+    )
+    normed_two, hidden, grad_gate, grad_up, grad_normed_two, w_down, down_grad = feed(
+        line, middle, ffn_gain, cot_full, w_gate, w_up, down_weight
+    )
+    grad_middle, ffn_gain_part, grad_attended, inner, up_grad, gate_parts, out_parts = give_back(
         line,
-        cut,
         grad_normed_two,
         middle,
         cotangent,
         ffn_gain,
         attended,
         w_out,
-        hidden,
         grad_gate,
         grad_up,
-        cot_full,
         normed_two,
     )
     grads, result, gate_grad = attend_back(
         line, qkv, halo_kv, floor, logs, grad_attended, inner, hidden, w_down, middle, gate_parts
     )
-    input_grad, gain_sums, query_grad, key_grad, value_grad, out_grad, up_grad = finish(
+    input_grad, gain_sums, query_grad, key_grad, value_grad, out_grad = finish(
         line,
         grads,
         w_qkv,
@@ -2291,10 +2217,29 @@
         tokens,
         attn_gain,
         grad_middle,
-        up_high,
-        up_low,
         out_parts,
         ffn_gain_part,
+    )
+    (
+        result,
+        input_grad,
+        query_grad,
+        key_grad,
+        value_grad,
+        out_grad,
+        gate_grad,
+        up_grad,
+        down_grad,
+    ) = deliver(
+        result,
+        input_grad,
+        query_grad,
+        key_grad,
+        value_grad,
+        out_grad,
+        gate_grad,
+        up_grad,
+        down_grad,
     )
     share = tokens.shape[1] // (line * lax.axis_size("head"))
     place = (lax.axis_index("seq") * lax.axis_size("head") + lax.axis_index("head")) * share
@@ -2308,8 +2253,8 @@
         value_grad,
         out_grad,
         gain_grads[1],
-        gate_grad,
-        up_grad,
+        gate_grad.T,
+        up_grad.T,
         down_grad,
     )
 

time: 688 us -> 632 us (0.919)
  Pallas kernels: 657 us -> 620 us
  local copies, waits for them, and re-layouts: 21.6 us -> 1.28 us
    pallas_call x4 -> x3, Pallas kernels: 329 us -> 286 us  [the longest x1 200 us: forward(): pl.pallas_call(functools.partial(forward_kernel, line), out_shape=(jax.Sh...]
    pallas_call x1, Pallas kernels: 127 us -> 161 us  [feed(): pl.pallas_call(functools.partial(feed_kernel, line), out_shape=(jax.Shape...]
    unnamed x53 -> x0, local copies, waits for them, and re-layouts: 20.3 us -> none
    pallas_call x1, Pallas kernels: 89.1 us -> 73 us  [attend_back(): pl.pallas_call(functools.partial(attend_back_kernel, line), out_shape=(ja...]
    pallas_call x1, Pallas kernels: 112 us -> 101 us  [finish(): pl.pallas_call(functools.partial(finish_kernel, line), out_shape=(jax.Sha...]
where the time goes in v4:
time: 632 us; the launch traced here: 623 us
  Pallas kernels  620 us (98%)
    pallas_call x1, Pallas kernels, forward(): pl.pallas_call(functools.partial(forward_kernel, line), out_shape=(jax.Sh...  200 us
    pallas_call x1, Pallas kernels, feed(): pl.pallas_call(functools.partial(feed_kernel, line), out_shape=(jax.Shape...  161 us
    pallas_call x1, Pallas kernels, finish(): pl.pallas_call(functools.partial(finish_kernel, line), out_shape=(jax.Sha...  101 us
    pallas_call x1, Pallas kernels, give_back(): pl.pallas_call(functools.partial(return_kernel, line), out_shape=(jax.Sha...  77.4 us
    pallas_call x1, Pallas kernels, attend_back(): pl.pallas_call(functools.partial(attend_back_kernel, line), out_shape=(ja...  73 us

profile of v4, /device:TPU:0, one launch (start us, length us, event | category | flops | bytes accessed | tf_op | source)
XLA Modules:
  0.0 622.5 jit_solution(6530429867370151424)
XLA Ops:
  0.6 200.1 %shard_map.203 = (bf16[3072,2048]{1,0:T(8,128)(2,1)}, bf16[3072,768]{1,0:T(8,128)(2,1)}, bf16[2048,768]{1,0:T(8,128)(2,1)}, s32[1,3072]{1,0:T(1,128)}, bf16[3072...) custom-call(bf16[384,2048]{1,0:T(8,128)(2,1)} %tokens.3, ...), custom_call_target="tpu_custom_call" | custom-call | flops 21474836480 | bytes 104857600 | tf_op jit(solution)/shard_map/pallas_call | solution.py:861
  200.7 160.6 %shard_map.204 = (bf16[3072,2048]{1,0:T(8,128)(2,1)}, bf16[3072,768]{1,0:T(8,128)(2,1)}, bf16[3072,688]{1,0:T(8,128)(2,1)}, bf16[3072,688]{1,0:T(8,128)(2,1)}, f...) custom-call(f32[384,2048]{1,0:T(8,128)} %get-tuple-element.59.middle, f32[1,2048]{1,0:T(1,128)} %bitcast.16, ...), custom_call_target="tpu_custom_call" | custom-call | flops 53687091200 | bytes 83886080 | tf_op jit(solution)/shard_map/pallas_call | solution.py:1214
  361.3 77.4 %shard_map.205 = (f32[384,2048]{1,0:T(8,128)}, f32[1,2048]{1,0:T(1,128)}, bf16[3072,256]{1,0:T(8,128)(2,1)}, f32[2,3072]{1,0:T(2,128)}, f32[688,512]{1,0:T(8,128...) custom-call(f32[384,2048]{1,0:T(8,128)} %get-tuple-element.63.grad_normed, ...), custom_call_target="tpu_custom_call" | custom-call | flops 26843545600 | bytes 83886080 | tf_op jit(solution)/shard_map/pallas_call | solution.py:1557
  438.7 73.0 %shard_map.206 = (bf16[3072,768]{1,0:T(8,128)(2,1)}, bf16[384,2048]{1,0:T(8,128)(2,1)}, f32[688,512]{1,0:T(8,128)}) custom-call(bf16[3072,768]{1,0:T(8,128)(2,1)} %get-tuple-element.55.qkv, bf16[2,1024,256]{2,1,0:T(8,128)(2,1)} %get-tuple-element.56.halo_kv, s32[1,3072]{1,0:T(1,128)} %get-tuple-element.57.floor, f32[2,3072]{1,0:T(2,128)} %get-tuple-element.58.logs, ...), custom_call_target="tpu_custom_call" | custom-call | flops 21474836480 | bytes 62914560 | tf_op jit(solution)/shard_map/pallas_call | solution.py:1859
  511.7 100.9 %shard_map.207 = (f32[384,2048]{1,0:T(8,128)}, f32[8,2048]{1,0:T(8,128)}, f32[512,256]{1,0:T(8,128)}, f32[512,256]{1,0:T(8,128)}, f32[512,256]{1,0:T(8,128)}, /*index=5*/f32[256,512]{1,0:T(8,128)}) custom-call(bf16[3072,768]{1,0:T(8,128)(2,1)} %get-tuple-element.75.grads, bf16[2048,768]{1,0:T(8,128)(2,1)} %get-tuple-element.76.weight, ...), custom_call_target="tpu_custom_call" | custom-call | flops 21474836480 | bytes 62914560 | tf_op jit(solution)/shard_map/pallas_call | solution.py:2059
  612.6 8.2 %shard_map.208 = (bf16[384,2048]{1,0:T(8,128)(2,1)}, f32[384,2048]{1,0:T(8,128)}, f32[512,256]{1,0:T(8,128)}, f32[512,256]{1,0:T(8,128)}, f32[512,256]{1,0:T(8,1...) custom-call(bf16[384,2048]{1,0:T(8,128)(2,1)} %get-tuple-element.74.refs_0_, ...), custom_call_target="tpu_custom_call" | custom-call | tf_op jit(solution)/shard_map/pallas_call | solution.py:2142
  620.8 0.8 constant_dynamic-slice_fusion
  621.6 0.5 slice_bitcast_fusion

commit v5 on v4

--- a/solution.py
+++ b/solution.py
@@ -352,6 +352,18 @@
                 pl.semaphore_wait(barrier, 4)
         else:
             pl.semaphore_wait(barrier, 3)
+
+
+def greet_line(place):
+    p = place
+    barrier = pltpu.get_barrier_semaphore()
+    for head in (p.core, p.first, p.second):
+        pl.semaphore_signal(barrier, inc=1, device_id=p.at(head), device_id_type=MESH)
+    for k in range(1, p.line):
+        pl.semaphore_signal(
+            barrier, inc=1, device_id=(lax.rem(p.s + k, p.line), p.h), device_id_type=MESH
+        )
+    pl.semaphore_wait(barrier, 2 + p.line)
 
 
 class HeadGather:
@@ -738,9 +750,10 @@
         halo[0].start()
         halo[1].start()
 
+    multiply(late, count // rows)
+    multiply(late, count // rows)
     out_gather.step(0)
     gate_gather.start(0)
-    multiply(late, count // rows)
     save(q, qkv_out.at[:, pl.ds(0, part)])
     save(k_ext.at[pl.ds(WINDOW, count)], qkv_out.at[:, pl.ds(part, part)])
     save(v_ext.at[pl.ds(WINDOW, count)], qkv_out.at[:, pl.ds(2 * part, part)])
@@ -758,17 +771,13 @@
 
     ahead = WINDOW // TILE
     turn(ahead, ahead + count // TILE)
-    tiles(ahead, ahead + 1)
-    out_gather.step(1)
-    up_gather.start(0)
-    tiles(ahead + 1, ahead + 4)
+    tiles(ahead, ahead + 5)
     cot_gather.got_core()
     cot_gather.got_first()
     cot_gather.got_second()
-    tiles(ahead + 4, ahead + 5)
-    out_gather.step(2)
+    out_gather.step(1)
+    up_gather.start(0)
     tiles(ahead + 5, count // TILE)
-    gate_gather.step(0)
 
     @pl.when(p.s > 0)
     def _():
@@ -780,8 +789,9 @@
     cot_gather.got_core_second()
     cot_gather.got_core_first()
     cot_gather.got_across()
+    gate_gather.step(0)
     tiles(2, ahead)
-    up_gather.step(0)
+    out_gather.step(2)
     for i, ext in enumerate((k_ext, v_ext)):
         save(ext.at[pl.ds(0, WINDOW)], halo_out.at[i])
     own_w_out.wait()
@@ -791,9 +801,8 @@
     def emit(j, target, *more):
         start = pl.multiple_of(j * rows, rows)
 
-        @pl.loop(0, line)
-        def _(n):
-            cols = pl.ds(pl.multiple_of(n * slab, slab), slab)
+        for n in range(line):
+            cols = slice(n * slab, (n + 1) * slab)
             value = product(attended[pl.ds(start, rows), :], w_out_full[n])
             for other in more:
                 value = value + other[:, cols].astype(F32)
@@ -815,15 +824,16 @@
     copies[1].wait_send()
     emit(p.core, out.at[1])
     copies[3].start()
-    gate_gather.step(1)
     copies[3].wait_recv()
     emit(p.h, middle, into.at[3], tokens)
+    up_gather.step(0)
+    gate_gather.step(1)
     copies[2].wait_recv()
     cot_gather.got_core_across()
+    up_gather.step(1)
     copies[5].wait_recv()
     emit(p.second, out.at[4], into.at[2], into.at[5])
     copies[6].start()
-    up_gather.step(1)
     gate_gather.step(2)
     copies[4].wait_recv()
     up_gather.step(2)
@@ -921,6 +931,10 @@
     )(tokens, gain.reshape(1, width), wq, wk, wv, segment.reshape(1, full), cot, w_out, w_gate, w_up)
 
 
+def sigmoid_of(value):
+    return 0.5 * jnp.tanh(0.5 * value) + 0.5
+
+
 def strips(width, most=256):
     return [(start, min(start + most, width)) for start in range(0, width, most)]
 
@@ -1002,10 +1016,10 @@
         p.core,
         p.first,
         p.second + p.turn,
+        p.first + p.turn,
+        p.second,
         p.across + p.turn,
         p.across,
-        p.first + p.turn,
-        p.second,
     )
     hidden_stores = [
         pltpu.make_async_copy(hidden.at[m % 2], rows_of(hidden_out, j), stage.at[m % 2])
@@ -1029,7 +1043,7 @@
             value, lift = found
             gates[slot, :, first:last] = value.astype(BF16)
             ups[slot, :, first:last] = lift.astype(BF16)
-            hidden[m % 2, :, first:last] = (value * jax.nn.sigmoid(value) * lift).astype(BF16)
+            hidden[m % 2, :, first:last] = (value * sigmoid_of(value) * lift).astype(BF16)
         hidden_stores[m].start()
 
     order = (
@@ -1071,7 +1085,7 @@
                 )
             gate = gates[slot, :, first:last].astype(F32)
             lift = ups[slot, :, first:last].astype(F32)
-            sigmoid = jax.nn.sigmoid(gate)
+            sigmoid = sigmoid_of(gate)
             grad_up[turn, :, first:last] = (grad * gate * sigmoid).astype(BF16)
             grad_gate[turn, :, first:last] = (
                 grad * lift * (sigmoid * (1.0 + gate * (1.0 - sigmoid)))
@@ -1084,9 +1098,8 @@
     def back(n, target, *more):
         turn = n % 2
 
-        @pl.loop(0, line)
-        def _(d):
-            cols = pl.ds(pl.multiple_of(d * slab, slab), slab)
+        for d in range(line):
+            cols = slice(d * slab, (d + 1) * slab)
             value = product(grad_gate[turn], w_gate[d]) + product(grad_up[turn], w_up[d])
             for other in more:
                 value = value + other[:, cols].astype(F32)
@@ -1096,7 +1109,7 @@
     down_reduce = LineReduce(
         p, lambda d: down_parts.at[d], down_up_in, down_down_in, *sum_sems
     )
-    wide = 256
+    wide = slab
     padded = hidden.shape[2]
     kept = slice(2 * wide, 2 * wide + units)
     hidden[:, :, units // 128 * 128 :] = jnp.zeros((2, rows, padded - units // 128 * 128), BF16)
@@ -1130,6 +1143,8 @@
     save(p.second + p.turn)
     save(p.first + p.turn)
     open_up(3, 3)
+    open_up(4, 4)
+    open_up(5, 5)
     clear_last(down_reduce)
     down_gather.step(2)
     started[3].wait()
@@ -1146,10 +1161,8 @@
     copies[4].start()
     gather.got_core_across()
     save(p.across + p.turn)
-    open_up(4, 2)
-    open_up(5, 3)
-    open_up(6, 4)
-    open_up(7, 5)
+    open_up(6, 2)
+    open_up(7, 3)
     gather.finish()
     for copy in saved:
         copy.wait()
@@ -1160,6 +1173,7 @@
     fill.wait()
     multiply(0, 1)
     down_reduce.start(0)
+    multiply(1, 2)
     close(2, 2)
     back(2, out.at[1])
     copies[1].start()
@@ -1167,8 +1181,8 @@
     copies[1].wait_recv()
     back(3, out.at[3], into.at[1])
     copies[5].start()
-    multiply(1, line)
     down_reduce.step(0)
+    multiply(2, line)
     close(4, 4)
     copies[0].wait_send()
     back(4, out.at[0])
@@ -1417,16 +1431,16 @@
 
 def return_kernel(
     line,
-    grad_normed,
-    middle,
-    cot_own,
+    grad_given,
+    middle_given,
+    cot_given,
     gain,
-    attended,
-    w_out,
+    attended_given,
+    w_out_given,
     grad_gate,
     grad_up,
     normed,
-    grad_middle,
+    grad_middle_out,
     gain_part,
     grad_attended,
     inner,
@@ -1435,7 +1449,6 @@
     out_parts,
     branch,
     units_in,
-    turned,
     strip,
     up_parts,
     other_parts,
@@ -1443,12 +1456,18 @@
     up_down_in,
     att_turned,
     out_sum,
+    grad_normed,
+    middle,
+    cot_own,
+    attended,
+    w_out,
+    grad_middle,
     g_send,
     g_recv,
     *sems,
 ):
     p = Place(line)
-    up_sems, loads, strips_sem, saves = sems[0:4], *sems[4:7]
+    up_sems, loads, strips_sem, saves, early, kept = sems[0:4], *sems[4:9]
     rows, width = grad_normed.shape
     slab = w_out.shape[2]
     part = attended.shape[1]
@@ -1459,15 +1478,39 @@
         pltpu.make_async_copy(source, units_in, loads.at[i])
         for i, source in enumerate((grad_up, grad_gate))
     ]
+    pieces = 4
+    piece_rows = rows // pieces
+    piece_at = [pl.ds(i * piece_rows, piece_rows) for i in range(pieces)]
+    arriving = [
+        [
+            pltpu.make_async_copy(source.at[at], target.at[at], early.at[3 * i + k])
+            for k, (source, target) in enumerate(
+                ((grad_given, grad_normed), (middle_given, middle), (cot_given, cot_own))
+            )
+        ]
+        for i, at in enumerate(piece_at)
+    ]
+    leaving = [
+        pltpu.make_async_copy(grad_middle.at[at], grad_middle_out.at[at], kept.at[i])
+        for i, at in enumerate(piece_at)
+    ]
+    later = [
+        pltpu.make_async_copy(attended_given, attended, early.at[3 * pieces]),
+        pltpu.make_async_copy(w_out_given, w_out, early.at[3 * pieces + 1]),
+    ]
+    for group in arriving:
+        for copy in group:
+            copy.start()
     load[0].start()
+    for copy in later:
+        copy.start()
     p.greet()
     mine = block(p.h)
     gain_part[...] = jnp.zeros_like(gain_part)
     step = 32
 
-    @pl.loop(0, rows // step)
-    def _(i):
-        at = pl.ds(pl.multiple_of(i * step, step), step)
+    def piece_back(number, i):
+        at = pl.ds(pl.multiple_of(number * piece_rows + i * step, step), step)
         value = middle[at]
         inverse = lax.rsqrt(jnp.mean(value * value, axis=-1, keepdims=True) + EPS)
         unit = value * inverse
@@ -1477,10 +1520,16 @@
         grad_middle[at] = result
         mine[at] = result.astype(BF16)
 
+    for number in range(pieces):
+        for copy in arriving[number]:
+            copy.wait()
+        pl.loop(0, piece_rows // step)(functools.partial(piece_back, number))
+        leaving[number].start()
+
     gather.start()
     clear_last(up_reduce)
     multiply = lambda parts, *some: weight_product(
-        lambda rows_in: product(turned[...], rows_in),
+        lambda rows_in: product_tn(units_in[...], rows_in),
         normed,
         lambda d: parts.at[d],
         strip.at.__getitem__,
@@ -1490,20 +1539,20 @@
         *some,
     )
     load[0].wait()
-    turn_rows(units_in, turned)
-    load[1].start()
     multiply(up_parts, 0, 1)
     up_reduce.start(0)
     multiply(up_parts, 1, line)
+    load[1].start()
     gather.got_core()
     load[1].wait()
-    turn_rows(units_in, turned)
     up_reduce.step(0)
     gather.got_first()
     gather.got_second()
     multiply(other_parts, 0, line)
     save_gate = pltpu.make_async_copy(other_parts, gate_parts, saves.at[1])
     save_gate.start()
+    for copy in later:
+        copy.wait()
     turn_rows(attended, att_turned)
     up_reduce.step(1)
     gather.got_core_second()
@@ -1544,6 +1593,8 @@
     gather.finish()
     up_reduce.finish()
     save_gate.wait()
+    for copy in leaving:
+        copy.wait()
 
 
 def give_back(
@@ -1565,9 +1616,9 @@
             jax.ShapeDtypeStruct((line, units, slab), BF16),
             jax.ShapeDtypeStruct((line, part, slab), BF16),
         ),
-        in_specs=[vmem_spec()] * 6 + [any_spec()] * 3,
+        in_specs=[any_spec()] * 3 + [vmem_spec()] + [any_spec()] * 5,
         out_specs=(
-            vmem_spec(),
+            any_spec(),
             vmem_spec(),
             vmem_spec(),
             vmem_spec(),
@@ -1578,20 +1629,27 @@
         scratch_shapes=[
             pltpu.VMEM((full, width), BF16),
             pltpu.VMEM((full, units), BF16),
-            pltpu.VMEM((units, full), BF16),
-            pltpu.VMEM((2, full, 256), BF16),
+            pltpu.VMEM((2, full, slab), BF16),
             pltpu.VMEM((line, units, slab), BF16),
             pltpu.VMEM((line, units, slab), BF16),
             pltpu.VMEM((line - 1, units, slab), BF16),
             pltpu.VMEM((line - 1, units, slab), BF16),
             pltpu.VMEM((part, full), BF16),
             pltpu.VMEM((line, part, slab), F32),
+            pltpu.VMEM((rows, width), F32),
+            pltpu.VMEM((rows, width), F32),
+            pltpu.VMEM((rows, width), BF16),
+            pltpu.VMEM((full, part), BF16),
+            pltpu.VMEM((line, part, slab), BF16),
+            pltpu.VMEM((rows, width), F32),
             pltpu.SemaphoreType.DMA((7,)),
             pltpu.SemaphoreType.DMA((7,)),
             *line_sems(line),
             pltpu.SemaphoreType.DMA((2,)),
             pltpu.SemaphoreType.DMA((2,)),
             pltpu.SemaphoreType.DMA((2,)),
+            pltpu.SemaphoreType.DMA((14,)),
+            pltpu.SemaphoreType.DMA((4,)),
         ],
         compiler_params=pltpu.CompilerParams(
             collective_id=3, has_side_effects=True, vmem_limit_bytes=62 * MIB
@@ -1640,10 +1698,10 @@
     halo_kv,
     floor,
     logs,
-    grad,
+    grad_given,
     inner,
     hidden,
-    w_down,
+    w_down_given,
     middle,
     gate_in,
     grads_out,
@@ -1664,6 +1722,8 @@
     into,
     total,
     hidden_block,
+    grad,
+    w_down,
     r_send,
     r_recv,
     *sems,
@@ -1690,7 +1750,9 @@
         pltpu.make_async_copy(halo_kv.at[0], k_ext.at[pl.ds(0, WINDOW)], loads.at[4]),
         pltpu.make_async_copy(halo_kv.at[1], v_ext.at[pl.ds(0, WINDOW)], loads.at[5]),
         pltpu.make_async_copy(middle, total, loads.at[6]),
+        pltpu.make_async_copy(grad_given, grad, loads.at[7]),
     ]
+    down_load = pltpu.make_async_copy(w_down_given, w_down, loads.at[8])
     halo = [
         remote(
             halo_out.at[i], halo_in.at[i], halo_send.at[i], halo_recv.at[i], (p.s - 1, p.h)
@@ -1718,9 +1780,8 @@
         if n + 1 < len(order):
             fetches[n + 1].start()
 
-        @pl.loop(0, line)
-        def _(d):
-            cols = pl.ds(pl.multiple_of(d * slab, slab), slab)
+        for d in range(line):
+            cols = slice(d * slab, (d + 1) * slab)
             value = product(hidden_block[n % 2][:, 0 : w_down.shape[1]], w_down[d])
             for other in more:
                 value = value + other[:, cols].astype(F32)
@@ -1733,13 +1794,15 @@
                 tile, q, k_ext, v_ext, k_t, floor, logs, inner, grad, key_sum, value_sum
             )
 
+    down_load.start()
+    fetches[0].start()
     for copy in started:
         copy.start()
-    fetches[0].start()
     p.greet()
     started[0].wait()
     gate_reduce.start(0)
     clear_last(gate_reduce)
+    down_load.wait()
     emit(0, out.at[0])
     copies[0].start()
     emit(1, out.at[1])
@@ -1864,8 +1927,8 @@
             jax.ShapeDtypeStruct((units, slab), F32),
         ),
         in_specs=[any_spec()] * 2
-        + [vmem_spec()] * 4
-        + [any_spec(), vmem_spec(), any_spec(), any_spec()],
+        + [vmem_spec(), vmem_spec(), any_spec(), vmem_spec()]
+        + [any_spec()] * 4,
         out_specs=(any_spec(), vmem_spec(), vmem_spec()),
         scratch_shapes=[
             pltpu.VMEM((count, part), BF16),
@@ -1883,10 +1946,12 @@
             pltpu.VMEM((7, rows, width), BF16),
             pltpu.VMEM((rows, width), F32),
             pltpu.VMEM((2, rows, hidden.shape[1]), BF16),
+            pltpu.VMEM((count, part), BF16),
+            pltpu.VMEM((line, units, slab), BF16),
             pltpu.SemaphoreType.DMA((7,)),
             pltpu.SemaphoreType.DMA((7,)),
             *line_sems(line),
-            pltpu.SemaphoreType.DMA((7,)),
+            pltpu.SemaphoreType.DMA((9,)),
             pltpu.SemaphoreType.DMA((2,)),
             pltpu.SemaphoreType.DMA((2,)),
             pltpu.SemaphoreType.DMA((2,)),
@@ -1903,10 +1968,10 @@
 
 def finish_kernel(
     line,
-    grads,
-    weight,
+    grads_given,
+    weight_given,
     normed,
-    tokens,
+    tokens_given,
     gain,
     grad_middle,
     out_given,
@@ -1917,7 +1982,6 @@
     key_grad,
     value_grad,
     out_grad,
-    turned,
     strip,
     parts,
     parts_up_in,
@@ -1930,13 +1994,17 @@
     total,
     gain_line,
     gain_in,
+    grads_in,
+    weight_in,
+    tokens_in,
     r_send,
     r_recv,
     *sems,
 ):
     p = Place(line)
-    part_sems, out_sems, gain_sems = sems[0:4], sems[4:8], sems[8:12]
-    loads, strip_sems, gain_send, gain_recv = sems[12:16]
+    part_sems, out_sems = sems[0:4], sems[4:8]
+    loads, strip_sems, gain_send, gain_recv, line_send, line_recv, block_sems = sems[8:15]
+    grads, weight, tokens = grads_in, weight_in, tokens_in
     rows, width = tokens.shape
     slab = width // line
     part = query_grad.shape[1]
@@ -1946,9 +2014,28 @@
         pltpu.make_async_copy(out_given, out_parts, loads.at[0]),
         pltpu.make_async_copy(grad_middle, input_grad, loads.at[1]),
     ]
-    for copy in started:
+    turns = (
+        p.second + p.turn,
+        p.across + p.turn,
+        p.first,
+        p.first + p.turn,
+        p.across,
+        p.core,
+        p.h,
+        p.second,
+    )
+    blocks = []
+    for n, j in enumerate(turns):
+        at = pl.ds(pl.multiple_of(j * rows, rows), rows)
+        blocks.append(pltpu.make_async_copy(grads_given.at[at], grads.at[at], block_sems.at[n]))
+    weight_load = pltpu.make_async_copy(weight_given, weight, loads.at[2])
+    tokens_load = pltpu.make_async_copy(tokens_given, tokens, loads.at[3])
+    weight_load.start()
+    blocks[0].start()
+    started[0].start()
+    for copy in blocks[1:] + [started[1], tokens_load]:
         copy.start()
-    p.greet()
+    greet_line(p)
     started[0].wait()
     out_reduce.start(0)
     for reduce in (part_reduce, out_reduce):
@@ -1958,33 +2045,40 @@
     def emit(j, target, *more):
         at = pl.ds(pl.multiple_of(j * rows, rows), rows)
 
-        @pl.loop(0, line)
-        def _(d):
-            cols = pl.ds(pl.multiple_of(d * slab, slab), slab)
+        for d in range(line):
+            cols = slice(d * slab, (d + 1) * slab)
             value = product_nt(grads[at, :], weight[cols, :])
             for other in more:
                 value = value + other[:, cols].astype(F32)
             target[:, cols] = value.astype(target.dtype)
 
+    weight_load.wait()
+    blocks[0].wait()
     emit(p.second + p.turn, out.at[0])
     copies[0].start()
+    blocks[1].wait()
     emit(p.across + p.turn, out.at[1])
     copies[1].start()
     copies[0].wait_recv()
+    blocks[2].wait()
     emit(p.first, out.at[2], into.at[0])
     copies[4].start()
     copies[0].wait_send()
+    blocks[3].wait()
     emit(p.first + p.turn, out.at[0])
     copies[2].start()
     copies[1].wait_recv()
+    blocks[4].wait()
     emit(p.across, out.at[3], into.at[1])
     copies[5].start()
     copies[1].wait_send()
+    blocks[5].wait()
     emit(p.core, out.at[1])
     copies[3].start()
-    turn_rows(grads, turned)
+    blocks[6].wait()
+    blocks[7].wait()
     multiply = lambda *some: weight_product(
-        lambda rows_in: product(turned[...], rows_in),
+        lambda rows_in: product_tn(grads[...], rows_in),
         normed,
         lambda d: parts.at[d],
         strip.at.__getitem__,
@@ -2012,6 +2106,7 @@
     part_reduce.step(1)
     copies[6].wait_recv()
     started[1].wait()
+    tokens_load.wait()
     gain_own = gain_line.at[p.s]
     gain_own[...] = jnp.zeros(gain_own.shape, F32)
     gain_own[1:2, :] = ffn_gain_part[...]
@@ -2030,10 +2125,30 @@
         copy.start()
         copy.wait()
         gain_own[...] += gain_in[i]
-    gain_gather = LineGather(p, lambda d: gain_line.at[d], *gain_sems)
-    gain_gather.start(0)
-    for t in range(line - 1):
-        gain_gather.step(t)
+    spread = [
+        remote(
+            gain_own,
+            gain_own,
+            line_send.at[k - 1],
+            line_recv.at[k - 1],
+            (lax.rem(p.s + k, line), p.h),
+        )
+        for k in range(1, line)
+    ]
+    came = [
+        remote(
+            gain_line.at[lax.rem(p.s + line - k, line)],
+            gain_line.at[lax.rem(p.s + line - k, line)],
+            line_send.at[k - 1],
+            line_recv.at[k - 1],
+            (lax.rem(p.s + k, line), p.h),
+        )
+        for k in range(1, line)
+    ]
+    for copy in spread:
+        copy.start()
+    for copy in came:
+        copy.wait_recv()
     summed = gain_line[0]
     for d in range(1, line):
         summed = summed + gain_line[d]
@@ -2046,7 +2161,8 @@
             ).T
     for i in range(2, 7):
         copies[i].wait_send()
-    gain_gather.finish()
+    for copy in spread:
+        copy.wait_send()
     for reduce in (part_reduce, out_reduce):
         reduce.finish()
 
@@ -2060,17 +2176,17 @@
         functools.partial(finish_kernel, line),
         out_shape=(
             jax.ShapeDtypeStruct((rows, width), F32),
-            jax.ShapeDtypeStruct((8, width), F32),
+            jax.ShapeDtypeStruct((2, width), F32),
             jax.ShapeDtypeStruct((slab, part), F32),
             jax.ShapeDtypeStruct((slab, part), F32),
             jax.ShapeDtypeStruct((slab, part), F32),
             jax.ShapeDtypeStruct((part, slab), F32),
         ),
         in_specs=[
-            vmem_spec(),
-            vmem_spec(),
             any_spec(),
-            vmem_spec(),
+            any_spec(),
+            any_spec(),
+            any_spec(),
             vmem_spec(),
             any_spec(),
             any_spec(),
@@ -2078,8 +2194,7 @@
         ],
         out_specs=(vmem_spec(),) * 6,
         scratch_shapes=[
-            pltpu.VMEM((3 * part, full), BF16),
-            pltpu.VMEM((2, full, 256), BF16),
+            pltpu.VMEM((2, full, slab), BF16),
             pltpu.VMEM((line, 3 * part, slab), BF16),
             pltpu.VMEM((line - 1, 3 * part, slab), BF16),
             pltpu.VMEM((line - 1, 3 * part, slab), BF16),
@@ -2089,15 +2204,21 @@
             pltpu.VMEM((5, rows, width), BF16),
             pltpu.VMEM((7, rows, width), BF16),
             pltpu.VMEM((rows, width), F32),
-            pltpu.VMEM((line, 8, width), F32),
-            pltpu.VMEM((3, 8, width), F32),
+            pltpu.VMEM((line, 2, width), F32),
+            pltpu.VMEM((3, 2, width), F32),
+            pltpu.VMEM(grads.shape, BF16),
+            pltpu.VMEM(weight.shape, BF16),
+            pltpu.VMEM((rows, width), BF16),
             pltpu.SemaphoreType.DMA((7,)),
             pltpu.SemaphoreType.DMA((7,)),
-            *line_sems(line, 3),
-            pltpu.SemaphoreType.DMA((2,)),
+            *line_sems(line, 2),
+            pltpu.SemaphoreType.DMA((4,)),
             pltpu.SemaphoreType.DMA((2,)),
             pltpu.SemaphoreType.DMA((3,)),
             pltpu.SemaphoreType.DMA((3,)),
+            pltpu.SemaphoreType.DMA((line - 1,)),
+            pltpu.SemaphoreType.DMA((line - 1,)),
+            pltpu.SemaphoreType.DMA((8,)),
         ],
         compiler_params=pltpu.CompilerParams(
             collective_id=5, has_side_effects=True, vmem_limit_bytes=62 * MIB

time: 632 us -> 605 us (0.957)
  Pallas kernels: 620 us -> 596 us
    pallas_call x1, Pallas kernels: 161 us -> 147 us  [feed(): pl.pallas_call(functools.partial(feed_kernel, line), out_shape=(jax.Shape...]
    pallas_call x1, Pallas kernels: 101 us -> 88.6 us  [finish(): pl.pallas_call(functools.partial(finish_kernel, line), out_shape=(jax.Sha...]
where the time goes in v5:
time: 605 us; the launch traced here: 598 us
  Pallas kernels  596 us (99%)
    pallas_call x1, Pallas kernels, forward(): pl.pallas_call(functools.partial(forward_kernel, line), out_shape=(jax.Sh...  205 us
    pallas_call x1, Pallas kernels, feed(): pl.pallas_call(functools.partial(feed_kernel, line), out_shape=(jax.Shape...  147 us
    pallas_call x1, Pallas kernels, finish(): pl.pallas_call(functools.partial(finish_kernel, line), out_shape=(jax.Sha...  88.6 us
    pallas_call x1, Pallas kernels, attend_back(): pl.pallas_call(functools.partial(attend_back_kernel, line), out_shape=(ja...  74.3 us
    pallas_call x1, Pallas kernels, give_back(): pl.pallas_call(functools.partial(return_kernel, line), out_shape=(jax.Sha...  72.2 us

profile of v5, /device:TPU:0, one launch (start us, length us, event | category | flops | bytes accessed | tf_op | source)
XLA Modules:
  0.0 598.0 jit_solution(2977511975738646130)
XLA Ops:
  0.6 204.7 %shard_map.203 = (bf16[3072,2048]{1,0:T(8,128)(2,1)}, bf16[3072,768]{1,0:T(8,128)(2,1)}, bf16[2048,768]{1,0:T(8,128)(2,1)}, s32[1,3072]{1,0:T(1,128)}, bf16[3072...) custom-call(bf16[384,2048]{1,0:T(8,128)(2,1)} %tokens_given.1, ...), custom_call_target="tpu_custom_call" | custom-call | flops 21474836480 | bytes 104857600 | tf_op jit(solution)/shard_map/pallas_call | solution.py:871
  205.3 147.5 %shard_map.204 = (bf16[3072,2048]{1,0:T(8,128)(2,1)}, bf16[3072,768]{1,0:T(8,128)(2,1)}, bf16[3072,688]{1,0:T(8,128)(2,1)}, bf16[3072,688]{1,0:T(8,128)(2,1)}, f...) custom-call(f32[384,2048]{1,0:T(8,128)} %get-tuple-element.59.middle.middle_given, ...), custom_call_target="tpu_custom_call" | custom-call | flops 53687091200 | bytes 83886080 | tf_op jit(solution)/shard_map/pallas_call | solution.py:1228
  352.8 72.2 %shard_map.205 = (f32[384,2048]{1,0:T(8,128)}, f32[1,2048]{1,0:T(1,128)}, bf16[3072,256]{1,0:T(8,128)(2,1)}, f32[2,3072]{1,0:T(2,128)}, f32[688,512]{1,0:T(8,128...) custom-call(f32[384,2048]{1,0:T(8,128)} %get-tuple-element.63.grad_given, ...), custom_call_target="tpu_custom_call" | custom-call | flops 26843545600 | bytes 83886080 | tf_op jit(solution)/shard_map/pallas_call | solution.py:1608
  425.1 74.3 %shard_map.206 = (bf16[3072,768]{1,0:T(8,128)(2,1)}, bf16[384,2048]{1,0:T(8,128)(2,1)}, f32[688,512]{1,0:T(8,128)}) custom-call(bf16[3072,768]{1,0:T(8,128)(2,1)} %get-tuple-element.55.qkv, bf16[2,1024,256]{2,1,0:T(8,128)(2,1)} %get-tuple-element.56.halo_kv, s32[1,3072]{1,0:T(1,128)} %get-tuple-element.57.floor, f32[2,3072]{1,0:T(2,128)} %get-tuple-element.58.logs, ...), custom_call_target="tpu_custom_call" | custom-call | flops 21474836480 | bytes 62914560 | tf_op jit(solution)/shard_map/pallas_call | solution.py:1922
  499.4 88.6 %shard_map.207 = (f32[384,2048]{1,0:T(8,128)}, f32[2,2048]{1,0:T(2,128)}, f32[512,256]{1,0:T(8,128)}, f32[512,256]{1,0:T(8,128)}, f32[512,256]{1,0:T(8,128)}, /*index=5*/f32[256,512]{1,0:T(8,128)}) custom-call(bf16[3072,768]{1,0:T(8,128)(2,1)} %get-tuple-element.75.grads_given, bf16[2048,768]{1,0:T(8,128)(2,1)} %get-tuple-element.76.weight_given, ...), custom_call_target="tpu_custom_call" | custom-call | flops 21474836480 | bytes 62914560 | tf_op jit(solution)/shard_map/pallas_call | solution.py:2175
  588.0 8.2 %shard_map.208 = (bf16[384,2048]{1,0:T(8,128)(2,1)}, f32[384,2048]{1,0:T(8,128)}, f32[512,256]{1,0:T(8,128)}, f32[512,256]{1,0:T(8,128)}, f32[512,256]{1,0:T(8,1...) custom-call(bf16[384,2048]{1,0:T(8,128)(2,1)} %get-tuple-element.74.refs_0_, ...), custom_call_target="tpu_custom_call" | custom-call | tf_op jit(solution)/shard_map/pallas_call | solution.py:2263
  596.3 0.7 constant_dynamic-slice_fusion
  597.0 0.5 slice_bitcast_fusion

commit v6 on v5

--- a/solution.py
+++ b/solution.py
@@ -1003,7 +1003,8 @@
         at = pl.ds(pl.multiple_of(i * step, step), step)
         mine[at] = norm_rows(grad_out[at], gain[...]).astype(BF16)
 
-    gather.start()
+    gather.out[0].start()
+    gather.out[2].start()
     saved = []
 
     def save(j):
@@ -1131,18 +1132,20 @@
     gather.got_core()
     save(p.core)
     open_up(1, 1)
+    gather.out[0].wait_send()
+    gather.out[1].start()
+    gather.got_first()
+    save(p.first)
     down_gather.step(0)
-    gather.got_first()
-    gather.got_second()
-    save(p.first)
-    save(p.second)
-    down_gather.step(1)
     open_up(2, 2)
     gather.got_core_second()
+    save(p.second + p.turn)
+    open_up(3, 3)
+    down_gather.step(1)
+    gather.got_second()
+    save(p.second)
     gather.got_core_first()
-    save(p.second + p.turn)
     save(p.first + p.turn)
-    open_up(3, 3)
     open_up(4, 4)
     open_up(5, 5)
     clear_last(down_reduce)
@@ -1163,7 +1166,8 @@
     save(p.across + p.turn)
     open_up(6, 2)
     open_up(7, 3)
-    gather.finish()
+    for copy in gather.out[1:]:
+        copy.wait_send()
     for copy in saved:
         copy.wait()
     for copy in hidden_stores[6:]:

time: 605 us -> 603 us (level)
  no operation moved by 1% of the time
where the time goes in v6:
time: 603 us; the launch traced here: 596 us
  Pallas kernels  594 us (99%)
    pallas_call x1, Pallas kernels, forward(): pl.pallas_call(functools.partial(forward_kernel, line), out_shape=(jax.Sh...  205 us
    pallas_call x1, Pallas kernels, feed(): pl.pallas_call(functools.partial(feed_kernel, line), out_shape=(jax.Shape...  150 us
    pallas_call x1, Pallas kernels, finish(): pl.pallas_call(functools.partial(finish_kernel, line), out_shape=(jax.Sha...  86.2 us
    pallas_call x1, Pallas kernels, attend_back(): pl.pallas_call(functools.partial(attend_back_kernel, line), out_shape=(ja...  75.2 us
    pallas_call x1, Pallas kernels, give_back(): pl.pallas_call(functools.partial(return_kernel, line), out_shape=(jax.Sha...  69.7 us

profile of v6, /device:TPU:0, one launch (start us, length us, event | category | flops | bytes accessed | tf_op | source)
XLA Modules:
  0.0 596.1 jit_solution(9216678894026872972)
XLA Ops:
  0.6 204.7 %shard_map.203 = (bf16[3072,2048]{1,0:T(8,128)(2,1)}, bf16[3072,768]{1,0:T(8,128)(2,1)}, bf16[2048,768]{1,0:T(8,128)(2,1)}, s32[1,3072]{1,0:T(1,128)}, bf16[3072...) custom-call(bf16[384,2048]{1,0:T(8,128)(2,1)} %tokens_given.1, ...), custom_call_target="tpu_custom_call" | custom-call | flops 21474836480 | bytes 104857600 | tf_op jit(solution)/shard_map/pallas_call | solution.py:871
  205.3 149.7 %shard_map.204 = (bf16[3072,2048]{1,0:T(8,128)(2,1)}, bf16[3072,768]{1,0:T(8,128)(2,1)}, bf16[3072,688]{1,0:T(8,128)(2,1)}, bf16[3072,688]{1,0:T(8,128)(2,1)}, f...) custom-call(f32[384,2048]{1,0:T(8,128)} %get-tuple-element.59.middle.middle_given, ...), custom_call_target="tpu_custom_call" | custom-call | flops 53687091200 | bytes 83886080 | tf_op jit(solution)/shard_map/pallas_call | solution.py:1232
  355.0 69.7 %shard_map.205 = (f32[384,2048]{1,0:T(8,128)}, f32[1,2048]{1,0:T(1,128)}, bf16[3072,256]{1,0:T(8,128)(2,1)}, f32[2,3072]{1,0:T(2,128)}, f32[688,512]{1,0:T(8,128...) custom-call(f32[384,2048]{1,0:T(8,128)} %get-tuple-element.63.grad_given, ...), custom_call_target="tpu_custom_call" | custom-call | flops 26843545600 | bytes 83886080 | tf_op jit(solution)/shard_map/pallas_call | solution.py:1612
  424.8 75.2 %shard_map.206 = (bf16[3072,768]{1,0:T(8,128)(2,1)}, bf16[384,2048]{1,0:T(8,128)(2,1)}, f32[688,512]{1,0:T(8,128)}) custom-call(bf16[3072,768]{1,0:T(8,128)(2,1)} %get-tuple-element.55.qkv, bf16[2,1024,256]{2,1,0:T(8,128)(2,1)} %get-tuple-element.56.halo_kv, s32[1,3072]{1,0:T(1,128)} %get-tuple-element.57.floor, f32[2,3072]{1,0:T(2,128)} %get-tuple-element.58.logs, ...), custom_call_target="tpu_custom_call" | custom-call | flops 21474836480 | bytes 62914560 | tf_op jit(solution)/shard_map/pallas_call | solution.py:1926
  500.0 86.2 %shard_map.207 = (f32[384,2048]{1,0:T(8,128)}, f32[2,2048]{1,0:T(2,128)}, f32[512,256]{1,0:T(8,128)}, f32[512,256]{1,0:T(8,128)}, f32[512,256]{1,0:T(8,128)}, /*index=5*/f32[256,512]{1,0:T(8,128)}) custom-call(bf16[3072,768]{1,0:T(8,128)(2,1)} %get-tuple-element.75.grads_given, bf16[2048,768]{1,0:T(8,128)(2,1)} %get-tuple-element.76.weight_given, ...), custom_call_target="tpu_custom_call" | custom-call | flops 21474836480 | bytes 62914560 | tf_op jit(solution)/shard_map/pallas_call | solution.py:2179
  586.2 8.2 %shard_map.208 = (bf16[384,2048]{1,0:T(8,128)(2,1)}, f32[384,2048]{1,0:T(8,128)}, f32[512,256]{1,0:T(8,128)}, f32[512,256]{1,0:T(8,128)}, f32[512,256]{1,0:T(8,1...) custom-call(bf16[384,2048]{1,0:T(8,128)(2,1)} %get-tuple-element.74.refs_0_, ...), custom_call_target="tpu_custom_call" | custom-call | tf_op jit(solution)/shard_map/pallas_call | solution.py:2267
  594.4 0.7 constant_dynamic-slice_fusion
  595.2 0.5 slice_bitcast_fusion

commit v7 on v6

--- a/solution.py
+++ b/solution.py
@@ -2103,11 +2103,11 @@
     copies[5].wait_recv()
     emit(p.second, out.at[4], into.at[2], into.at[5])
     copies[6].start()
+    part_reduce.step(1)
     out_reduce.step(2)
     for first, last in strips(part, 128):
         out_grad[first:last, :] = out_reduce.total(slice(first, last))
     copies[4].wait_recv()
-    part_reduce.step(1)
     copies[6].wait_recv()
     started[1].wait()
     tokens_load.wait()

time: 603 us -> 603 us (level)
  no operation moved by 1% of the time
where the time goes in v7:
time: 603 us; the launch traced here: 596 us
  Pallas kernels  594 us (99%)
    pallas_call x1, Pallas kernels, forward(): pl.pallas_call(functools.partial(forward_kernel, line), out_shape=(jax.Sh...  205 us
    pallas_call x1, Pallas kernels, feed(): pl.pallas_call(functools.partial(feed_kernel, line), out_shape=(jax.Shape...  150 us
    pallas_call x1, Pallas kernels, finish(): pl.pallas_call(functools.partial(finish_kernel, line), out_shape=(jax.Sha...  86.2 us
    pallas_call x1, Pallas kernels, attend_back(): pl.pallas_call(functools.partial(attend_back_kernel, line), out_shape=(ja...  75.2 us
    pallas_call x1, Pallas kernels, give_back(): pl.pallas_call(functools.partial(return_kernel, line), out_shape=(jax.Sha...  69.7 us

profile of v7, /device:TPU:0, one launch (start us, length us, event | category | flops | bytes accessed | tf_op | source)
XLA Modules:
  0.0 596.1 jit_solution(2755032712325055277)
XLA Ops:
  0.6 204.7 %shard_map.203 = (bf16[3072,2048]{1,0:T(8,128)(2,1)}, bf16[3072,768]{1,0:T(8,128)(2,1)}, bf16[2048,768]{1,0:T(8,128)(2,1)}, s32[1,3072]{1,0:T(1,128)}, bf16[3072...) custom-call(bf16[384,2048]{1,0:T(8,128)(2,1)} %tokens_given.1, ...), custom_call_target="tpu_custom_call" | custom-call | flops 21474836480 | bytes 104857600 | tf_op jit(solution)/shard_map/pallas_call | solution.py:871
  205.3 149.7 %shard_map.204 = (bf16[3072,2048]{1,0:T(8,128)(2,1)}, bf16[3072,768]{1,0:T(8,128)(2,1)}, bf16[3072,688]{1,0:T(8,128)(2,1)}, bf16[3072,688]{1,0:T(8,128)(2,1)}, f...) custom-call(f32[384,2048]{1,0:T(8,128)} %get-tuple-element.59.middle.middle_given, ...), custom_call_target="tpu_custom_call" | custom-call | flops 53687091200 | bytes 83886080 | tf_op jit(solution)/shard_map/pallas_call | solution.py:1232
  355.0 69.7 %shard_map.205 = (f32[384,2048]{1,0:T(8,128)}, f32[1,2048]{1,0:T(1,128)}, bf16[3072,256]{1,0:T(8,128)(2,1)}, f32[2,3072]{1,0:T(2,128)}, f32[688,512]{1,0:T(8,128...) custom-call(f32[384,2048]{1,0:T(8,128)} %get-tuple-element.63.grad_given, ...), custom_call_target="tpu_custom_call" | custom-call | flops 26843545600 | bytes 83886080 | tf_op jit(solution)/shard_map/pallas_call | solution.py:1612
  424.8 75.2 %shard_map.206 = (bf16[3072,768]{1,0:T(8,128)(2,1)}, bf16[384,2048]{1,0:T(8,128)(2,1)}, f32[688,512]{1,0:T(8,128)}) custom-call(bf16[3072,768]{1,0:T(8,128)(2,1)} %get-tuple-element.55.qkv, bf16[2,1024,256]{2,1,0:T(8,128)(2,1)} %get-tuple-element.56.halo_kv, s32[1,3072]{1,0:T(1,128)} %get-tuple-element.57.floor, f32[2,3072]{1,0:T(2,128)} %get-tuple-element.58.logs, ...), custom_call_target="tpu_custom_call" | custom-call | flops 21474836480 | bytes 62914560 | tf_op jit(solution)/shard_map/pallas_call | solution.py:1926
  500.0 86.2 %shard_map.207 = (f32[384,2048]{1,0:T(8,128)}, f32[2,2048]{1,0:T(2,128)}, f32[512,256]{1,0:T(8,128)}, f32[512,256]{1,0:T(8,128)}, f32[512,256]{1,0:T(8,128)}, /*index=5*/f32[256,512]{1,0:T(8,128)}) custom-call(bf16[3072,768]{1,0:T(8,128)(2,1)} %get-tuple-element.75.grads_given, bf16[2048,768]{1,0:T(8,128)(2,1)} %get-tuple-element.76.weight_given, ...), custom_call_target="tpu_custom_call" | custom-call | flops 21474836480 | bytes 62914560 | tf_op jit(solution)/shard_map/pallas_call | solution.py:2179
  586.2 8.2 %shard_map.208 = (bf16[384,2048]{1,0:T(8,128)(2,1)}, f32[384,2048]{1,0:T(8,128)}, f32[512,256]{1,0:T(8,128)}, f32[512,256]{1,0:T(8,128)}, f32[512,256]{1,0:T(8,1...) custom-call(bf16[384,2048]{1,0:T(8,128)(2,1)} %get-tuple-element.74.refs_0_, ...), custom_call_target="tpu_custom_call" | custom-call | tf_op jit(solution)/shard_map/pallas_call | solution.py:2267
  594.4 0.7 constant_dynamic-slice_fusion
  595.2 0.5 slice_bitcast_fusion
